TPU v7x, 256 devices: a whole 4x4x8 slice. The times are simulated.
256 devices in a mesh: rep: 8 (over x, core), dom: 32 (over y, z).
Axes of the slice: x: 4, y: 4, z: 8, core: 2. Of those that a mesh axis runs over, the one named last changes fastest.
Arguments:
- node_latent: bfloat16 [8, 16384, 256], P('rep', 'dom'), may hold values from -6 to 6
- edge_latent: bfloat16 [8, 131072, 256], P('rep', 'dom'), may hold values from -6 to 6
- node_cot: bfloat16 [8, 16384, 256], P('rep', 'dom'), may hold values from -6 to 6
- edge_cot: bfloat16 [8, 131072, 256], P('rep', 'dom'), may hold values from -6 to 6
- edge_w_in: bfloat16 [768, 256], replicated, may hold values from -0.21875 to 0.21875
- edge_b_in: float32 [256], replicated, may hold values from -3 to 3
- edge_w_out: bfloat16 [256, 256], replicated, may hold values from -0.375 to 0.375
- edge_gain: float32 [256], replicated, may hold values from 0.5 to 1.5
- node_w_in: bfloat16 [512, 256], replicated, may hold values from -0.25 to 0.25
- node_b_in: float32 [256], replicated, may hold values from -3 to 3
- node_w_out: bfloat16 [256, 256], replicated, may hold values from -0.375 to 0.375
- node_gain: float32 [256], replicated, may hold values from 0.5 to 1.5
- edge_senders: int32 [8, 131072], P('rep', 'dom'), may hold values from 0 to 767, as said below
- edge_receivers: int32 [8, 131072], P('rep', 'dom'), may hold values from 0 to 511, as said below
- block_fill: int32 [8, 1024], P('rep', 'dom'), may hold values from 0 to 128, as said below
- send_rows: int32 [8, 64, 128], P('rep', 'dom'), may hold values from 0 to 511, as said below
Outputs:
- grad_nodes: bfloat16 [8, 16384, 256], P('rep', 'dom')
- grad_edges: bfloat16 [8, 131072, 256], P('rep', 'dom')
- grad_edge_w_in: float32 [768, 256], P('dom')
- grad_edge_b_in: float32 [256], P('dom')
- grad_edge_w_out: float32 [256, 256], P('dom')
- grad_edge_gain: float32 [256], P('dom')
- grad_node_w_in: float32 [512, 256], P('dom')
- grad_node_b_in: float32 [256], P('dom')
- grad_node_w_out: float32 [256, 256], P('dom')
- grad_node_gain: float32 [256], P('dom')
Inputs may be any that keep to these rules, and one draw needn't show every extreme that they name: Each partition has 32 blocks of 128 slots; blocks in use come first and every partition uses at least one; a block's first block_fill slots are live edges, the rest padding. `edge_receivers`: along a partition's live slots the receivers never fall; padding slots hold 0. `edge_senders`: rows of the partition's table: own rows, then the 128 rows from the lower neighbour, then the 128 from the upper; the first and last partitions never name a missing neighbour; padding slots hold 0. `send_rows`: for each partition, two lists of 128 distinct own rows: first those sent to the lower neighbour, then those sent to the upper.
All inputs are finite; a program needn't handle non-finite values.
Results may differ from a plain program's by a relative error of at most 0.01.
Values may be sent and summed in bfloat16 or wider, within the bound.
No kernel may reach another device: no remote copies, remote signals or barrier semaphores. Data moves between devices by JAX's collectives and lax.ppermute only.
A program may use at most 128 MiB of HBM per device.

v0:
```python
import jax
import jax.numpy as jnp
from jax import lax
from jax.sharding import PartitionSpec as P

EBLOCK = 128


NORM_EPS = 1e-05


def with_halo(cells, sides, width):
    for axis, dim in sides:
        count = lax.axis_size(axis)
        ends = count - 1
        head = lax.slice_in_dim(cells, 0, width, axis=dim)
        tail = lax.slice_in_dim(cells, cells.shape[dim] - width, cells.shape[dim], axis=dim)
        cells = jnp.concatenate(
            [
                lax.ppermute(tail, axis, [(i, (i + 1) % count) for i in range(ends)]),
                cells,
                lax.ppermute(head, axis, [((i + 1) % count, i) for i in range(ends)]),
            ],
            axis=dim,
        )
    return cells


def norm_forward(values):
    centred = values - jnp.mean(values, -1, keepdims=True)
    inverse = lax.rsqrt(jnp.mean(centred * centred, -1, keepdims=True) + NORM_EPS)
    return (centred * inverse, inverse)


def norm_backward(out_grad, normed, inverse, gain_vec):
    scaled = out_grad * gain_vec
    return inverse * (
        scaled
        - jnp.mean(scaled, -1, keepdims=True)
        - normed * jnp.mean(scaled * normed, -1, keepdims=True)
    )


def silu_slope(values):
    sigma = jax.nn.sigmoid(values)
    return sigma * (1.0 + values * (1.0 - sigma))


def local_terms(
    node_rows,
    halo_rows,
    edge_rows,
    node_grad_in,
    edge_grad_in,
    senders,
    receivers,
    live_mask,
    weights,
):
    edge_w_in, edge_b_in, edge_w_out, edge_gain, node_w_in, node_b_in, node_w_out, node_gain = (
        weights
    )
    feat_width = node_rows.shape[1]
    node_total = node_rows.shape[0]
    table_rows = jnp.concatenate([node_rows, halo_rows], 0)
    edge_input = jnp.concatenate([edge_rows, table_rows[senders], node_rows[receivers]], 1)
    edge_pre = jnp.dot(edge_input, edge_w_in, preferred_element_type=jnp.float32) + edge_b_in
    edge_act = jax.nn.silu(edge_pre).astype(jnp.bfloat16)
    edge_out = jnp.dot(edge_act, edge_w_out, preferred_element_type=jnp.float32)
    edge_normed, edge_inv = norm_forward(edge_out)
    live_col = live_mask[:, None]
    message = live_col * (edge_rows.astype(jnp.float32) + edge_gain * edge_normed)
    aggregate = jax.ops.segment_sum(message, receivers, num_segments=node_total).astype(
        jnp.bfloat16
    )
    node_input = jnp.concatenate([node_rows, aggregate], 1)
    node_pre = jnp.dot(node_input, node_w_in, preferred_element_type=jnp.float32) + node_b_in
    node_act = jax.nn.silu(node_pre).astype(jnp.bfloat16)
    node_out = jnp.dot(node_act, node_w_out, preferred_element_type=jnp.float32)
    node_normed, node_inv = norm_forward(node_out)
    up_grad = node_grad_in.astype(jnp.float32)
    node_back = norm_backward(up_grad, node_normed, node_inv, node_gain).astype(jnp.bfloat16)
    node_act_grad = jnp.dot(node_back, node_w_out.T, preferred_element_type=jnp.float32)
    node_pre_grad = (node_act_grad * silu_slope(node_pre)).astype(jnp.bfloat16)
    node_input_grad = jnp.dot(node_pre_grad, node_w_in.T, preferred_element_type=jnp.float32)
    edge_msg_grad = live_col * (
        edge_grad_in.astype(jnp.float32) + node_input_grad[:, feat_width:][receivers]
    )
    edge_back = norm_backward(edge_msg_grad, edge_normed, edge_inv, edge_gain).astype(jnp.bfloat16)
    edge_act_grad = jnp.dot(edge_back, edge_w_out.T, preferred_element_type=jnp.float32)
    edge_pre_grad = (edge_act_grad * silu_slope(edge_pre)).astype(jnp.bfloat16)
    edge_input_grad = jnp.dot(edge_pre_grad, edge_w_in.T, preferred_element_type=jnp.float32)
    edge_grad = (edge_msg_grad + edge_input_grad[:, :feat_width]).astype(jnp.bfloat16)
    table_grad = jax.ops.segment_sum(
        edge_input_grad[:, feat_width : 2 * feat_width], senders, num_segments=table_rows.shape[0]
    )
    recv_grad = jax.ops.segment_sum(
        edge_input_grad[:, 2 * feat_width :], receivers, num_segments=node_total
    )
    own_grad = up_grad + node_input_grad[:, :feat_width] + recv_grad + table_grad[:node_total]
    terms = (
        jnp.dot(edge_input.T, edge_pre_grad, preferred_element_type=jnp.float32),
        jnp.sum(edge_pre_grad.astype(jnp.float32), 0),
        jnp.dot(edge_act.T, edge_back, preferred_element_type=jnp.float32),
        jnp.sum(edge_msg_grad * edge_normed, 0),
        jnp.dot(node_input.T, node_pre_grad, preferred_element_type=jnp.float32),
        jnp.sum(node_pre_grad.astype(jnp.float32), 0),
        jnp.dot(node_act.T, node_back, preferred_element_type=jnp.float32),
        jnp.sum(up_grad * node_normed, 0),
    )
    return (own_grad, table_grad[node_total:], edge_grad, terms)


def per_device(
    node_latent,
    edge_latent,
    node_cot,
    edge_cot,
    edge_w_in,
    edge_b_in,
    edge_w_out,
    edge_gain,
    node_w_in,
    node_b_in,
    node_w_out,
    node_gain,
    edge_senders,
    edge_receivers,
    block_fill,
    send_rows,
):
    node_rows = node_latent[0]
    send_lists = send_rows[0]
    outgoing = node_rows[send_lists]
    framed = with_halo(outgoing, (("dom", 0),), 1)
    halo_rows = jnp.concatenate([framed[0], framed[3]], 0)
    live_mask = (
        (jnp.arange(EBLOCK)[None, :] < block_fill[0][:, None]).reshape(-1).astype(jnp.float32)
    )
    weights = (
        edge_w_in,
        edge_b_in,
        edge_w_out,
        edge_gain,
        node_w_in,
        node_b_in,
        node_w_out,
        node_gain,
    )
    own_grad, halo_grad, edge_grad, terms = local_terms(
        node_rows,
        halo_rows,
        edge_latent[0],
        node_cot[0],
        edge_cot[0],
        edge_senders[0],
        edge_receivers[0],
        live_mask,
        weights,
    )
    parted = halo_grad.reshape(2, -1, halo_grad.shape[1])
    returned = with_halo(parted.astype(jnp.bfloat16), (("dom", 0),), 1).astype(parted.dtype)
    own_grad = own_grad.at[send_lists[0]].add(returned[0]).at[send_lists[1]].add(returned[3])
    mean_factor = 1.0 / (lax.axis_size("rep") * lax.axis_size("dom"))
    terms = tuple((term * mean_factor for term in terms))
    summed = lax.psum(terms, ("rep", "dom"))
    position = lax.axis_index("dom")
    dom_count = lax.axis_size("dom")
    shares = tuple(
        (
            lax.dynamic_slice_in_dim(
                total, position * (total.shape[0] // dom_count), total.shape[0] // dom_count, 0
            )
            for total in summed
        )
    )
    return (
        own_grad.astype(jnp.bfloat16)[None],
        edge_grad[None],
        shares[0],
        shares[1],
        shares[2],
        shares[3],
        shares[4],
        shares[5],
        shares[6],
        shares[7],
    )


def solution(mesh):
    placed = (
        P("rep", "dom", None),
        P("rep", "dom", None),
        P("rep", "dom", None),
        P("rep", "dom", None),
        P(),
        P(),
        P(),
        P(),
        P(),
        P(),
        P(),
        P(),
        P("rep", "dom"),
        P("rep", "dom"),
        P("rep", "dom"),
        P("rep", "dom", None),
    )
    return jax.shard_map(
        per_device,
        mesh=mesh,
        in_specs=placed,
        out_specs=(
            P("rep", "dom", None),
            P("rep", "dom", None),
            P("dom", None),
            P("dom"),
            P("dom", None),
            P("dom"),
            P("dom", None),
            P("dom"),
            P("dom", None),
            P("dom"),
        ),
        check_vma=False,
    )
```

profile of v0, /device:TPU:1, one launch (start us, length us, event | category | flops | bytes accessed | tf_op | source)
XLA Modules:
  0.0 497.0 jit_solution(11055200915567042953)
XLA Ops:
  8.0 1.9 gather_fusion
  10.6 1.3 collective-permute-start.1
  11.9 5.6 %collective-permute-start = (bf16[1,128,256]{2,1,0:T(8,128)(2,1)}, bf16[1,128,256]{2,1,0:T(8,128)(2,1)}, u32[]{:S(2)}, u32[]{:S(2)}) collective-permute-start(bf16[1,128,256]{2,1,0:T(8,128)(2,1)} %get-tuple-element.49), channel_id=1, source_target_pairs={{0,1},{1,2},{2,3},{3,4},{4,5},{5,6},{6,7},{7,8},{8,9},{9,10},{10,1... | collective-permute-start | bytes 196616 | tf_op jit(solution)/shard_map/ppermute | solution.py:20
  19.8 1.3 fusion.34
  21.0 14.6 %gather_fusion.2 = bf16[4096,256]{1,0:T(8,128)(2,1)S(1)} fusion(bf16[512,256]{1,0:T(8,128)(2,1)S(1)} %bitcast.77, s32[4096]{0:T(1024)S(1)} %broadcast_clamp_fusion), kind=kCustom, calls=%fused_computation.2 | custom fusion | bytes 4210688 | tf_op jit(solution)/shard_map/gather | solution.py:66
  35.7 2.9 copy.42
  38.5 4.1 copy.40
  42.8 2.9 copy.45
  46.6 16.9 %gather_fusion.1 = bf16[4096,256]{1,0:T(8,128)(2,1)} fusion(bf16[768,256]{1,0:T(8,128)(2,1)S(1)} %pad_maximum_fusion.6, s32[4096]{0:T(1024)S(1)} %broadcast_clamp_fusion.1), kind=kCustom, calls=%fused_computation.1 | custom fusion | bytes 4210688 | tf_op jit(solution)/shard_map/gather | solution.py:66
  63.5 4.1 copy.41
  67.7 5.5 %multiply_convert_fusion.1 = (bf16[4096,256]{1,0:T(8,128)(2,1)S(1)}, f32[4096,256]{1,0:T(8,128)}) fusion(f32[256]{0:T(256)S(1)} %copy-done.20, bf16[768,256]{1,0:T(8,128)(2,1)S(1)} %copy-done, bf16[4096,256]{0,1:T(8,128)(2,1)} %copy.42, bf16[4096,256]{0,1:T(8,128)(2,1)} %copy.41, bf16[4096,256]{0,1:T(8,128)(2,1)} %bitcast.81), kind=kOutput, calls=%fused_computation.26 | convolution fusion | flops 1635778560 | bytes 12977152 | tf_op jit(solution)/shard_map/dot_general | solution.py:67
  73.2 1.3 copy-done.8
  75.8 1.6 copy-done.2
  78.4 2.9 add_multiply_fusion
  81.3 5.6 %copy.43 = f32[4096,256]{1,0:T(8,128)} copy(f32[4096,256]{0,1:T(8,128)} %add_multiply_fusion) | data formatting | bytes 8388608 | tf_op jit(solution)/shard_map/mul | solution.py:72
  86.9 27.4 %scatter_custom_fusion = f32[512,256]{1,0:T(8,128)} fusion(s32[4096]{0:T(1024)} %bitcast.89, f32[4096,256]{1,0:T(8,128)} %copy.43, f32[]{:T(128)} %constant.12.clone.1), kind=kCustom, calls=%fused_computation.60 | custom fusion | flops 1048576 | bytes 524800 | tf_op jit(solution)/shard_map/scatter-add | solution.py:73
  115.4 1.2 convolution_add_fusion.1
  116.7 1.3 fusion.43
  118.5 1.8 convert_reduce_fusion.1
  123.8 16.1 %gather_fusion.3 = f32[4096,256]{1,0:T(8,128)} fusion(f32[512,256]{1,0:T(8,128)S(1)} %get-tuple-element.46, s32[4096]{0:T(1024)S(1)} %broadcast_clamp_fusion), kind=kCustom, calls=%fused_computation.3 | custom fusion | bytes 8404992 | tf_op jit(solution)/shard_map/gather | solution.py:87
  139.9 5.6 %copy.46 = f32[4096,256]{0,1:T(8,128)} copy(f32[4096,256]{1,0:T(8,128)} %gather_fusion.3) | data formatting | bytes 8388608 | tf_op jit(solution)/shard_map/gather | solution.py:87
  145.5 4.8 multiply_reduce_fusion
  150.4 1.2 multiply_convert_fusion
  153.5 1.5 convolution_multiply_fusion.4
  155.9 1.9 convert_reduce_fusion
  158.7 2.8 fusion.8
  161.5 1.8 fusion.45
  163.3 4.6 copy-done.4
  167.9 2.2 slice.93
  170.1 24.2 %scatter_custom_fusion.1 = f32[768,256]{1,0:T(8,128)S(1)} fusion(s32[4096]{0:T(1024)} %bitcast.88, f32[4096,768]{1,0:T(8,128)} %copy-done.4, f32[]{:T(128)} %constant.12.clone.1), kind=kCustom, calls=%fused_computation.15 | custom fusion | flops 1048576 | bytes 4981248 | tf_op jit(solution)/shard_map/scatter-add | solution.py:94
  195.9 5.6 %copy.53 = f32[4096,256]{0,1:T(8,128)} copy(f32[4096,256]{1,0:T(8,128)} %slice.93) | data formatting | bytes 8388608
  201.6 4.0 fusion.7
  205.6 1.2 copy.52
  206.8 2.0 copy.51
  208.8 1.5 slice_bitcast_fusion.1
  210.4 6.5 %collective-permute-start.2 = (bf16[1,128,256]{2,1,0:T(8,128)(2,1)}, bf16[1,128,256]{2,1,0:T(8,128)(2,1)S(1)}, u32[]{:S(2)}, u32[]{:S(2)}) collective-permute-start(bf16[1,128,256]{2,1,0:T(8,128)(2,1)} %get-tuple-element.47), channel_id=1, source_target_pairs={{0,1},{1,2},{2,3},{3,4},{4,5},{5,6},{6,7},{7,8},{8,9},{9,10},{10,1... | collective-permute-start | bytes 196616 | tf_op jit(solution)/shard_map/ppermute | solution.py:20
  216.9 1.3 collective-permute-start.3
  218.2 2.0 fusion.17
  221.2 85.7 %all-reduce = (f32[256]{0:T(256)S(1)}, f32[256]{0:T(256)S(1)}, f32[256]{0:T(256)S(1)}, f32[256]{0:T(256)S(1)}) all-reduce(f32[256]{0:T(256)S(1)} %broadcast_multiply_fusion.9, f32[256]{0:T(256)S(1)} %broadcast_multiply_fusion.8, f32[256]{0:T(256)S(1)} %broadcast_multiply_fusion.7, ...), channel_id=1, replica_groups=mesh['rep'=8,'dom'=32] {'rep','dom'}, use_global_device_ids=true, to_apply=%region_15.16 | all-reduce | flops 1024 | bytes 8192 | tf_op jit(solution)/shard_map/psum | solution.py:166
  309.3 2.4 copy.50
  311.9 27.1 %scatter_custom_fusion.2 = f32[512,256]{1,0:T(8,128)S(1)} fusion(f32[512,256]{1,0:T(8,128)S(1)} %copy.48, s32[4096]{0:T(1024)} %bitcast.90, f32[4096,768]{1,0:T(8,128)} %copy-done.4), kind=kCustom, calls=%fused_computation.13 | custom fusion | flops 1048576 | bytes 4718592 | tf_op jit(solution)/shard_map/scatter-add | solution.py:97
  339.0 1.6 scatter_custom_fusion.3
  340.6 1.6 scatter_custom_fusion.4
  343.0 141.8 %all-reduce.4.cloned.1.call-done = (f32[768,256]{1,0:T(8,128)}, f32[256,256]{1,0:T(8,128)}, f32[512,256]{1,0:T(8,128)}, f32[256,256]{1,0:T(8,128)}) async-done(((f32[768,256]{1,0:T(8,128)}, f32[256,256]{1,0:T(8,128)}, f32[512,256]{1,0:T(8,128)}, f32[256,256]{1,0:T(8,128)}), (f32[768,256]{1,0:T(8,128)}, f32[256,256]{1,0:T(8,128)}, f32[512,256]{1,0:T(8,128)}, ...) | async-done | bytes 1835024 | tf_op jit(solution)/shard_map/psum | solution.py:166
  484.9 1.3 constant_dynamic-slice_fusion
  486.1 1.3 constant_dynamic-slice_fusion.2
  487.4 1.3 constant_dynamic-slice_fusion.3
  488.8 1.3 constant_dynamic-slice_fusion.1
  (89 shorter events, 21.6 us)
Async XLA Ops:
  7.2 60.5 %copy-start = (bf16[768,256]{1,0:T(8,128)(2,1)S(1)}, bf16[768,256]{1,0:T(8,128)(2,1)}, u32[]{:S(2)}) copy-start(bf16[768,256]{1,0:T(8,128)(2,1)} %param.20) | copy-start | bytes 1179652
  7.2 13.8 %copy-start.1 = (bf16[1,512,256]{2,1,0:T(8,128)(2,1)S(1)}, bf16[1,512,256]{2,1,0:T(8,128)(2,1)}, u32[]{:S(2)}) copy-start(bf16[1,512,256]{2,1,0:T(8,128)(2,1)} %param.16) | copy-start | bytes 786436
  7.2 477.6 %all-reduce.4.cloned.1.call-start = ((), (), s32[]{:S(2)}) async-start(), calls=%async_computation | async-start | bytes 3670016 | tf_op jit(solution)/shard_map/psum | solution.py:166
  10.6 35.1 %collective-permute-start.1 = (bf16[1,128,256]{2,1,0:T(8,128)(2,1)}, bf16[1,128,256]{2,1,0:T(8,128)(2,1)S(1)}, u32[]{:S(2)}, u32[]{:S(2)}) collective-permute-start(bf16[1,128,256]{2,1,0:T(8,128)(2,1)} %get-tuple-element.50), channel_id=1, source_target_pairs={{1,0},{2,1},{3,2},{4,3},{5,4},{6,5},{7,6},{8,7},{9,8},{10,9},{11,1... | collective-permute-start | bytes 196616 | tf_op jit(solution)/shard_map/ppermute | solution.py:22
  11.9 33.8 %collective-permute-start = (bf16[1,128,256]{2,1,0:T(8,128)(2,1)}, bf16[1,128,256]{2,1,0:T(8,128)(2,1)}, u32[]{:S(2)}, u32[]{:S(2)}) collective-permute-start(bf16[1,128,256]{2,1,0:T(8,128)(2,1)} %get-tuple-element.49), channel_id=1, source_target_pairs={{0,1},{1,2},{2,3},{3,4},{4,5},{5,6},{6,7},{7,8},{8,9},{9,10},{10,1... | collective-permute-start | bytes 196616 | tf_op jit(solution)/shard_map/ppermute | solution.py:20
  35.6 7.0 %copy-start.13 = (bf16[1,512,256]{2,1,0:T(8,128)(2,1)S(1)}, bf16[1,512,256]{2,1,0:T(8,128)(2,1)}, u32[]{:S(2)}) copy-start(bf16[1,512,256]{2,1,0:T(8,128)(2,1)} %param.18) | copy-start | bytes 786436
  63.5 4.1 copy-start.20
  67.7 6.9 %copy-start.15 = (bf16[256,256]{1,0:T(8,128)(2,1)S(1)}, bf16[256,256]{1,0:T(8,128)(2,1)}, u32[]{:S(2)}) copy-start(bf16[256,256]{1,0:T(8,128)(2,1)} %param.22) | copy-start | bytes 393220
  73.2 1.3 copy-start.8
  75.3 2.1 copy-start.2
  75.3 3.1 copy-start.6
  75.3 3.1 copy-start.17
  81.3 34.1 %copy-start.21 = (f32[256]{0:T(256)S(1)}, f32[256]{0:T(256)}, u32[]{:S(2)}) copy-start(f32[256]{0:T(256)} %param.25) | copy-start | bytes 3076
  86.9 31.2 %copy-start.18 = (f32[256]{0:T(256)S(1)}, f32[256]{0:T(256)}, u32[]{:S(2)}) copy-start(f32[256]{0:T(256)} %param.27) | copy-start | bytes 3076
  116.7 3.7 copy-start.14
  145.5 4.9 copy-start.3
  150.4 2.1 copy-start.5
  150.4 3.1 copy-start.9
  153.5 1.5 copy-start.16
  153.5 2.4 copy-start.22
  155.8 1.9 copy-start.7
  155.8 2.2 copy-start.11
  155.9 2.9 copy-start.12
  163.3 4.6 copy-start.4
  205.5 12.7 %copy-start.19 = (f32[256]{0:T(256)S(1)}, f32[256]{0:T(256)}, u32[]{:S(2)}) copy-start(f32[256]{0:T(256)} %get-tuple-element.61) | copy-start | bytes 3076
  210.4 128.6 %collective-permute-start.2 = (bf16[1,128,256]{2,1,0:T(8,128)(2,1)}, bf16[1,128,256]{2,1,0:T(8,128)(2,1)S(1)}, u32[]{:S(2)}, u32[]{:S(2)}) collective-permute-start(bf16[1,128,256]{2,1,0:T(8,128)(2,1)} %get-tuple-element.47), channel_id=1, source_target_pairs={{0,1},{1,2},{2,3},{3,4},{4,5},{5,6},{6,7},{7,8},{8,9},{9,10},{10,1... | collective-permute-start | bytes 196616 | tf_op jit(solution)/shard_map/ppermute | solution.py:20
  216.9 122.1 %collective-permute-start.3 = (bf16[1,128,256]{2,1,0:T(8,128)(2,1)}, bf16[1,128,256]{2,1,0:T(8,128)(2,1)S(1)}, u32[]{:S(2)}, u32[]{:S(2)}) collective-permute-start(bf16[1,128,256]{2,1,0:T(8,128)(2,1)} %get-tuple-element.48), channel_id=1, source_target_pairs={{1,0},{2,1},{3,2},{4,3},{5,4},{6,5},{7,6},{8,7},{9,8},{10,9},{11,1... | collective-permute-start | bytes 196616 | tf_op jit(solution)/shard_map/ppermute | solution.py:22
  220.2 91.5 %copy-start.10 = (f32[512,256]{0,1:T(8,128)S(1)}, f32[512,256]{0,1:T(8,128)}, u32[]{:S(2)}) copy-start(f32[512,256]{0,1:T(8,128)} %fusion.17) | copy-start | bytes 1572868
Sparse Core Ops, SparseCore 0:
  218.3 266.4 all-reduce.3
where the time goes:
time: 499 us; the launch traced here: 497 us
  waiting for transfers between devices  142 us (28%)
  local copies, waits for them, and re-layouts  113 us (23%)
  other arithmetic  106 us (21%)
  blocking collectives  85.7 us (17%)
  matrix products  21.2 us (4%)
  starting transfers between devices  14.8 us (3%)
  between operations  14.5 us (3%)
    psum x1, waiting for transfers between devices, per_device(): summed = lax.psum(terms, ('rep', 'dom'))  142 us
    psum x1, blocking collectives, per_device(): summed = lax.psum(terms, ('rep', 'dom'))  85.7 us
    unnamed x53, local copies, waits for them, and re-layouts  30.8 us
    scatter-add x1, other arithmetic, local_terms(): jax.ops.segment_sum(message, receivers, num_segments=node_total)  27.4 us
    scatter-add x1, other arithmetic, local_terms(): jax.ops.segment_sum(edge_input_grad[:, 2 * feat_width:], receivers, num_s...  27.1 us
    scatter-add x1, other arithmetic, local_terms(): jax.ops.segment_sum(edge_input_grad[:, feat_width:2 * feat_width], sender...  24.2 us
    gather x2, local copies, waits for them, and re-layouts, local_terms(): node_input_grad[:, feat_width:][receivers]  21.7 us
    gather x2, local copies, waits for them, and re-layouts, local_terms(): table_rows[senders]  21.1 us
  transfers between devices with their start and end apart: 5, of which 1 were waited for; matrix products, arithmetic and copies ran while one was open for 14% of the time, Pallas kernels for 0%

commit v1 on v0

v1 whole, which is shorter than its diff:
```python
import functools

import jax
import jax.numpy as jnp
from jax import lax
from jax.experimental import pallas as pl
from jax.experimental.pallas import tpu as pltpu
from jax.sharding import PartitionSpec as P

D = 256
NODE = 512
EDGE = 4096
HALO = 128
TABLE = NODE + 2 * HALO
EBLOCK = 128
NBLK = EDGE // EBLOCK
CHUNK = 512
NCHUNK = EDGE // CHUNK
PER = CHUNK // EBLOCK
SUB = 128
LANE = 128
NORM_EPS = 1e-05
N_DOM = 32
EDGE_ROWS = 40
NODE_ROWS = 32

BF = jnp.bfloat16
F32 = jnp.float32


def mm(a, b):
    return lax.dot_general(a, b, (((1,), (0,)), ((), ())), preferred_element_type=F32)


def mm_nt(a, b):
    return lax.dot_general(a, b, (((1,), (1,)), ((), ())), preferred_element_type=F32)


def mm_tn(a, b):
    return lax.dot_general(a, b, (((0,), (0,)), ((), ())), preferred_element_type=F32)


def as_columns(row):
    return jnp.broadcast_to(row, (LANE, LANE)).T


def one_hot_rows(row, count):
    places = lax.broadcasted_iota(jnp.int32, (count, row.shape[1]), 0)
    return jnp.where(places == row, 1.0, 0.0).astype(BF)


def one_hot_cols(cols, count):
    places = lax.broadcasted_iota(jnp.int32, (cols.shape[0], LANE), 1)
    parts = [
        jnp.where(cols == places + k * LANE, 1.0, 0.0).astype(BF) for k in range(count // LANE)
    ]
    return jnp.concatenate(parts, 1)


def norm_forward(values):
    centred = values - jnp.mean(values, -1, keepdims=True)
    inverse = lax.rsqrt(jnp.mean(centred * centred, -1, keepdims=True) + NORM_EPS)
    return centred * inverse, inverse


def pick_kernel(rows_ref, node_ref, low_ref, up_ref):
    for side, out in ((0, low_ref), (1, up_ref)):
        hot = one_hot_cols(as_columns(rows_ref[side : side + 1, :]), NODE)
        out[...] = mm(hot, node_ref[...]).astype(BF)


def layer_kernel(
    send_ref,
    recv_ref,
    fill_ref,
    edge_ref,
    ecot_ref,
    node_ref,
    hlow_ref,
    hup_ref,
    ncot_ref,
    ewi_ref,
    eb_ref,
    ewo_ref,
    eg_ref,
    nwi_ref,
    nb_ref,
    nwo_ref,
    ng_ref,
    gedge_ref,
    own_ref,
    glow_ref,
    gup_ref,
    edge_sum_ref,
    node_sum_ref,
    wp_ref,
    x_ref,
    hot_ref,
    hott_ref,
    act_ref,
    slope_ref,
    normed_ref,
    inv_ref,
    agg_ref,
    back_node_ref,
    sums_ref,
    sumr_ref,
    dw0_ref,
    dwo_ref,
    dgain_ref,
    base_ref,
):
    table = jnp.concatenate([node_ref[...], hlow_ref[...], hup_ref[...]], 0)
    wp_ref[0:D, :] = (ewi_ref[0:D, :].astype(F32) * 0.5).astype(BF)
    wp_ref[D : D + TABLE, :] = (mm(table, ewi_ref[D : 2 * D, :]) * 0.5).astype(BF)
    wp_ref[D + TABLE :, :] = (
        (mm(node_ref[...], ewi_ref[2 * D :, :]) + eb_ref[...]) * 0.5
    ).astype(BF)
    agg_ref[...] = jnp.zeros_like(agg_ref)
    gain = eg_ref[...]
    lanes = lax.broadcasted_iota(jnp.int32, (1, LANE), 1)

    def forward(i, carry):
        at = pl.multiple_of(i * CHUNK, CHUNK)
        parts = []
        for k in range(PER):
            here = pl.ds(pl.multiple_of(at + k * LANE, LANE), LANE)
            fill = fill_ref[0, i * PER + k]
            row = jnp.where(lanes < fill, recv_ref[:, here], -1)
            parts.append(row)
            cols = as_columns(row)
            hot = one_hot_cols(cols, NODE)
            rows = pl.ds(k * LANE, LANE)
            x_ref[rows, D + TABLE :] = hot
            hot_ref[here, :] = hot
            x_ref[rows, D : D + TABLE] = one_hot_cols(as_columns(send_ref[:, here]), TABLE)
            x_ref[rows, 0:D] = edge_ref[here, :]
        hott = one_hot_rows(jnp.concatenate(parts, 1), NODE)
        hott_ref[i] = hott
        half = mm(x_ref[...], wp_ref[...])
        t = jnp.tanh(half)
        ht = half * t
        act = (half + ht).astype(BF)
        slope = (t + 1.0) * ((half - ht) + 1.0)
        here = pl.ds(at, CHUNK)
        act_ref[here, :] = act
        slope_ref[here, :] = slope
        out = mm(act, ewo_ref[...])
        normed, inverse = norm_forward(out)
        normed_ref[here, :] = normed
        inv_ref[here, :] = jnp.broadcast_to(inverse, (CHUNK, LANE))
        message = (edge_ref[here, :].astype(F32) + gain * normed).astype(BF)
        agg_ref[...] += mm(hott, message)
        return carry

    lax.fori_loop(0, NCHUNK, forward, 0)

    agg = agg_ref[...].astype(BF)
    node = node_ref[...]
    half = (mm(node, nwi_ref[0:D, :]) + mm(agg, nwi_ref[D:, :]) + nb_ref[...]) * 0.5
    t = jnp.tanh(half)
    ht = half * t
    act = (half + ht).astype(BF)
    slope = (t + 1.0) * ((half - ht) + 1.0) * 0.5
    normed, inverse = norm_forward(mm(act, nwo_ref[...]))
    up = ncot_ref[...].astype(F32)
    c = up * ng_ref[...]
    back = (
        inverse
        * (
            c
            - jnp.mean(c, -1, keepdims=True)
            - normed * jnp.mean(c * normed, -1, keepdims=True)
        )
    ).astype(BF)
    pre_grad = (mm_nt(back, nwo_ref[...]) * slope).astype(BF)
    base_ref[...] = up + mm_nt(pre_grad, nwi_ref[0:D, :])
    back_node_ref[...] = mm_nt(pre_grad, nwi_ref[D:, :]).astype(BF)
    mean = 1.0 / 256.0

    def put(ref, row, block):
        size = block.shape[0] // N_DOM
        block = (block * mean).reshape(N_DOM, size, D)
        for side in range(2):
            ref[side, :, row : row + size, :] = block[:, :, side * LANE : (side + 1) * LANE]

    def put_vectors(ref, row, first, second):
        both = jnp.concatenate([first, second, jnp.zeros((6, D), F32)], 0) * mean
        for side in range(2):
            ref[side, :, row : row + 8, :] = jnp.broadcast_to(
                both[None, :, side * LANE : (side + 1) * LANE], (N_DOM, 8, LANE)
            )

    put(node_sum_ref, 0, jnp.concatenate([mm_tn(node, pre_grad), mm_tn(agg, pre_grad)], 0))
    put(node_sum_ref, 16, mm_tn(act, back))
    put_vectors(
        node_sum_ref,
        24,
        jnp.sum(pre_grad.astype(F32), 0, keepdims=True),
        jnp.sum(up * normed, 0, keepdims=True),
    )

    sums_ref[...] = jnp.zeros_like(sums_ref)
    sumr_ref[...] = jnp.zeros_like(sumr_ref)
    dw0_ref[...] = jnp.zeros_like(dw0_ref)
    dwo_ref[...] = jnp.zeros_like(dwo_ref)
    dgain_ref[...] = jnp.zeros_like(dgain_ref)
    wo_half = (ewo_ref[...].astype(F32) * 0.5).astype(BF)

    def backward(i, carry):
        at = pl.multiple_of(i * CHUNK, CHUNK)
        here = pl.ds(at, CHUNK)
        gathered = mm(hot_ref[here, :], back_node_ref[...])
        masks = []
        for k in range(PER):
            fill = fill_ref[0, i * PER + k]
            slots = lax.broadcasted_iota(jnp.int32, (LANE, D), 0)
            masks.append(slots < fill)
        live = jnp.concatenate(masks, 0)
        msg = jnp.where(live, ecot_ref[here, :].astype(F32), 0.0) + gathered
        normed = normed_ref[here, :]
        c = msg * gain
        q = c * normed
        dgain_ref[...] += jnp.sum(q.reshape(CHUNK // 8, 8, D), 0)
        inverse = inv_ref[here, :]
        inverse = jnp.concatenate([inverse, inverse], 1)
        back = (
            inverse
            * (c - jnp.mean(c, -1, keepdims=True) - normed * jnp.mean(q, -1, keepdims=True))
        ).astype(BF)
        pre_grad = (mm_nt(back, wo_half) * slope_ref[here, :]).astype(BF)
        gedge_ref[here, :] = (msg + mm_nt(pre_grad, ewi_ref[0:D, :])).astype(BF)
        dwo_ref[...] += mm_tn(act_ref[here, :], back)
        dw0_ref[...] += mm_tn(edge_ref[here, :], pre_grad)
        sums_ref[...] += mm(one_hot_rows(send_ref[:, here], TABLE), pre_grad)
        sumr_ref[...] += mm(hott_ref[i], pre_grad)
        return carry

    lax.fori_loop(0, NCHUNK, backward, 0)

    sums = sums_ref[...]
    sumr = sumr_ref[...].astype(BF)
    sums_bf = sums.astype(BF)
    put(
        edge_sum_ref,
        0,
        jnp.concatenate([dw0_ref[...], mm_tn(table, sums_bf), mm_tn(node, sumr)], 0),
    )
    put(edge_sum_ref, 24, dwo_ref[...])
    put_vectors(
        edge_sum_ref,
        32,
        jnp.sum(sums, 0, keepdims=True),
        jnp.sum(dgain_ref[...], 0, keepdims=True) / gain,
    )
    table_grad = mm_nt(sums_bf, ewi_ref[D : 2 * D, :])
    own_ref[...] = base_ref[...] + mm_nt(sumr, ewi_ref[2 * D :, :]) + table_grad[0:NODE]
    glow_ref[...] = table_grad[NODE : NODE + HALO].astype(BF)
    gup_ref[...] = table_grad[NODE + HALO :].astype(BF)


def finish_kernel(rows_ref, own_ref, low_ref, up_ref, out_ref):
    out_ref[...] = (
        own_ref[...]
        + mm(one_hot_rows(rows_ref[0:1, :], NODE), low_ref[...])
        + mm(one_hot_rows(rows_ref[1:2, :], NODE), up_ref[...])
    ).astype(BF)


def on_device(kernel, outs, scratch, in_smem, count):
    vmem = pl.BlockSpec(memory_space=pltpu.VMEM)
    smem = pl.BlockSpec(memory_space=pltpu.SMEM)
    return pl.pallas_call(
        kernel,
        out_shape=outs,
        in_specs=[smem if k in in_smem else vmem for k in range(count)],
        out_specs=jax.tree.map(lambda _: vmem, outs),
        scratch_shapes=scratch,
        compiler_params=pltpu.CompilerParams(vmem_limit_bytes=56 * 1024 * 1024),
    )


def shape(*dims, dtype=F32):
    return jax.ShapeDtypeStruct(dims, dtype)


def pick(rows, node):
    outs = (shape(HALO, D, dtype=BF),) * 2
    return on_device(pick_kernel, outs, [], (), 2)(rows, node)


def layer(*args):
    outs = (
        shape(EDGE, D, dtype=BF),
        shape(NODE, D),
        shape(HALO, D, dtype=BF),
        shape(HALO, D, dtype=BF),
        shape(2, N_DOM, EDGE_ROWS, LANE),
        shape(2, N_DOM, NODE_ROWS, LANE),
    )
    scratch = [
        pltpu.VMEM((D + TABLE + NODE, D), BF),
        pltpu.VMEM((CHUNK, D + TABLE + NODE), BF),
        pltpu.VMEM((EDGE, NODE), BF),
        pltpu.VMEM((NCHUNK, NODE, CHUNK), BF),
        pltpu.VMEM((EDGE, D), BF),
        pltpu.VMEM((EDGE, D), F32),
        pltpu.VMEM((EDGE, D), F32),
        pltpu.VMEM((EDGE, LANE), F32),
        pltpu.VMEM((NODE, D), F32),
        pltpu.VMEM((NODE, D), BF),
        pltpu.VMEM((TABLE, D), F32),
        pltpu.VMEM((NODE, D), F32),
        pltpu.VMEM((D, D), F32),
        pltpu.VMEM((D, D), F32),
        pltpu.VMEM((8, D), F32),
        pltpu.VMEM((NODE, D), F32),
    ]
    return on_device(layer_kernel, outs, scratch, (2,), 17)(*args)


def finish(rows, own, low, up):
    return on_device(finish_kernel, shape(NODE, D, dtype=BF), [], (), 4)(rows, own, low, up)


def swap(values, axis, flip):
    count = lax.axis_size(axis)
    return lax.ppermute(values, axis, [(i, i ^ flip) for i in range(count)])


def exchange_sum(values, axis, groups):
    parts = lax.all_to_all(values, axis, 0, 0, tiled=True, axis_index_groups=groups)
    return jnp.sum(parts.astype(F32), 0)


def reduce_shares(values):
    core = lax.axis_index("rep") % 2
    away = lax.dynamic_index_in_dim(values, 1 - core, 0, keepdims=False).astype(BF)
    kept = lax.dynamic_index_in_dim(values, core, 0, keepdims=False)
    values = kept + swap(away, "rep", 1).astype(F32)
    values = values.reshape((4, 8) + values.shape[1:]).astype(BF)
    same_z = [[y * 8 + z for y in range(4)] for z in range(8)]
    same_y = [[y * 8 + z for z in range(8)] for y in range(4)]
    values = exchange_sum(values, "dom", same_z)
    values = exchange_sum(values.astype(BF), "dom", same_y)
    others = [swap(values, "rep", flip) for flip in (2, 4, 6)]
    values = values + others[0] + others[1] + others[2]
    other = swap(values, "rep", 1)
    left = jnp.where(core == 0, values, other)
    right = jnp.where(core == 0, other, values)
    return jnp.concatenate([left, right], 1)


def per_device(
    node_latent,
    edge_latent,
    node_cot,
    edge_cot,
    edge_w_in,
    edge_b_in,
    edge_w_out,
    edge_gain,
    node_w_in,
    node_b_in,
    node_w_out,
    node_gain,
    edge_senders,
    edge_receivers,
    block_fill,
    send_rows,
):
    node_rows = node_latent[0]
    lists = send_rows[0]
    count = lax.axis_size("dom")
    rise = [(i, i + 1) for i in range(count - 1)]
    fall = [(i + 1, i) for i in range(count - 1)]
    to_lower, to_upper = pick(lists, node_rows)
    halo_lower = lax.ppermute(to_upper, "dom", rise)
    halo_upper = lax.ppermute(to_lower, "dom", fall)
    gedge, own, glow, gup, edge_sums, node_sums = layer(
        edge_senders,
        edge_receivers,
        block_fill,
        edge_latent[0],
        edge_cot[0],
        node_rows,
        halo_lower,
        halo_upper,
        node_cot[0],
        edge_w_in,
        edge_b_in[None],
        edge_w_out,
        edge_gain[None],
        node_w_in,
        node_b_in[None],
        node_w_out,
        node_gain[None],
    )
    back_upper = lax.ppermute(glow, "dom", fall)
    back_lower = lax.ppermute(gup, "dom", rise)
    grad_nodes = finish(lists, own, back_lower, back_upper)
    share = reduce_shares(jnp.concatenate([edge_sums, node_sums], 2))
    edge_share, node_share = share[:EDGE_ROWS], share[EDGE_ROWS:]
    spot = lax.axis_index("dom") * 8
    vectors = lax.dynamic_slice_in_dim(
        jnp.concatenate([edge_share[32:34], node_share[24:26]], 0), spot, 8, 1
    )
    return (
        grad_nodes[None],
        gedge[None],
        edge_share[0:24],
        vectors[0],
        edge_share[24:32],
        vectors[1],
        node_share[0:16],
        vectors[2],
        node_share[16:24],
        vectors[3],
    )


def solution(mesh):
    placed = (
        P("rep", "dom", None),
        P("rep", "dom", None),
        P("rep", "dom", None),
        P("rep", "dom", None),
        P(),
        P(),
        P(),
        P(),
        P(),
        P(),
        P(),
        P(),
        P("rep", "dom"),
        P("rep", "dom"),
        P("rep", "dom"),
        P("rep", "dom", None),
    )
    return jax.shard_map(
        per_device,
        mesh=mesh,
        in_specs=placed,
        out_specs=(
            P("rep", "dom", None),
            P("rep", "dom", None),
            P("dom", None),
            P("dom"),
            P("dom", None),
            P("dom"),
            P("dom", None),
            P("dom"),
            P("dom", None),
            P("dom"),
        ),
        check_vma=False,
    )
```

time: 499 us -> 96.2 us (0.19)
  the two profiles are of different devices: /device:TPU:1 before, /device:TPU:10 now
where the time goes in v1:
time: 96.2 us; the launch traced here: 95.8 us
  Pallas kernels  32 us (33%)
  blocking collectives  29.5 us (31%)
  starting transfers between devices  21.9 us (23%)
  waiting for transfers between devices  5.89 us (6%)
  local copies, waits for them, and re-layouts  3.54 us (4%)
  other arithmetic  2.16 us (2%)
    all_to_all x2, blocking collectives, exchange_sum(): lax.all_to_all(values, axis, 0, 0, tiled=True, axis_index_groups=groups)  29.5 us
    pallas_call x1, Pallas kernels, layer(): return on_device(layer_kernel, outs, scratch, (2,), 17)(*args)  28.1 us
    ppermute x1, starting transfers between devices, per_device(): halo_upper = lax.ppermute(to_lower, 'dom', fall)  5.75 us
    ppermute x1, starting transfers between devices, per_device(): back_upper = lax.ppermute(glow, 'dom', fall)  5.48 us
    ppermute x5, starting transfers between devices, swap(): return lax.ppermute(values, axis, [(i, i ^ flip) for i in range(count)])  4.37 us
    ppermute x1, starting transfers between devices, per_device(): halo_lower = lax.ppermute(to_upper, 'dom', rise)  3.81 us
    unnamed x15, local copies, waits for them, and re-layouts  2.86 us
    ppermute x1, starting transfers between devices, per_device(): back_lower = lax.ppermute(gup, 'dom', rise)  2.46 us
  transfers between devices with their start and end apart: 9, of which 5 were waited for; matrix products, arithmetic and copies ran while one was open for 0% of the time, Pallas kernels for 2%

profile of v1, /device:TPU:10, one launch (start us, length us, event | category | flops | bytes accessed | tf_op | source)
XLA Modules:
  0.0 95.8 jit_solution(3750840860506538762)
XLA Ops:
  0.6 1.9 %shard_map.231 = (bf16[128,256]{1,0:T(8,128)(2,1)}, bf16[128,256]{1,0:T(8,128)(2,1)}) custom-call(s32[2,128]{1,0:T(2,128)} %bitcast.33, bf16[512,256]{1,0:T(8,128)(2,1)} %bitcast.29), custom_call_target="tpu_custom_call" | custom-call | tf_op jit(solution)/shard_map/pallas_call | solution.py:289
  2.5 3.8 %collective-permute-start = (bf16[128,256]{1,0:T(8,128)(2,1)}, bf16[128,256]{1,0:T(8,128)(2,1)S(1)}, u32[]{:S(2)}, u32[]{:S(2)}) collective-permute-start(bf16[128,256]{1,0:T(8,128)(2,1)} %get-tuple-element.18), channel_id=1, source_target_pairs={{0,1},{1,2},{2,3},{3,4},{4,5},{5,6},{6,7},{7,8},{8,9},{9,10},{10,1... | collective-permute-start | bytes 196616 | tf_op jit(solution)/shard_map/ppermute | solution.py:378
  6.4 5.7 %collective-permute-start.1 = (bf16[128,256]{1,0:T(8,128)(2,1)}, bf16[128,256]{1,0:T(8,128)(2,1)S(1)}, u32[]{:S(2)}, u32[]{:S(2)}) collective-permute-start(bf16[128,256]{1,0:T(8,128)(2,1)} %get-tuple-element.19), channel_id=1, source_target_pairs={{1,0},{2,1},{3,2},{4,3},{5,4},{6,5},{7,6},{8,7},{9,8},{10,9},{11,1... | collective-permute-start | bytes 196616 | tf_op jit(solution)/shard_map/ppermute | solution.py:379
  12.1 0.5 collective-permute-done.hlow_ref
  12.6 0.0 copy-start.3
  12.6 1.7 %collective-permute-done.1.hup_ref = bf16[128,256]{1,0:T(8,128)(2,1)S(1)} collective-permute-done((bf16[128,256]{1,0:T(8,128)(2,1)}, bf16[128,256]{1,0:T(8,128)(2,1)S(1)}, u32[]{:S(2)}, u32[]{:S(2)}) %collective-permute-start.1) | collective-permute-done | bytes 65568 | tf_op jit(solution)/shard_map/ppermute | solution.py:379
  14.3 0.0 copy-start.4
  14.3 0.0 copy-done.3
  14.3 0.6 copy-done.4
  14.9 28.1 %shard_map.232 = (bf16[4096,256]{1,0:T(8,128)(2,1)}, f32[512,256]{1,0:T(8,128)}, bf16[128,256]{1,0:T(8,128)(2,1)}, bf16[128,256]{1,0:T(8,128)(2,1)}, f32[2,32,40...) custom-call(s32[1,4096]{1,0:T(1,128)} %send_ref.1, s32[1,4096]{1,0:T(1,128)} %recv_ref.1, s32[1,32]{1,0:T(1,128)} %fill_ref.1, ...), custom_call_target="tpu_custom_call" | custom-call | tf_op jit(solution)/shard_map/pallas_call | solution.py:319
  43.1 0.0 copy-start
  43.1 1.5 %constant_dynamic-update-slice_fusion.1 = f32[2,32,72,128]{3,2,1,0:T(8,128)S(1)} fusion(f32[2,32,40,128]{3,2,1,0:T(8,128)} %get-tuple-element.24), kind=kLoop, calls=%fused_computation.23 | loop fusion | bytes 2621440
  44.6 0.1 copy-done
  44.7 0.1 constant_dynamic-update-slice_fusion
  44.7 0.1 fusion.1
  44.8 0.1 collective-permute-start.4
  44.9 2.0 %collective-permute-done.4 = bf16[32,72,128]{2,1,0:T(8,128)(2,1)S(1)} collective-permute-done((bf16[32,72,128]{2,1,0:T(8,128)(2,1)S(1)}, bf16[32,72,128]{2,1,0:T(8,128)(2,1)S(1)}, u32[]{:S(2)}, u32[]{:S(2)}) %collective-permute-start.4) | collective-permute-done | bytes 589856 | tf_op jit(solution)/shard_map/ppermute | solution.py:328
  46.9 0.0 copy-start.6
  46.9 0.0 copy-start.5
  46.9 0.1 fusion
  47.1 13.9 %all_to_all.10 = bf16[4,8,72,128]{3,2,1,0:T(8,128)(2,1)S(1)} all-to-all(bf16[4,8,72,128]{3,2,1,0:T(8,128)(2,1)S(1)} %bitcast.26), channel_id=1, replica_groups={{0,8,16,24},{1,9,17,25},{2,10,18,26},{3,11,19,27},{4,12,20,28},{5,13,21..., dimensions={0} | all-to-all | bytes 1179648 | tf_op jit(solution)/shard_map/all_to_all | solution.py:332
  60.9 0.1 reduce_sum.21
  61.0 15.7 %all_to_all.11 = bf16[8,72,128]{2,1,0:T(8,128)(2,1)S(1)} all-to-all(bf16[8,72,128]{2,1,0:T(8,128)(2,1)S(1)} %reduce_sum.21), channel_id=1, replica_groups={{0,1,2,3,4,5,6,7},{8,9,10,11,12,13,14,15},{16,17,18,19,20,21,22,23},{24..., dimensions={0} | all-to-all | bytes 294912 | tf_op jit(solution)/shard_map/all_to_all | solution.py:332
  76.7 1.6 %collective-permute-start.7 = (f32[72,128]{1,0:T(8,128)S(1)}, f32[72,128]{1,0:T(8,128)S(1)}, u32[]{:S(2)}, u32[]{:S(2)}) collective-permute-start(f32[72,128]{1,0:T(8,128)S(1)} %convert_reduce_fusion), channel_id=1, source_target_pairs={{0,192},{32,224},{64,128},{96,160},{128,64},{160,96},{192,0},{224,... | collective-permute-start | bytes 110600 | tf_op jit(solution)/shard_map/ppermute | solution.py:328
  78.3 1.1 %collective-permute-start.6 = (f32[72,128]{1,0:T(8,128)S(1)}, f32[72,128]{1,0:T(8,128)S(1)}, u32[]{:S(2)}, u32[]{:S(2)}) collective-permute-start(f32[72,128]{1,0:T(8,128)S(1)} %convert_reduce_fusion), channel_id=1, source_target_pairs={{0,128},{32,160},{64,192},{96,224},{128,0},{160,32},{192,64},{224,... | collective-permute-start | bytes 110600 | tf_op jit(solution)/shard_map/ppermute | solution.py:328
  79.4 1.5 %collective-permute-start.5 = (f32[72,128]{1,0:T(8,128)S(1)}, f32[72,128]{1,0:T(8,128)S(1)}, u32[]{:S(2)}, u32[]{:S(2)}) collective-permute-start(f32[72,128]{1,0:T(8,128)S(1)} %convert_reduce_fusion), channel_id=1, source_target_pairs={{0,64},{32,96},{64,0},{96,32},{128,192},{160,224},{192,128},{224,1... | collective-permute-start | bytes 110600 | tf_op jit(solution)/shard_map/ppermute | solution.py:328
  80.9 0.0 copy-done.6
  80.9 2.5 %collective-permute-start.2 = (bf16[128,256]{1,0:T(8,128)(2,1)S(1)}, bf16[128,256]{1,0:T(8,128)(2,1)S(1)}, u32[]{:S(2)}, u32[]{:S(2)}) collective-permute-start(bf16[128,256]{1,0:T(8,128)(2,1)S(1)} %copy-done.6), channel_id=1, source_target_pairs={{0,1},{1,2},{2,3},{3,4},{4,5},{5,6},{6,7},{7,8},{8,9},{9,10},{10,1... | collective-permute-start | bytes 196616 | tf_op jit(solution)/shard_map/ppermute | solution.py:400
  83.4 0.0 copy-done.5
  83.4 5.5 %collective-permute-start.3 = (bf16[128,256]{1,0:T(8,128)(2,1)S(1)}, bf16[128,256]{1,0:T(8,128)(2,1)S(1)}, u32[]{:S(2)}, u32[]{:S(2)}) collective-permute-start(bf16[128,256]{1,0:T(8,128)(2,1)S(1)} %copy-done.5), channel_id=1, source_target_pairs={{1,0},{2,1},{3,2},{4,3},{5,4},{6,5},{7,6},{8,7},{9,8},{10,9},{11,1... | collective-permute-start | bytes 196616 | tf_op jit(solution)/shard_map/ppermute | solution.py:399
  88.9 0.0 collective-permute-done.7
  88.9 0.0 collective-permute-done.6
  88.9 0.0 collective-permute-done.5
  88.9 0.1 collective-permute-start.8
  89.0 0.1 collective-permute-done.2.low_ref
  89.1 0.0 copy-start.1
  89.1 1.6 %collective-permute-done.3.up_ref = bf16[128,256]{1,0:T(8,128)(2,1)S(1)} collective-permute-done((bf16[128,256]{1,0:T(8,128)(2,1)S(1)}, bf16[128,256]{1,0:T(8,128)(2,1)S(1)}, u32[]{:S(2)}, u32[]{:S(2)}) %collective-permute-start.3) | collective-permute-done | bytes 65568 | tf_op jit(solution)/shard_map/ppermute | solution.py:399
  90.7 0.0 copy-start.2
  90.7 0.0 copy-done.1
  90.7 0.6 copy-done.2
  91.3 2.0 %shard_map.233 = bf16[512,256]{1,0:T(8,128)(2,1)} custom-call(s32[2,128]{1,0:T(2,128)} %bitcast.34, f32[512,256]{1,0:T(8,128)} %get-tuple-element.20.own_ref, bf16[128,256]{1,0:T(8,128)(2,1)} %copy-done.1, bf16[128,256]{1,0:T(8,128)(2,1)} %copy-done.2), custom_call_target="tpu_custom_call" | custom-call | tf_op jit(solution)/shard_map/pallas_call | solution.py:323
  93.4 0.0 collective-permute-done.8
  93.4 0.6 fusion.2
  94.0 0.6 pad_maximum_fusion
  94.6 0.6 fusion.3
  95.2 0.1 fusion.7
  95.3 0.5 slice_bitcast_fusion
  (4 shorter events, 0.0 us)
Async XLA Ops:
  2.5 10.1 %collective-permute-start = (bf16[128,256]{1,0:T(8,128)(2,1)}, bf16[128,256]{1,0:T(8,128)(2,1)S(1)}, u32[]{:S(2)}, u32[]{:S(2)}) collective-permute-start(bf16[128,256]{1,0:T(8,128)(2,1)} %get-tuple-element.18), channel_id=1, source_target_pairs={{0,1},{1,2},{2,3},{3,4},{4,5},{5,6},{6,7},{7,8},{8,9},{9,10},{10,1... | collective-permute-start | bytes 196616 | tf_op jit(solution)/shard_map/ppermute | solution.py:378
  6.4 8.0 %collective-permute-start.1 = (bf16[128,256]{1,0:T(8,128)(2,1)}, bf16[128,256]{1,0:T(8,128)(2,1)S(1)}, u32[]{:S(2)}, u32[]{:S(2)}) collective-permute-start(bf16[128,256]{1,0:T(8,128)(2,1)} %get-tuple-element.19), channel_id=1, source_target_pairs={{1,0},{2,1},{3,2},{4,3},{5,4},{6,5},{7,6},{8,7},{9,8},{10,9},{11,1... | collective-permute-start | bytes 196616 | tf_op jit(solution)/shard_map/ppermute | solution.py:379
  12.6 1.7 %copy-start.3 = (bf16[128,256]{1,0:T(8,128)(2,1)}, bf16[128,256]{1,0:T(8,128)(2,1)S(1)}, u32[]{:S(2)}) copy-start(bf16[128,256]{1,0:T(8,128)(2,1)S(1)} %collective-permute-done.hlow_ref) | copy-start | bytes 196612
  14.3 0.6 copy-start.4
  43.1 1.6 %copy-start = (f32[2,32,32,128]{3,2,1,0:T(8,128)S(1)}, f32[2,32,32,128]{3,2,1,0:T(8,128)}, u32[]{:S(2)}) copy-start(f32[2,32,32,128]{3,2,1,0:T(8,128)} %get-tuple-element.25) | copy-start | bytes 3145732
  44.8 2.1 %collective-permute-start.4 = (bf16[32,72,128]{2,1,0:T(8,128)(2,1)S(1)}, bf16[32,72,128]{2,1,0:T(8,128)(2,1)S(1)}, u32[]{:S(2)}, u32[]{:S(2)}) collective-permute-start(bf16[32,72,128]{2,1,0:T(8,128)(2,1)S(1)} %fusion.1), channel_id=1, source_target_pairs={{0,32},{32,0},{64,96},{96,64},{128,160},{160,128},{192,224},{224,1... | collective-permute-start | bytes 1769480 | tf_op jit(solution)/shard_map/ppermute | solution.py:328
  46.9 34.0 %copy-start.6 = (bf16[128,256]{1,0:T(8,128)(2,1)S(1)}, bf16[128,256]{1,0:T(8,128)(2,1)}, u32[]{:S(2)}) copy-start(bf16[128,256]{1,0:T(8,128)(2,1)} %get-tuple-element.21) | copy-start | bytes 196612
  46.9 36.4 %copy-start.5 = (bf16[128,256]{1,0:T(8,128)(2,1)S(1)}, bf16[128,256]{1,0:T(8,128)(2,1)}, u32[]{:S(2)}) copy-start(bf16[128,256]{1,0:T(8,128)(2,1)} %get-tuple-element.22) | copy-start | bytes 196612
  76.7 12.2 %collective-permute-start.7 = (f32[72,128]{1,0:T(8,128)S(1)}, f32[72,128]{1,0:T(8,128)S(1)}, u32[]{:S(2)}, u32[]{:S(2)}) collective-permute-start(f32[72,128]{1,0:T(8,128)S(1)} %convert_reduce_fusion), channel_id=1, source_target_pairs={{0,192},{32,224},{64,128},{96,160},{128,64},{160,96},{192,0},{224,... | collective-permute-start | bytes 110600 | tf_op jit(solution)/shard_map/ppermute | solution.py:328
  78.3 10.6 %collective-permute-start.6 = (f32[72,128]{1,0:T(8,128)S(1)}, f32[72,128]{1,0:T(8,128)S(1)}, u32[]{:S(2)}, u32[]{:S(2)}) collective-permute-start(f32[72,128]{1,0:T(8,128)S(1)} %convert_reduce_fusion), channel_id=1, source_target_pairs={{0,128},{32,160},{64,192},{96,224},{128,0},{160,32},{192,64},{224,... | collective-permute-start | bytes 110600 | tf_op jit(solution)/shard_map/ppermute | solution.py:328
  79.4 9.5 %collective-permute-start.5 = (f32[72,128]{1,0:T(8,128)S(1)}, f32[72,128]{1,0:T(8,128)S(1)}, u32[]{:S(2)}, u32[]{:S(2)}) collective-permute-start(f32[72,128]{1,0:T(8,128)S(1)} %convert_reduce_fusion), channel_id=1, source_target_pairs={{0,64},{32,96},{64,0},{96,32},{128,192},{160,224},{192,128},{224,1... | collective-permute-start | bytes 110600 | tf_op jit(solution)/shard_map/ppermute | solution.py:328
  80.9 8.3 %collective-permute-start.2 = (bf16[128,256]{1,0:T(8,128)(2,1)S(1)}, bf16[128,256]{1,0:T(8,128)(2,1)S(1)}, u32[]{:S(2)}, u32[]{:S(2)}) collective-permute-start(bf16[128,256]{1,0:T(8,128)(2,1)S(1)} %copy-done.6), channel_id=1, source_target_pairs={{0,1},{1,2},{2,3},{3,4},{4,5},{5,6},{6,7},{7,8},{8,9},{9,10},{10,1... | collective-permute-start | bytes 196616 | tf_op jit(solution)/shard_map/ppermute | solution.py:400
  83.4 7.4 %collective-permute-start.3 = (bf16[128,256]{1,0:T(8,128)(2,1)S(1)}, bf16[128,256]{1,0:T(8,128)(2,1)S(1)}, u32[]{:S(2)}, u32[]{:S(2)}) collective-permute-start(bf16[128,256]{1,0:T(8,128)(2,1)S(1)} %copy-done.5), channel_id=1, source_target_pairs={{1,0},{2,1},{3,2},{4,3},{5,4},{6,5},{7,6},{8,7},{9,8},{10,9},{11,1... | collective-permute-start | bytes 196616 | tf_op jit(solution)/shard_map/ppermute | solution.py:399
  88.9 4.5 %collective-permute-start.8 = (f32[72,128]{1,0:T(8,128)S(1)}, f32[72,128]{1,0:T(8,128)S(1)}, u32[]{:S(2)}, u32[]{:S(2)}) collective-permute-start(f32[72,128]{1,0:T(8,128)S(1)} %add_add_fusion), channel_id=1, source_target_pairs={{0,32},{32,0},{64,96},{96,64},{128,160},{160,128},{192,224},{224,1... | collective-permute-start | bytes 110600 | tf_op jit(solution)/shard_map/ppermute | solution.py:328
  89.1 1.6 %copy-start.1 = (bf16[128,256]{1,0:T(8,128)(2,1)}, bf16[128,256]{1,0:T(8,128)(2,1)S(1)}, u32[]{:S(2)}) copy-start(bf16[128,256]{1,0:T(8,128)(2,1)S(1)} %collective-permute-done.2.low_ref) | copy-start | bytes 196612
  90.7 0.6 copy-start.2

commit v2 on v1

v2 whole, which is shorter than its diff:
```python
import functools

import jax
import jax.numpy as jnp
from jax import lax
from jax.experimental import pallas as pl
from jax.experimental.pallas import tpu as pltpu
from jax.sharding import PartitionSpec as P

D = 256
NODE = 512
EDGE = 4096
HALO = 128
TABLE = NODE + 2 * HALO
EBLOCK = 128
NBLK = EDGE // EBLOCK
CHUNK = 1024
NCHUNK = EDGE // CHUNK
PER = CHUNK // EBLOCK
LANE = 128
NORM_EPS = 1e-05
N_DOM = 32
ROWS = 64
VECTOR_ROW = 56
WINDOW = 256

BF = jnp.bfloat16
F32 = jnp.float32


def mm(a, b):
    return lax.dot_general(a, b, (((1,), (0,)), ((), ())), preferred_element_type=F32)


def mm_nt(a, b):
    return lax.dot_general(a, b, (((1,), (1,)), ((), ())), preferred_element_type=F32)


def mm_tn(a, b):
    return lax.dot_general(a, b, (((0,), (0,)), ((), ())), preferred_element_type=F32)


def as_columns(row):
    return jnp.broadcast_to(row, (LANE, LANE)).T


def one_hot_rows(row, count):
    places = lax.broadcasted_iota(jnp.int32, (count, row.shape[1]), 0).astype(jnp.int16)
    row = jnp.broadcast_to(row, (16, row.shape[1])).astype(jnp.int16)[0:1]
    return jnp.where(places == row, BF(1.0), BF(0.0))


def one_hot_cols(cols, count):
    places = lax.broadcasted_iota(jnp.int32, (cols.shape[0], LANE), 1).astype(jnp.int16)
    cols = cols.astype(jnp.int16)
    parts = [
        jnp.where(cols == places + jnp.int16(k * LANE), BF(1.0), BF(0.0))
        for k in range(count // LANE)
    ]
    return jnp.concatenate(parts, 1)


def norm_forward(values):
    centred = values - jnp.mean(values, -1, keepdims=True)
    inverse = lax.rsqrt(jnp.mean(centred * centred, -1, keepdims=True) + NORM_EPS)
    return centred * inverse, inverse


def chunk_cols(row, first, count):
    row = row - first
    hots = [
        one_hot_cols(as_columns(row[:, k * LANE : (k + 1) * LANE]), count) for k in range(PER)
    ]
    return jnp.concatenate(hots, 0)


def live_lanes(fill_ref, i):
    lanes = lax.broadcasted_iota(jnp.int32, (1, LANE), 1)
    return jnp.concatenate([lanes < fill_ref[0, i * PER + k] for k in range(PER)], 1)


def chunk_used(fill_ref, i):
    total = fill_ref[0, i * PER]
    for k in range(1, PER):
        total = total + fill_ref[0, i * PER + k]
    return total > 0


def chunk_ids(send_ref, recv_ref, fill_ref, i):
    here = pl.ds(pl.multiple_of(i * CHUNK, CHUNK), CHUNK)
    live = live_lanes(fill_ref, i)
    send = send_ref[:, here]
    recv = recv_ref[:, here]
    own = send < NODE
    low = jnp.minimum(recv, jnp.where(own, send, NODE - 1))
    high = jnp.maximum(recv, jnp.where(own, send, 0))
    low = jnp.min(jnp.where(live, low, NODE - 1))
    high = jnp.max(jnp.where(live, high, 0))
    first = jnp.minimum((low // 16) * 16, NODE - WINDOW)
    fits = high < first + WINDOW
    first = pl.multiple_of(jnp.where(fits, first, 0), 16)
    return send, jnp.where(live, recv, -1), first, fits


def pick_kernel(rows_ref, node_ref, low_ref, up_ref):
    for side, out in ((0, low_ref), (1, up_ref)):
        hot = one_hot_cols(as_columns(rows_ref[side : side + 1, :]), NODE)
        out[...] = mm(hot, node_ref[...]).astype(BF)


def local_kernel(
    send_ref,
    recv_ref,
    fill_ref,
    edge_hbm,
    node_ref,
    ewi_ref,
    eb_ref,
    half_hbm,
    edge_ref,
    half_ref,
    wp_ref,
    in_sem,
    out_sem,
):
    def fetch(i):
        here = pl.ds(i * CHUNK, CHUNK)
        return pltpu.make_async_copy(edge_hbm.at[here], edge_ref.at[here], in_sem.at[i])

    def flush(i):
        here = pl.ds(i * CHUNK, CHUNK)
        return pltpu.make_async_copy(half_ref.at[here], half_hbm.at[here], out_sem.at[i])

    for i in range(NCHUNK):
        fetch(i).start()
    wp_ref[0:D, :] = (ewi_ref[0:D, :].astype(F32) * 0.5).astype(BF)
    wp_ref[D : D + NODE, :] = (mm(node_ref[...], ewi_ref[D : 2 * D, :]) * 0.5).astype(BF)
    wp_ref[D + NODE :, :] = (
        (mm(node_ref[...], ewi_ref[2 * D :, :]) + eb_ref[...]) * 0.5
    ).astype(BF)

    def step(i, carry):
        here = pl.ds(pl.multiple_of(i * CHUNK, CHUNK), CHUNK)
        fetch(i).wait()

        @pl.when(chunk_used(fill_ref, i))
        def _():
            send, recv, first, fits = chunk_ids(send_ref, recv_ref, fill_ref, i)

            def nodes_part(first):
                return mm(
                    chunk_cols(send, first, WINDOW), wp_ref[pl.ds(D + first, WINDOW), :]
                ) + mm(
                    chunk_cols(recv, first, WINDOW), wp_ref[pl.ds(D + NODE + first, WINDOW), :]
                )

            half_ref[here, :] = mm(edge_ref[here, :], wp_ref[0:D, :]) + nodes_part(first)

            @pl.when(jnp.logical_not(fits))
            def _():
                half_ref[here, :] += nodes_part(WINDOW)

        flush(i).start()
        return carry

    lax.fori_loop(0, NCHUNK, step, 0)
    for i in range(NCHUNK):
        flush(i).wait()


def layer_kernel(
    send_ref,
    recv_ref,
    fill_ref,
    core_ref,
    half_hbm,
    edge_hbm,
    ecot_hbm,
    node_ref,
    hlow_ref,
    hup_ref,
    ncot_ref,
    ewi_ref,
    ewo_ref,
    eg_ref,
    nwi_ref,
    nb_ref,
    nwo_ref,
    ng_ref,
    gedge_hbm,
    own_ref,
    glow_ref,
    gup_ref,
    away_ref,
    kept_ref,
    half_ref,
    edge_ref,
    ecot_ref,
    gedge_ref,
    halo_ref,
    hott_ref,
    act_ref,
    normed_ref,
    inv_ref,
    agg_ref,
    back_node_ref,
    msg_ref,
    grad_ref,
    sums_ref,
    sumr_ref,
    dw0_ref,
    dwo_ref,
    dgain_ref,
    base_ref,
    share_ref,
    half_sem,
    edge_sem,
    ecot_sem,
    out_sem,
):
    def copy_of(source, target, sems, i):
        here = pl.ds(i * CHUNK, CHUNK)
        return pltpu.make_async_copy(source.at[here], target.at[here], sems.at[i])

    copy_of(half_hbm, half_ref, half_sem, 0).start()
    copy_of(edge_hbm, edge_ref, edge_sem, 0).start()

    halo = jnp.concatenate([hlow_ref[...], hup_ref[...]], 0)
    halo_ref[...] = (mm(halo, ewi_ref[D : 2 * D, :]) * 0.5).astype(BF)
    agg_ref[...] = jnp.zeros_like(agg_ref)
    gain = eg_ref[...]

    def forward(i, carry):
        here = pl.ds(pl.multiple_of(i * CHUNK, CHUNK), CHUNK)
        copy_of(half_hbm, half_ref, half_sem, i).wait()
        copy_of(edge_hbm, edge_ref, edge_sem, i).wait()

        @pl.when(i + 1 < NCHUNK)
        def _():
            copy_of(half_hbm, half_ref, half_sem, i + 1).start()
            copy_of(edge_hbm, edge_ref, edge_sem, i + 1).start()

        copy_of(ecot_hbm, ecot_ref, ecot_sem, i).start()

        @pl.when(chunk_used(fill_ref, i))
        def _():
            send, recv, first, fits = chunk_ids(send_ref, recv_ref, fill_ref, i)
            half = half_ref[here, :] + mm(chunk_cols(send, NODE, 2 * HALO), halo_ref[...])
            t = jnp.tanh(half)
            ht = half * t
            act = (half + ht).astype(BF)
            act_ref[here, :] = act
            half_ref[here, :] = (t + 1.0) * ((half - ht) + 1.0)
            normed, inverse = norm_forward(mm(act, ewo_ref[...]))
            normed_ref[here, :] = normed
            inv_ref[here, :] = jnp.broadcast_to(inverse, (CHUNK, LANE))
            message = (edge_ref[here, :].astype(F32) + gain * normed).astype(BF)
            hott = one_hot_rows(recv - first, WINDOW)
            hott_ref[i] = hott
            agg_ref[pl.ds(first, WINDOW), :] += mm(hott, message)

            @pl.when(jnp.logical_not(fits))
            def _():
                again = (edge_ref[here, :].astype(F32) + gain * normed_ref[here, :]).astype(BF)
                agg_ref[WINDOW:, :] += mm(one_hot_rows(recv - WINDOW, WINDOW), again)

        return carry

    lax.fori_loop(0, NCHUNK, forward, 0)

    both = jnp.concatenate([node_ref[...], agg_ref[...].astype(BF)], 1)
    half = (mm(both, nwi_ref[...]) + nb_ref[...]) * 0.5
    t = jnp.tanh(half)
    ht = half * t
    act = (half + ht).astype(BF)
    slope = (t + 1.0) * ((half - ht) + 1.0) * 0.5
    normed, inverse = norm_forward(mm(act, nwo_ref[...]))
    up = ncot_ref[...].astype(F32)
    c = up * ng_ref[...]
    back = (
        inverse
        * (
            c
            - jnp.mean(c, -1, keepdims=True)
            - normed * jnp.mean(c * normed, -1, keepdims=True)
        )
    ).astype(BF)
    pre_grad = (mm_nt(back, nwo_ref[...]) * slope).astype(BF)
    input_grad = mm_nt(pre_grad, nwi_ref[...])
    base_ref[...] = up + input_grad[:, 0:D]
    back_node_ref[...] = input_grad[:, D:].astype(BF)
    mean = 1.0 / 256.0

    def put(row, block):
        size = block.shape[0] // N_DOM
        block = (block * mean).reshape(N_DOM, size, D)
        for side in range(2):
            share_ref[side, :, row : row + size, :] = block[:, :, side * LANE : (side + 1) * LANE]

    put(32, mm_tn(both, pre_grad))
    put(48, mm_tn(act, back))
    node_bias = jnp.sum(pre_grad.astype(F32), 0, keepdims=True)
    node_gain = jnp.sum(up * normed, 0, keepdims=True)

    sums_ref[...] = jnp.zeros_like(sums_ref)
    sumr_ref[...] = jnp.zeros_like(sumr_ref)
    dw0_ref[...] = jnp.zeros_like(dw0_ref)
    dwo_ref[...] = jnp.zeros_like(dwo_ref)
    dgain_ref[...] = jnp.zeros_like(dgain_ref)
    wo_half = (ewo_ref[...].astype(F32) * 0.5).astype(BF)

    def backward(i, carry):
        at = pl.multiple_of(i * CHUNK, CHUNK)
        here = pl.ds(at, CHUNK)
        copy_of(ecot_hbm, ecot_ref, ecot_sem, i).wait()
        used = chunk_used(fill_ref, i)

        @pl.when(used)
        def _():
            send, recv, first, fits = chunk_ids(send_ref, recv_ref, fill_ref, i)
            slots = lax.broadcasted_iota(jnp.int32, (LANE, D), 0)
            live = jnp.concatenate(
                [slots < fill_ref[0, i * PER + k] for k in range(PER)], 0
            )
            msg_ref[...] = jnp.where(live, ecot_ref[here, :].astype(F32), 0.0) + mm(
                chunk_cols(recv, first, WINDOW), back_node_ref[pl.ds(first, WINDOW), :]
            )

            @pl.when(jnp.logical_not(fits))
            def _():
                msg_ref[...] += mm(chunk_cols(recv, WINDOW, WINDOW), back_node_ref[WINDOW:, :])

            msg = msg_ref[...]
            normed = normed_ref[here, :]
            c = msg * gain
            q = c * normed
            dgain_ref[...] += jnp.sum(q.reshape(CHUNK // 8, 8, D), 0)
            inverse = inv_ref[here, :]
            inverse = jnp.concatenate([inverse, inverse], 1)
            back = (
                inverse
                * (c - jnp.mean(c, -1, keepdims=True) - normed * jnp.mean(q, -1, keepdims=True))
            ).astype(BF)
            pre_grad = (mm_nt(back, wo_half) * half_ref[here, :]).astype(BF)
            grad_ref[...] = pre_grad
            gedge_ref[here, :] = (msg + mm_nt(pre_grad, ewi_ref[0:D, :])).astype(BF)
            dwo_ref[...] += mm_tn(act_ref[here, :], back)
            dw0_ref[...] += mm_tn(edge_ref[here, :], pre_grad)
            hott = jnp.concatenate(
                [
                    hott_ref[i],
                    one_hot_rows(send - first, WINDOW),
                    one_hot_rows(send - NODE, 2 * HALO),
                ],
                0,
            )
            sums = mm(hott, pre_grad)
            sumr_ref[pl.ds(first, WINDOW), :] += sums[0:WINDOW]
            sums_ref[pl.ds(first, WINDOW), :] += sums[WINDOW : 2 * WINDOW]
            sums_ref[NODE:, :] += sums[2 * WINDOW :]

            @pl.when(jnp.logical_not(fits))
            def _():
                hott = jnp.concatenate(
                    [one_hot_rows(recv - WINDOW, WINDOW), one_hot_rows(send - WINDOW, WINDOW)], 0
                )
                sums = mm(hott, grad_ref[...])
                sumr_ref[WINDOW:, :] += sums[0:WINDOW]
                sums_ref[WINDOW : 2 * WINDOW, :] += sums[WINDOW:]

        @pl.when(jnp.logical_not(used))
        def _():
            gedge_ref[here, :] = jnp.zeros((CHUNK, D), BF)

        copy_of(gedge_ref, gedge_hbm, out_sem, i).start()
        return carry

    lax.fori_loop(0, NCHUNK, backward, 0)

    table = jnp.concatenate([node_ref[...], hlow_ref[...], hup_ref[...]], 0)
    sums = sums_ref[...]
    sumr = sumr_ref[...].astype(BF)
    sums_bf = sums.astype(BF)
    put(
        0,
        jnp.concatenate([dw0_ref[...], mm_tn(table, sums_bf), mm_tn(node_ref[...], sumr)], 0),
    )
    put(24, dwo_ref[...])
    vectors = (
        jnp.sum(sums, 0, keepdims=True),
        jnp.sum(dgain_ref[...], 0, keepdims=True) / gain,
        node_bias,
        node_gain,
    )
    place = lax.broadcasted_iota(jnp.int32, (N_DOM, D), 1) // 8
    mine = place == lax.broadcasted_iota(jnp.int32, (N_DOM, D), 0)
    spread = jnp.concatenate([jnp.where(mine, v * mean, 0.0) for v in vectors], 1)
    source = lax.broadcasted_iota(jnp.int32, (4 * D, LANE), 0)
    target = lax.broadcasted_iota(jnp.int32, (4 * D, LANE), 1)
    moves = jnp.where(target == (source // D) * 8 + source % 8, 1.0, 0.0).astype(BF)
    large = spread.astype(BF)
    row = mm(large, moves) + mm((spread - large.astype(F32)).astype(BF), moves)
    eight = lax.broadcasted_iota(jnp.int32, (N_DOM, 8, LANE), 1)
    share_ref[0, :, VECTOR_ROW:, :] = jnp.where(eight == 0, row[:, None, :], 0.0)
    share_ref[1, :, VECTOR_ROW:, :] = jnp.zeros((N_DOM, 8, LANE), F32)
    core = core_ref[0, 0]
    kept_ref[...] = share_ref[core]
    away_ref[...] = share_ref[1 - core].astype(BF)
    table_grad = mm_nt(sums_bf, ewi_ref[D : 2 * D, :])
    own_ref[...] = base_ref[...] + mm_nt(sumr, ewi_ref[2 * D :, :]) + table_grad[0:NODE]
    glow_ref[...] = table_grad[NODE : NODE + HALO].astype(BF)
    gup_ref[...] = table_grad[NODE + HALO :].astype(BF)
    for i in range(NCHUNK):
        copy_of(gedge_ref, gedge_hbm, out_sem, i).wait()


def finish_kernel(rows_ref, own_ref, low_ref, up_ref, out_ref):
    hots = jnp.concatenate(
        [one_hot_rows(rows_ref[0:1, :], NODE), one_hot_rows(rows_ref[1:2, :], NODE)], 1
    )
    parts = jnp.concatenate([low_ref[...], up_ref[...]], 0)
    out_ref[...] = (own_ref[...] + mm(hots, parts)).astype(BF)


def unpack_kernel(core_ref, mine_ref, other_ref, ewi_ref, ewo_ref, nwi_ref, nwo_ref, vec_ref):
    flip = core_ref[0, 0] == 1
    mine = mine_ref[...]
    other = other_ref[...]
    both = jnp.concatenate([jnp.where(flip, other, mine), jnp.where(flip, mine, other)], 1)
    ewi_ref[...] = both[0:24]
    ewo_ref[...] = both[24:32]
    nwi_ref[...] = both[32:48]
    nwo_ref[...] = both[48:56]
    vec_ref[...] = both[VECTOR_ROW : VECTOR_ROW + 8, 0:LANE]


def on_device(kernel, outs, scratch, specs, out_specs=None):
    vmem = pl.BlockSpec(memory_space=pltpu.VMEM)
    kinds = {
        "v": vmem,
        "s": pl.BlockSpec(memory_space=pltpu.SMEM),
        "a": pl.BlockSpec(memory_space=pl.ANY),
    }
    flat, tree = jax.tree.flatten(outs)
    out_specs = out_specs or "v" * len(flat)
    return pl.pallas_call(
        kernel,
        out_shape=outs,
        in_specs=[kinds[k] for k in specs],
        out_specs=jax.tree.unflatten(tree, [kinds[k] for k in out_specs]),
        scratch_shapes=scratch,
        compiler_params=pltpu.CompilerParams(vmem_limit_bytes=56 * 1024 * 1024),
    )


def shape(*dims, dtype=F32):
    return jax.ShapeDtypeStruct(dims, dtype)


def pick(rows, node):
    outs = (shape(HALO, D, dtype=BF),) * 2
    return on_device(pick_kernel, outs, [], "vv")(rows, node)


def local(*args):
    scratch = [
        pltpu.VMEM((EDGE, D), BF),
        pltpu.VMEM((EDGE, D), F32),
        pltpu.VMEM((D + 2 * NODE, D), BF),
        pltpu.SemaphoreType.DMA((NCHUNK,)),
        pltpu.SemaphoreType.DMA((NCHUNK,)),
    ]
    return on_device(local_kernel, shape(EDGE, D), scratch, "vvsavvv", "a")(*args)


def layer(*args):
    outs = (
        shape(EDGE, D, dtype=BF),
        shape(NODE, D),
        shape(HALO, D, dtype=BF),
        shape(HALO, D, dtype=BF),
        shape(N_DOM, ROWS, LANE, dtype=BF),
        shape(N_DOM, ROWS, LANE),
    )
    scratch = [
        pltpu.VMEM((EDGE, D), F32),
        pltpu.VMEM((EDGE, D), BF),
        pltpu.VMEM((EDGE, D), BF),
        pltpu.VMEM((EDGE, D), BF),
        pltpu.VMEM((2 * HALO, D), BF),
        pltpu.VMEM((NCHUNK, WINDOW, CHUNK), BF),
        pltpu.VMEM((EDGE, D), BF),
        pltpu.VMEM((EDGE, D), F32),
        pltpu.VMEM((EDGE, LANE), F32),
        pltpu.VMEM((NODE, D), F32),
        pltpu.VMEM((NODE, D), BF),
        pltpu.VMEM((CHUNK, D), F32),
        pltpu.VMEM((CHUNK, D), BF),
        pltpu.VMEM((TABLE, D), F32),
        pltpu.VMEM((NODE, D), F32),
        pltpu.VMEM((D, D), F32),
        pltpu.VMEM((D, D), F32),
        pltpu.VMEM((8, D), F32),
        pltpu.VMEM((NODE, D), F32),
        pltpu.VMEM((2, N_DOM, ROWS, LANE), F32),
        pltpu.SemaphoreType.DMA((NCHUNK,)),
        pltpu.SemaphoreType.DMA((NCHUNK,)),
        pltpu.SemaphoreType.DMA((NCHUNK,)),
        pltpu.SemaphoreType.DMA((NCHUNK,)),
    ]
    return on_device(layer_kernel, outs, scratch, "vvssaaavvvvvvvvvvv", "avvvvv")(*args)


def finish(rows, own, low, up):
    return on_device(finish_kernel, shape(NODE, D, dtype=BF), [], "vvvv")(rows, own, low, up)


def unpack(core, mine, other):
    outs = (shape(24, D), shape(8, D), shape(16, D), shape(8, D), shape(8, LANE))
    return on_device(unpack_kernel, outs, [], "svv")(core, mine, other)


def swap(values, axis, flip):
    count = lax.axis_size(axis)
    return lax.ppermute(values, axis, [(i, i ^ flip) for i in range(count)])


def exchange_sum(values, axis, groups):
    parts = lax.all_to_all(values, axis, 0, 0, tiled=True, axis_index_groups=groups)
    return jnp.sum(parts.astype(F32), 0)


def per_device(
    node_latent,
    edge_latent,
    node_cot,
    edge_cot,
    edge_w_in,
    edge_b_in,
    edge_w_out,
    edge_gain,
    node_w_in,
    node_b_in,
    node_w_out,
    node_gain,
    edge_senders,
    edge_receivers,
    block_fill,
    send_rows,
):
    node_rows = node_latent[0]
    lists = send_rows[0]
    count = lax.axis_size("dom")
    rise = [(i, i + 1) for i in range(count - 1)]
    fall = [(i + 1, i) for i in range(count - 1)]
    core = lax.rem(lax.axis_index("rep"), 2).reshape(1, 1)
    to_lower, to_upper = pick(lists, node_rows)
    halo_lower = lax.ppermute(to_upper, "dom", rise)
    halo_upper = lax.ppermute(to_lower, "dom", fall)
    half = local(
        edge_senders,
        edge_receivers,
        block_fill,
        edge_latent[0],
        node_rows,
        edge_w_in,
        edge_b_in[None],
    )
    gedge, own, glow, gup, away, kept = layer(
        edge_senders,
        edge_receivers,
        block_fill,
        core,
        half,
        edge_latent[0],
        edge_cot[0],
        node_rows,
        halo_lower,
        halo_upper,
        node_cot[0],
        edge_w_in,
        edge_w_out,
        edge_gain[None],
        node_w_in,
        node_b_in[None],
        node_w_out,
        node_gain[None],
    )
    back_upper = lax.ppermute(glow, "dom", fall)
    back_lower = lax.ppermute(gup, "dom", rise)
    same_z = [[y * 8 + z for y in range(4)] for z in range(8)]
    same_y = [[y * 8 + z for z in range(8)] for y in range(4)]
    values = (kept + swap(away, "rep", 1).astype(F32)).astype(BF)
    values = exchange_sum(values.reshape(4, 8, ROWS, LANE), "dom", same_z).astype(BF)
    values, back_lower, back_upper = lax.optimization_barrier((values, back_lower, back_upper))
    values = exchange_sum(values, "dom", same_y)
    others = [swap(values, "rep", flip) for flip in (2, 4, 6)]
    grad_nodes = finish(lists, own, back_lower, back_upper)
    values = values + others[0] + others[1] + others[2]
    ewi, ewo, nwi, nwo, vec = unpack(core, values, swap(values, "rep", 1))
    return (
        grad_nodes[None],
        gedge[None],
        ewi,
        vec[0, 0:8],
        ewo,
        vec[0, 8:16],
        nwi,
        vec[0, 16:24],
        nwo,
        vec[0, 24:32],
    )


def solution(mesh):
    placed = (
        P("rep", "dom", None),
        P("rep", "dom", None),
        P("rep", "dom", None),
        P("rep", "dom", None),
        P(),
        P(),
        P(),
        P(),
        P(),
        P(),
        P(),
        P(),
        P("rep", "dom"),
        P("rep", "dom"),
        P("rep", "dom"),
        P("rep", "dom", None),
    )
    return jax.shard_map(
        per_device,
        mesh=mesh,
        in_specs=placed,
        out_specs=(
            P("rep", "dom", None),
            P("rep", "dom", None),
            P("dom", None),
            P("dom"),
            P("dom", None),
            P("dom"),
            P("dom", None),
            P("dom"),
            P("dom", None),
            P("dom"),
        ),
        check_vma=False,
    )
```

time: 96.2 us -> 89.1 us (0.926)
  the two profiles are of different devices: /device:TPU:10 before, /device:TPU:1 now
where the time goes in v2:
time: 89.1 us; the launch traced here: 88.7 us
  starting transfers between devices  30 us (34%)
  Pallas kernels  28.2 us (32%)
  blocking collectives  12.9 us (14%)
  waiting for transfers between devices  11.9 us (13%)
  local copies, waits for them, and re-layouts  2.67 us (3%)
  other arithmetic  2.28 us (3%)
    pallas_call x1, Pallas kernels, layer(): on_device(layer_kernel, outs, scratch, 'vvssaaavvvvvvvvvvv', 'avvvvv')  16.8 us
    all_to_all x1, starting transfers between devices, exchange_sum(): lax.all_to_all(values, axis, 0, 0, tiled=True, axis_index_groups=groups)  12.9 us
    all_to_all x1, blocking collectives, exchange_sum(): lax.all_to_all(values, axis, 0, 0, tiled=True, axis_index_groups=groups)  12.9 us
    ppermute x5, starting transfers between devices, swap(): return lax.ppermute(values, axis, [(i, i ^ flip) for i in range(count)])  8.85 us
    all_to_all x1, waiting for transfers between devices, exchange_sum(): lax.all_to_all(values, axis, 0, 0, tiled=True, axis_index_groups=groups)  6.31 us
    pallas_call x1, Pallas kernels, local(): on_device(local_kernel, shape(EDGE, D), scratch, 'vvsavvv', 'a')(*args)  6.09 us
    ppermute x5, waiting for transfers between devices, swap(): return lax.ppermute(values, axis, [(i, i ^ flip) for i in range(count)])  5.61 us
    ppermute x1, starting transfers between devices, per_device(): halo_lower = lax.ppermute(to_upper, 'dom', rise)  4.36 us
  transfers between devices with their start and end apart: 10, of which 4 were waited for; matrix products, arithmetic and copies ran while one was open for 0% of the time, Pallas kernels for 9%

profile of v2, /device:TPU:1, one launch (start us, length us, event | category | flops | bytes accessed | tf_op | source)
XLA Modules:
  0.0 88.7 jit_solution(4460728070375852324)
XLA Ops:
  0.6 1.9 %shard_map.232 = (bf16[128,256]{1,0:T(8,128)(2,1)}, bf16[128,256]{1,0:T(8,128)(2,1)}) custom-call(s32[2,128]{1,0:T(2,128)} %bitcast.29, bf16[512,256]{1,0:T(8,128)(2,1)} %bitcast.23), custom_call_target="tpu_custom_call" | custom-call | tf_op jit(solution)/shard_map/pallas_call | solution.py:462
  2.5 4.4 %collective-permute-start = (bf16[128,256]{1,0:T(8,128)(2,1)}, bf16[128,256]{1,0:T(8,128)(2,1)S(1)}, u32[]{:S(2)}, u32[]{:S(2)}) collective-permute-start(bf16[128,256]{1,0:T(8,128)(2,1)} %get-tuple-element.26), channel_id=1, source_target_pairs={{0,1},{1,2},{2,3},{3,4},{4,5},{5,6},{6,7},{7,8},{8,9},{9,10},{10,1... | collective-permute-start | bytes 196616 | tf_op jit(solution)/shard_map/ppermute | solution.py:558
  6.9 1.3 %collective-permute-start.1 = (bf16[128,256]{1,0:T(8,128)(2,1)}, bf16[128,256]{1,0:T(8,128)(2,1)S(1)}, u32[]{:S(2)}, u32[]{:S(2)}) collective-permute-start(bf16[128,256]{1,0:T(8,128)(2,1)} %get-tuple-element.27), channel_id=1, source_target_pairs={{1,0},{2,1},{3,2},{4,3},{5,4},{6,5},{7,6},{8,7},{9,8},{10,9},{11,1... | collective-permute-start | bytes 196616 | tf_op jit(solution)/shard_map/ppermute | solution.py:559
  8.2 6.1 %shard_map.231.half_hbm = f32[4096,256]{1,0:T(8,128)} custom-call(s32[1,4096]{1,0:T(1,128)} %send_ref.3, s32[1,4096]{1,0:T(1,128)} %recv_ref.3, s32[1,32]{1,0:T(1,128)} %fill_ref.3, bf16[4096,256]{1,0:T(8,128)(2,1)} %bitcast.21, bf16[512,256]{1,0:T(8,128)(2,1)} %bitcast.24, bf16[768,256]{1,0:T(8,128)(2,1)} %ewi_ref.3, f32[1,256]{1,0:T(1,128)} %bitcast.31), custom_call_target="tpu_custom_call" | custom-call | tf_op jit(solution)/shard_map/pallas_call | solution.py:473
  14.3 0.0 collective-permute-done.hlow_ref
  14.3 0.0 copy-start.1
  14.3 0.0 collective-permute-done.1.hup_ref
  14.3 0.0 copy-start.2
  14.3 0.6 copy-done.1
  14.9 0.0 copy-done.2
  15.0 16.8 %shard_map.233 = (bf16[4096,256]{1,0:T(8,128)(2,1)}, f32[512,256]{1,0:T(8,128)}, bf16[128,256]{1,0:T(8,128)(2,1)}, bf16[128,256]{1,0:T(8,128)(2,1)}, bf16[32,64,...) custom-call(s32[1,4096]{1,0:T(1,128)} %send_ref.3, s32[1,4096]{1,0:T(1,128)} %recv_ref.3, s32[1,32]{1,0:T(1,128)} %fill_ref.3, ...), custom_call_target="tpu_custom_call" | custom-call | tf_op jit(solution)/shard_map/pallas_call | solution.py:511
  31.8 0.0 copy-start.7
  31.8 0.0 copy-start.6
  31.8 0.1 collective-permute-start.2
  31.9 2.1 %collective-permute-done.2 = bf16[32,64,128]{2,1,0:T(8,128)(2,1)S(1)} collective-permute-done((bf16[32,64,128]{2,1,0:T(8,128)(2,1)}, bf16[32,64,128]{2,1,0:T(8,128)(2,1)S(1)}, u32[]{:S(2)}, u32[]{:S(2)}) %collective-permute-start.2) | collective-permute-done | bytes 524320 | tf_op jit(solution)/shard_map/ppermute | solution.py:525
  34.0 2.2 %add_convert_fusion = bf16[32,64,128]{2,1,0:T(8,128)(2,1)} fusion(f32[32,64,128]{2,1,0:T(8,128)} %get-tuple-element.29, bf16[32,64,128]{2,1,0:T(8,128)(2,1)S(1)} %collective-permute-done.2), kind=kLoop, calls=%fused_computation | loop fusion | flops 786432 | bytes 2097152 | tf_op jit(solution)/shard_map/convert_element_type | solution.py:593
  36.2 12.9 %all-to-all-start = ((bf16[4,8,64,128]{3,2,1,0:T(8,128)(2,1)}), bf16[4,8,64,128]{3,2,1,0:T(8,128)(2,1)S(1)}, u32[]{:S(2)}, u32[]{:S(2)}) async-start(bf16[4,8,64,128]{3,2,1,0:T(8,128)(2,1)} %bitcast.10), calls=%async_computation | async-start | bytes 1048576 | tf_op jit(solution)/shard_map/all_to_all | solution.py:529
  49.1 0.0 copy-done.7
  49.1 1.3 %collective-permute-start.3 = (bf16[128,256]{1,0:T(8,128)(2,1)S(1)}, bf16[128,256]{1,0:T(8,128)(2,1)S(1)}, u32[]{:S(2)}, u32[]{:S(2)}) collective-permute-start(bf16[128,256]{1,0:T(8,128)(2,1)S(1)} %copy-done.7), channel_id=1, source_target_pairs={{0,1},{1,2},{2,3},{3,4},{4,5},{5,6},{6,7},{7,8},{8,9},{9,10},{10,1... | collective-permute-start | bytes 196616 | tf_op jit(solution)/shard_map/ppermute | solution.py:590
  50.4 0.0 copy-done.6
  50.4 1.3 %collective-permute-start.4 = (bf16[128,256]{1,0:T(8,128)(2,1)S(1)}, bf16[128,256]{1,0:T(8,128)(2,1)S(1)}, u32[]{:S(2)}, u32[]{:S(2)}) collective-permute-start(bf16[128,256]{1,0:T(8,128)(2,1)S(1)} %copy-done.6), channel_id=1, source_target_pairs={{1,0},{2,1},{3,2},{4,3},{5,4},{6,5},{7,6},{8,7},{9,8},{10,9},{11,1... | collective-permute-start | bytes 196616 | tf_op jit(solution)/shard_map/ppermute | solution.py:589
  51.7 6.3 %all-to-all-done = bf16[4,8,64,128]{3,2,1,0:T(8,128)(2,1)S(1)} async-done(((bf16[4,8,64,128]{3,2,1,0:T(8,128)(2,1)}), bf16[4,8,64,128]{3,2,1,0:T(8,128)(2,1)S(1)}, u32[]{:S(2)}, u32[]{:S(2)}) %all-to-all-start) | async-done | bytes 524320 | tf_op jit(solution)/shard_map/all_to_all | solution.py:529
  58.0 0.1 reduce_sum.21
  58.1 0.0 collective-permute-done.3.low_ref
  58.1 0.0 copy-start.3
  58.1 0.0 collective-permute-done.4.up_ref
  58.1 0.0 copy-start.4
  58.1 12.9 %all_to_all.10 = bf16[8,64,128]{2,1,0:T(8,128)(2,1)S(1)} all-to-all(bf16[8,64,128]{2,1,0:T(8,128)(2,1)S(1)} %reduce_sum.21), channel_id=1, replica_groups={{0,1,2,3,4,5,6,7},{8,9,10,11,12,13,14,15},{16,17,18,19,20,21,22,23},{24..., dimensions={0} | all-to-all | bytes 262144 | tf_op jit(solution)/shard_map/all_to_all | solution.py:529
  71.0 2.7 %collective-permute-start.7 = (f32[64,128]{1,0:T(8,128)S(1)}, f32[64,128]{1,0:T(8,128)S(1)}, u32[]{:S(2)}, u32[]{:S(2)}) collective-permute-start(f32[64,128]{1,0:T(8,128)S(1)} %convert_reduce_fusion), channel_id=1, source_target_pairs={{0,192},{32,224},{64,128},{96,160},{128,64},{160,96},{192,0},{224,... | collective-permute-start | bytes 98312 | tf_op jit(solution)/shard_map/ppermute | solution.py:525
  73.7 0.8 collective-permute-start.6
  74.4 0.0 collective-permute-start.5
  74.4 0.6 collective-permute-done.7
  75.1 2.9 %collective-permute-done.6 = f32[64,128]{1,0:T(8,128)S(1)} collective-permute-done((f32[64,128]{1,0:T(8,128)S(1)}, f32[64,128]{1,0:T(8,128)S(1)}, u32[]{:S(2)}, u32[]{:S(2)}) %collective-permute-start.6) | collective-permute-done | bytes 32800 | tf_op jit(solution)/shard_map/ppermute | solution.py:525
  77.9 0.0 collective-permute-done.5
  78.0 0.0 copy-start
  78.0 5.3 %collective-permute-start.8 = (f32[64,128]{1,0:T(8,128)S(1)}, f32[64,128]{1,0:T(8,128)S(1)}, u32[]{:S(2)}, u32[]{:S(2)}) collective-permute-start(f32[64,128]{1,0:T(8,128)S(1)} %add_add_fusion.mine_ref), channel_id=1, source_target_pairs={{0,32},{32,0},{64,96},{96,64},{128,160},{160,128},{192,224},{224,1... | collective-permute-start | bytes 98312 | tf_op jit(solution)/shard_map/ppermute | solution.py:525
  83.3 0.0 copy-done.3
  83.3 0.0 copy-done.4
  83.3 2.0 %shard_map.234 = bf16[512,256]{1,0:T(8,128)(2,1)} custom-call(s32[2,128]{1,0:T(2,128)} %bitcast.30, f32[512,256]{1,0:T(8,128)} %get-tuple-element.28.own_ref, bf16[128,256]{1,0:T(8,128)(2,1)} %copy-done.3, bf16[128,256]{1,0:T(8,128)(2,1)} %copy-done.4), custom_call_target="tpu_custom_call" | custom-call | tf_op jit(solution)/shard_map/pallas_call | solution.py:515
  85.2 0.0 collective-permute-done.8.other_ref
  85.2 0.0 copy-done
  85.3 0.0 copy-start.5
  85.3 0.6 copy-done.5
  85.9 1.4 %shard_map.235 = (f32[24,256]{1,0:T(8,128)}, f32[8,256]{1,0:T(8,128)}, f32[16,256]{1,0:T(8,128)}, f32[8,256]{1,0:T(8,128)}, f32[8,128]{1,0:T(8,128)}) custom-call(s32[1,1]{1,0:T(1,128)} %bitcast.1.core_ref, f32[64,128]{1,0:T(8,128)} %copy-done, f32[64,128]{1,0:T(8,128)} %copy-done.5), custom_call_target="tpu_custom_call" | custom-call | tf_op jit(solution)/shard_map/pallas_call | solution.py:520
  87.3 1.4 %slice_bitcast_fusion = (f32[8]{0:T(128)}, f32[8]{0:T(128)}, f32[8]{0:T(128)}, f32[8]{0:T(128)}) fusion(f32[8,128]{1,0:T(8,128)} %get-tuple-element.38), kind=kLoop, calls=%fused_computation.3 | loop fusion | bytes 256 | tf_op jit(solution)/shard_map/squeeze | solution.py:611
  (2 shorter events, 0.0 us)
Async XLA Ops:
  2.5 11.8 %collective-permute-start = (bf16[128,256]{1,0:T(8,128)(2,1)}, bf16[128,256]{1,0:T(8,128)(2,1)S(1)}, u32[]{:S(2)}, u32[]{:S(2)}) collective-permute-start(bf16[128,256]{1,0:T(8,128)(2,1)} %get-tuple-element.26), channel_id=1, source_target_pairs={{0,1},{1,2},{2,3},{3,4},{4,5},{5,6},{6,7},{7,8},{8,9},{9,10},{10,1... | collective-permute-start | bytes 196616 | tf_op jit(solution)/shard_map/ppermute | solution.py:558
  6.9 7.4 %collective-permute-start.1 = (bf16[128,256]{1,0:T(8,128)(2,1)}, bf16[128,256]{1,0:T(8,128)(2,1)S(1)}, u32[]{:S(2)}, u32[]{:S(2)}) collective-permute-start(bf16[128,256]{1,0:T(8,128)(2,1)} %get-tuple-element.27), channel_id=1, source_target_pairs={{1,0},{2,1},{3,2},{4,3},{5,4},{6,5},{7,6},{8,7},{9,8},{10,9},{11,1... | collective-permute-start | bytes 196616 | tf_op jit(solution)/shard_map/ppermute | solution.py:559
  14.3 0.6 copy-start.1
  14.3 0.6 copy-start.2
  31.8 17.3 %copy-start.7 = (bf16[128,256]{1,0:T(8,128)(2,1)S(1)}, bf16[128,256]{1,0:T(8,128)(2,1)}, u32[]{:S(2)}) copy-start(bf16[128,256]{1,0:T(8,128)(2,1)} %get-tuple-element.31) | copy-start | bytes 196612
  31.8 18.6 %copy-start.6 = (bf16[128,256]{1,0:T(8,128)(2,1)S(1)}, bf16[128,256]{1,0:T(8,128)(2,1)}, u32[]{:S(2)}) copy-start(bf16[128,256]{1,0:T(8,128)(2,1)} %get-tuple-element.32) | copy-start | bytes 196612
  31.8 2.2 %collective-permute-start.2 = (bf16[32,64,128]{2,1,0:T(8,128)(2,1)}, bf16[32,64,128]{2,1,0:T(8,128)(2,1)S(1)}, u32[]{:S(2)}, u32[]{:S(2)}) collective-permute-start(bf16[32,64,128]{2,1,0:T(8,128)(2,1)} %get-tuple-element.30), channel_id=1, source_target_pairs={{0,32},{32,0},{64,96},{96,64},{128,160},{160,128},{192,224},{224,1... | collective-permute-start | bytes 1572872 | tf_op jit(solution)/shard_map/ppermute | solution.py:525
  36.2 21.8 %all-to-all-start = ((bf16[4,8,64,128]{3,2,1,0:T(8,128)(2,1)}), bf16[4,8,64,128]{3,2,1,0:T(8,128)(2,1)S(1)}, u32[]{:S(2)}, u32[]{:S(2)}) async-start(bf16[4,8,64,128]{3,2,1,0:T(8,128)(2,1)} %bitcast.10), calls=%async_computation | async-start | bytes 1048576 | tf_op jit(solution)/shard_map/all_to_all | solution.py:529
  49.1 9.0 %collective-permute-start.3 = (bf16[128,256]{1,0:T(8,128)(2,1)S(1)}, bf16[128,256]{1,0:T(8,128)(2,1)S(1)}, u32[]{:S(2)}, u32[]{:S(2)}) collective-permute-start(bf16[128,256]{1,0:T(8,128)(2,1)S(1)} %copy-done.7), channel_id=1, source_target_pairs={{0,1},{1,2},{2,3},{3,4},{4,5},{5,6},{6,7},{7,8},{8,9},{9,10},{10,1... | collective-permute-start | bytes 196616 | tf_op jit(solution)/shard_map/ppermute | solution.py:590
  50.4 7.7 %collective-permute-start.4 = (bf16[128,256]{1,0:T(8,128)(2,1)S(1)}, bf16[128,256]{1,0:T(8,128)(2,1)S(1)}, u32[]{:S(2)}, u32[]{:S(2)}) collective-permute-start(bf16[128,256]{1,0:T(8,128)(2,1)S(1)} %copy-done.6), channel_id=1, source_target_pairs={{1,0},{2,1},{3,2},{4,3},{5,4},{6,5},{7,6},{8,7},{9,8},{10,9},{11,1... | collective-permute-start | bytes 196616 | tf_op jit(solution)/shard_map/ppermute | solution.py:589
  58.1 25.2 %copy-start.3 = (bf16[128,256]{1,0:T(8,128)(2,1)}, bf16[128,256]{1,0:T(8,128)(2,1)S(1)}, u32[]{:S(2)}) copy-start(bf16[128,256]{1,0:T(8,128)(2,1)S(1)} %collective-permute-done.3.low_ref) | copy-start | bytes 196612
  58.1 25.2 %copy-start.4 = (bf16[128,256]{1,0:T(8,128)(2,1)}, bf16[128,256]{1,0:T(8,128)(2,1)S(1)}, u32[]{:S(2)}) copy-start(bf16[128,256]{1,0:T(8,128)(2,1)S(1)} %collective-permute-done.4.up_ref) | copy-start | bytes 196612
  71.0 4.1 %collective-permute-start.7 = (f32[64,128]{1,0:T(8,128)S(1)}, f32[64,128]{1,0:T(8,128)S(1)}, u32[]{:S(2)}, u32[]{:S(2)}) collective-permute-start(f32[64,128]{1,0:T(8,128)S(1)} %convert_reduce_fusion), channel_id=1, source_target_pairs={{0,192},{32,224},{64,128},{96,160},{128,64},{160,96},{192,0},{224,... | collective-permute-start | bytes 98312 | tf_op jit(solution)/shard_map/ppermute | solution.py:525
  73.7 4.3 %collective-permute-start.6 = (f32[64,128]{1,0:T(8,128)S(1)}, f32[64,128]{1,0:T(8,128)S(1)}, u32[]{:S(2)}, u32[]{:S(2)}) collective-permute-start(f32[64,128]{1,0:T(8,128)S(1)} %convert_reduce_fusion), channel_id=1, source_target_pairs={{0,128},{32,160},{64,192},{96,224},{128,0},{160,32},{192,64},{224,... | collective-permute-start | bytes 98312 | tf_op jit(solution)/shard_map/ppermute | solution.py:525
  74.4 3.5 %collective-permute-start.5 = (f32[64,128]{1,0:T(8,128)S(1)}, f32[64,128]{1,0:T(8,128)S(1)}, u32[]{:S(2)}, u32[]{:S(2)}) collective-permute-start(f32[64,128]{1,0:T(8,128)S(1)} %convert_reduce_fusion), channel_id=1, source_target_pairs={{0,64},{32,96},{64,0},{96,32},{128,192},{160,224},{192,128},{224,1... | collective-permute-start | bytes 98312 | tf_op jit(solution)/shard_map/ppermute | solution.py:525
  78.0 7.3 %copy-start = (f32[64,128]{1,0:T(8,128)}, f32[64,128]{1,0:T(8,128)S(1)}, u32[]{:S(2)}) copy-start(f32[64,128]{1,0:T(8,128)S(1)} %add_add_fusion.mine_ref) | copy-start | bytes 98308
  78.0 7.3 %collective-permute-start.8 = (f32[64,128]{1,0:T(8,128)S(1)}, f32[64,128]{1,0:T(8,128)S(1)}, u32[]{:S(2)}, u32[]{:S(2)}) collective-permute-start(f32[64,128]{1,0:T(8,128)S(1)} %add_add_fusion.mine_ref), channel_id=1, source_target_pairs={{0,32},{32,0},{64,96},{96,64},{128,160},{160,128},{192,224},{224,1... | collective-permute-start | bytes 98312 | tf_op jit(solution)/shard_map/ppermute | solution.py:525
  85.3 0.6 copy-start.5

commit v3 on v2

v3 whole, which is shorter than its diff:
```python
import functools

import jax
import jax.numpy as jnp
from jax import lax
from jax.experimental import pallas as pl
from jax.experimental.pallas import tpu as pltpu
from jax.sharding import PartitionSpec as P

D = 256
NODE = 512
EDGE = 4096
HALO = 128
TABLE = NODE + 2 * HALO
EBLOCK = 128
NBLK = EDGE // EBLOCK
CHUNK = 1024
NCHUNK = EDGE // CHUNK
PER = CHUNK // EBLOCK
LANE = 128
NORM_EPS = 1e-05
N_DOM = 32
ROWS = 64
VECTOR_ROW = 56
WINDOW = 256

BF = jnp.bfloat16
F32 = jnp.float32


def mm(a, b):
    return lax.dot_general(a, b, (((1,), (0,)), ((), ())), preferred_element_type=F32)


def mm_nt(a, b):
    return lax.dot_general(a, b, (((1,), (1,)), ((), ())), preferred_element_type=F32)


def mm_tn(a, b):
    return lax.dot_general(a, b, (((0,), (0,)), ((), ())), preferred_element_type=F32)


def as_columns(row):
    return jnp.broadcast_to(row, (LANE, LANE)).T


def one_hot_rows(row, count):
    places = lax.broadcasted_iota(jnp.int32, (count, row.shape[1]), 0).astype(jnp.int16)
    row = jnp.broadcast_to(row, (16, row.shape[1])).astype(jnp.int16)[0:1]
    return jnp.where(places == row, BF(1.0), BF(0.0))


def one_hot_cols(cols, count):
    places = lax.broadcasted_iota(jnp.int32, (cols.shape[0], LANE), 1).astype(jnp.int16)
    cols = cols.astype(jnp.int16)
    parts = [
        jnp.where(cols == places + jnp.int16(k * LANE), BF(1.0), BF(0.0))
        for k in range(count // LANE)
    ]
    return jnp.concatenate(parts, 1)


def norm_forward(values):
    centred = values - jnp.mean(values, -1, keepdims=True)
    inverse = lax.rsqrt(jnp.mean(centred * centred, -1, keepdims=True) + NORM_EPS)
    return centred * inverse, inverse


def chunk_cols(row, first, count):
    row = row - first
    hots = [
        one_hot_cols(as_columns(row[:, k * LANE : (k + 1) * LANE]), count) for k in range(PER)
    ]
    return jnp.concatenate(hots, 0)


def live_lanes(fill_ref, i):
    lanes = lax.broadcasted_iota(jnp.int32, (1, LANE), 1)
    return jnp.concatenate([lanes < fill_ref[0, i * PER + k] for k in range(PER)], 1)


def chunk_used(fill_ref, i):
    total = fill_ref[0, i * PER]
    for k in range(1, PER):
        total = total + fill_ref[0, i * PER + k]
    return total > 0


def chunk_ids(send_ref, recv_ref, fill_ref, i):
    here = pl.ds(i * CHUNK, CHUNK)
    return send_ref[:, here], jnp.where(live_lanes(fill_ref, i), recv_ref[:, here], -1)


def windows(send_ref, recv_ref, fill_ref):
    firsts, all_fit = [], None
    for i in range(NCHUNK):
        here = pl.ds(i * CHUNK, CHUNK)
        live = live_lanes(fill_ref, i)
        send = send_ref[:, here]
        recv = recv_ref[:, here]
        own = send < NODE
        low = jnp.minimum(recv, jnp.where(own, send, NODE - 1))
        high = jnp.maximum(recv, jnp.where(own, send, 0))
        low = jnp.min(jnp.where(live, low, NODE - 1))
        high = jnp.max(jnp.where(live, high, 0))
        first = jnp.minimum((low // 16) * 16, NODE - WINDOW)
        fits = high < first + WINDOW
        firsts.append(pl.multiple_of(first, 16))
        all_fit = fits if all_fit is None else jnp.logical_and(all_fit, fits)
    return firsts, all_fit


def over_chunks(step, idle, fill_ref, firsts):
    if firsts is not None:
        for i in range(NCHUNK):
            step(i, firsts[i], WINDOW)
        return
    for i in range(NCHUNK - 1):
        step(i, 0, NODE)
    used = chunk_used(fill_ref, NCHUNK - 1)

    @pl.when(used)
    def _():
        step(NCHUNK - 1, 0, NODE)

    @pl.when(jnp.logical_not(used))
    def _():
        idle(NCHUNK - 1)


def either_way(body, send_ref, recv_ref, fill_ref):
    firsts, all_fit = windows(send_ref, recv_ref, fill_ref)

    @pl.when(all_fit)
    def _():
        body(firsts)

    @pl.when(jnp.logical_not(all_fit))
    def _():
        body(None)


def fetch_all(sources, targets, sems):
    copies = [
        pltpu.make_async_copy(source, target, sems.at[k])
        for k, (source, target) in enumerate(zip(sources, targets))
    ]
    for copy in copies:
        copy.start()
    return copies


def pick_kernel(rows_hbm, node_hbm, low_ref, up_ref, rows_ref, node_ref, sems):
    for copy in fetch_all((rows_hbm, node_hbm), (rows_ref, node_ref), sems):
        copy.wait()
    for side, out in ((0, low_ref), (1, up_ref)):
        hot = one_hot_cols(as_columns(rows_ref[side : side + 1, :]), NODE)
        out[...] = mm(hot, node_ref[...]).astype(BF)


def local_kernel(
    send_hbm,
    recv_hbm,
    fill_hbm,
    edge_hbm,
    node_hbm,
    ewi_hbm,
    eb_hbm,
    half_ref,
    send_ref,
    recv_ref,
    fill_ref,
    edge_ref,
    node_ref,
    ewi_ref,
    eb_ref,
    wp_ref,
    sems,
):
    copies = fetch_all(
        (node_hbm, ewi_hbm, eb_hbm, send_hbm, recv_hbm, fill_hbm, edge_hbm),
        (node_ref, ewi_ref, eb_ref, send_ref, recv_ref, fill_ref, edge_ref),
        sems,
    )
    for copy in copies[:-1]:
        copy.wait()
    wp_ref[0:D, :] = (ewi_ref[0:D, :].astype(F32) * 0.5).astype(BF)
    wp_ref[D : D + NODE, :] = (mm(node_ref[...], ewi_ref[D : 2 * D, :]) * 0.5).astype(BF)
    wp_ref[D + NODE :, :] = (
        (mm(node_ref[...], ewi_ref[2 * D :, :]) + eb_ref[...]) * 0.5
    ).astype(BF)

    def step(i, first, width):
        here = pl.ds(i * CHUNK, CHUNK)
        send, recv = chunk_ids(send_ref, recv_ref, fill_ref, i)
        half_ref[here, :] = (
            mm(edge_ref[here, :], wp_ref[0:D, :])
            + mm(chunk_cols(send, first, width), wp_ref[pl.ds(D + first, width), :])
            + mm(chunk_cols(recv, first, width), wp_ref[pl.ds(D + NODE + first, width), :])
        )

    def body(firsts):
        over_chunks(step, lambda i: None, fill_ref, firsts)

    copies[-1].wait()
    either_way(body, send_ref, recv_ref, fill_ref)


def layer_kernel(
    send_ref,
    recv_ref,
    fill_ref,
    core_ref,
    half_ref,
    edge_ref,
    ecot_ref,
    node_ref,
    hlow_ref,
    hup_ref,
    ncot_ref,
    ewi_ref,
    ewo_ref,
    eg_ref,
    nwi_ref,
    nb_ref,
    nwo_ref,
    ng_ref,
    gedge_hbm,
    own_ref,
    glow_ref,
    gup_ref,
    away_ref,
    kept_ref,
    slope_ref,
    gedge_ref,
    halo_ref,
    hott_ref,
    act_ref,
    normed_ref,
    inv_ref,
    agg_ref,
    back_node_ref,
    sums_ref,
    sumr_ref,
    dw0_ref,
    dwo_ref,
    dgain_ref,
    base_ref,
    share_ref,
    out_sem,
):
    def body(firsts):
        def copy_of(source, target, sems, i):
            here = pl.ds(i * CHUNK, CHUNK)
            return pltpu.make_async_copy(source.at[here], target.at[here], sems.at[i])


        halo = jnp.concatenate([hlow_ref[...], hup_ref[...]], 0)
        halo_ref[...] = (mm(halo, ewi_ref[D : 2 * D, :]) * 0.5).astype(BF)
        agg_ref[...] = jnp.zeros_like(agg_ref)
        gain = eg_ref[...]

        def forward(i, first, width):
            here = pl.ds(i * CHUNK, CHUNK)
            send, recv = chunk_ids(send_ref, recv_ref, fill_ref, i)
            half = half_ref[here, :] + mm(chunk_cols(send, NODE, 2 * HALO), halo_ref[...])
            t = jnp.tanh(half)
            ht = half * t
            act = (half + ht).astype(BF)
            act_ref[here, :] = act
            slope_ref[here, :] = (t + 1.0) * ((half - ht) + 1.0)
            normed, inverse = norm_forward(mm(act, ewo_ref[...]))
            normed_ref[here, :] = normed
            inv_ref[here, :] = jnp.broadcast_to(inverse, (CHUNK, LANE))
            message = (edge_ref[here, :].astype(F32) + gain * normed).astype(BF)
            hott = one_hot_rows(recv - first, width)
            hott_ref[i, 0:width, :] = hott
            agg_ref[pl.ds(first, width), :] += mm(hott, message)

        over_chunks(forward, lambda i: None, fill_ref, firsts)

        both = jnp.concatenate([node_ref[...], agg_ref[...].astype(BF)], 1)
        half = (mm(both, nwi_ref[...]) + nb_ref[...]) * 0.5
        t = jnp.tanh(half)
        ht = half * t
        act = (half + ht).astype(BF)
        slope = (t + 1.0) * ((half - ht) + 1.0) * 0.5
        normed, inverse = norm_forward(mm(act, nwo_ref[...]))
        up = ncot_ref[...].astype(F32)
        c = up * ng_ref[...]
        back = (
            inverse
            * (
                c
                - jnp.mean(c, -1, keepdims=True)
                - normed * jnp.mean(c * normed, -1, keepdims=True)
            )
        ).astype(BF)
        pre_grad = (mm_nt(back, nwo_ref[...]) * slope).astype(BF)
        input_grad = mm_nt(pre_grad, nwi_ref[...])
        base_ref[...] = up + input_grad[:, 0:D]
        back_node_ref[...] = input_grad[:, D:].astype(BF)
        mean = 1.0 / 256.0

        def put(row, block):
            size = block.shape[0] // N_DOM
            block = (block * mean).reshape(N_DOM, size, D)
            for side in range(2):
                share_ref[side, :, row : row + size, :] = block[:, :, side * LANE : (side + 1) * LANE]

        put(32, mm_tn(both, pre_grad))
        put(48, mm_tn(act, back))
        node_bias = jnp.sum(pre_grad.astype(F32), 0, keepdims=True)
        node_gain = jnp.sum(up * normed, 0, keepdims=True)

        sums_ref[...] = jnp.zeros_like(sums_ref)
        sumr_ref[...] = jnp.zeros_like(sumr_ref)
        dw0_ref[...] = jnp.zeros_like(dw0_ref)
        dwo_ref[...] = jnp.zeros_like(dwo_ref)
        dgain_ref[...] = jnp.zeros_like(dgain_ref)
        wo_half = (ewo_ref[...].astype(F32) * 0.5).astype(BF)

        def backward(i, first, width):
            here = pl.ds(i * CHUNK, CHUNK)
            send, recv = chunk_ids(send_ref, recv_ref, fill_ref, i)
            slots = lax.broadcasted_iota(jnp.int32, (LANE, D), 0)
            live = jnp.concatenate([slots < fill_ref[0, i * PER + k] for k in range(PER)], 0)
            msg = jnp.where(live, ecot_ref[here, :].astype(F32), 0.0) + mm(
                chunk_cols(recv, first, width), back_node_ref[pl.ds(first, width), :]
            )
            normed = normed_ref[here, :]
            c = msg * gain
            q = c * normed
            dgain_ref[...] += jnp.sum(q.reshape(CHUNK // 8, 8, D), 0)
            inverse = inv_ref[here, :]
            inverse = jnp.concatenate([inverse, inverse], 1)
            back = (
                inverse
                * (c - jnp.mean(c, -1, keepdims=True) - normed * jnp.mean(q, -1, keepdims=True))
            ).astype(BF)
            pre_grad = (mm_nt(back, wo_half) * slope_ref[here, :]).astype(BF)
            gedge_ref[here, :] = (msg + mm_nt(pre_grad, ewi_ref[0:D, :])).astype(BF)
            dwo_ref[...] += mm_tn(act_ref[here, :], back)
            dw0_ref[...] += mm_tn(edge_ref[here, :], pre_grad)
            hott = jnp.concatenate(
                [
                    hott_ref[i, 0:width, :],
                    one_hot_rows(send - first, width),
                    one_hot_rows(send - NODE, 2 * HALO),
                ],
                0,
            )
            sums = mm(hott, pre_grad)
            sumr_ref[pl.ds(first, width), :] += sums[0:width]
            sums_ref[pl.ds(first, width), :] += sums[width : 2 * width]
            sums_ref[NODE:, :] += sums[2 * width :]

        def padding(i):
            gedge_ref[pl.ds(i * CHUNK, CHUNK), :] = jnp.zeros((CHUNK, D), BF)

        over_chunks(backward, padding, fill_ref, firsts)
        for i in range(NCHUNK):
            copy_of(gedge_ref, gedge_hbm, out_sem, i).start()

        table = jnp.concatenate([node_ref[...], hlow_ref[...], hup_ref[...]], 0)
        sums = sums_ref[...]
        sumr = sumr_ref[...].astype(BF)
        sums_bf = sums.astype(BF)
        put(
            0,
            jnp.concatenate([dw0_ref[...], mm_tn(table, sums_bf), mm_tn(node_ref[...], sumr)], 0),
        )
        put(24, dwo_ref[...])
        vectors = (
            jnp.sum(sums, 0, keepdims=True),
            jnp.sum(dgain_ref[...], 0, keepdims=True) / gain,
            node_bias,
            node_gain,
        )
        place = lax.broadcasted_iota(jnp.int32, (N_DOM, D), 1) // 8
        mine = place == lax.broadcasted_iota(jnp.int32, (N_DOM, D), 0)
        spread = jnp.concatenate([jnp.where(mine, v * mean, 0.0) for v in vectors], 1)
        source = lax.broadcasted_iota(jnp.int32, (4 * D, LANE), 0)
        target = lax.broadcasted_iota(jnp.int32, (4 * D, LANE), 1)
        moves = jnp.where(target == (source // D) * 8 + source % 8, 1.0, 0.0).astype(BF)
        large = spread.astype(BF)
        row = mm(large, moves) + mm((spread - large.astype(F32)).astype(BF), moves)
        eight = lax.broadcasted_iota(jnp.int32, (N_DOM, 8, LANE), 1)
        share_ref[0, :, VECTOR_ROW:, :] = jnp.where(eight == 0, row[:, None, :], 0.0)
        share_ref[1, :, VECTOR_ROW:, :] = jnp.zeros((N_DOM, 8, LANE), F32)
        core = core_ref[0, 0]
        kept_ref[...] = share_ref[core]
        away_ref[...] = share_ref[1 - core].astype(BF)
        table_grad = mm_nt(sums_bf, ewi_ref[D : 2 * D, :])
        own_ref[...] = base_ref[...] + mm_nt(sumr, ewi_ref[2 * D :, :]) + table_grad[0:NODE]
        glow_ref[...] = table_grad[NODE : NODE + HALO].astype(BF)
        gup_ref[...] = table_grad[NODE + HALO :].astype(BF)
        for i in range(NCHUNK):
            copy_of(gedge_ref, gedge_hbm, out_sem, i).wait()

    either_way(body, send_ref, recv_ref, fill_ref)


def finish_kernel(rows_ref, own_ref, low_ref, up_ref, out_ref):
    hots = jnp.concatenate(
        [one_hot_rows(rows_ref[0:1, :], NODE), one_hot_rows(rows_ref[1:2, :], NODE)], 1
    )
    parts = jnp.concatenate([low_ref[...], up_ref[...]], 0)
    out_ref[...] = (own_ref[...] + mm(hots, parts)).astype(BF)


def unpack_kernel(core_ref, mine_ref, other_ref, ewi_ref, ewo_ref, nwi_ref, nwo_ref, *vec_refs):
    flip = core_ref[0, 0] == 1
    mine = mine_ref[...]
    other = other_ref[...]
    both = jnp.concatenate([jnp.where(flip, other, mine), jnp.where(flip, mine, other)], 1)
    ewi_ref[...] = both[0:24]
    ewo_ref[...] = both[24:32]
    nwi_ref[...] = both[32:48]
    nwo_ref[...] = both[48:56]
    for k in range(4):
        vec_refs[k][...] = both[VECTOR_ROW : VECTOR_ROW + 1, 8 * k : 8 * k + 8]


def on_device(kernel, outs, scratch, specs, out_specs=None, megabytes=8):
    vmem = pl.BlockSpec(memory_space=pltpu.VMEM)
    kinds = {
        "v": vmem,
        "s": pl.BlockSpec(memory_space=pltpu.SMEM),
        "a": pl.BlockSpec(memory_space=pl.ANY),
        "h": pl.BlockSpec(memory_space=pltpu.HBM),
    }
    flat, tree = jax.tree.flatten(outs)
    out_specs = out_specs or "v" * len(flat)
    return pl.pallas_call(
        kernel,
        out_shape=outs,
        in_specs=[kinds[k] for k in specs],
        out_specs=jax.tree.unflatten(tree, [kinds[k] for k in out_specs]),
        scratch_shapes=scratch,
        compiler_params=pltpu.CompilerParams(vmem_limit_bytes=megabytes * 1024 * 1024),
    )


def in_hbm(*args):
    return [pltpu.with_memory_space_constraint(a, pltpu.HBM) for a in args]


def shape(*dims, dtype=F32):
    return jax.ShapeDtypeStruct(dims, dtype)


def pick(rows, node):
    outs = (shape(HALO, D, dtype=BF),) * 2
    scratch = [
        pltpu.VMEM((2, HALO), jnp.int32),
        pltpu.VMEM((NODE, D), BF),
        pltpu.SemaphoreType.DMA((2,)),
    ]
    return on_device(pick_kernel, outs, scratch, "hh")(*in_hbm(rows, node))


def local(*args):
    scratch = [
        pltpu.VMEM((1, EDGE), jnp.int32),
        pltpu.VMEM((1, EDGE), jnp.int32),
        pltpu.SMEM((1, NBLK), jnp.int32),
        pltpu.VMEM((EDGE, D), BF),
        pltpu.VMEM((NODE, D), BF),
        pltpu.VMEM((3 * D, D), BF),
        pltpu.VMEM((1, D), F32),
        pltpu.VMEM((D + 2 * NODE, D), BF),
        pltpu.SemaphoreType.DMA((7,)),
    ]
    return on_device(local_kernel, shape(EDGE, D), scratch, "hhhhhhh", "v", 16)(*in_hbm(*args))


def layer(*args):
    outs = (
        shape(EDGE, D, dtype=BF),
        shape(NODE, D),
        shape(HALO, D, dtype=BF),
        shape(HALO, D, dtype=BF),
        shape(N_DOM, ROWS, LANE, dtype=BF),
        shape(N_DOM, ROWS, LANE),
    )
    scratch = [
        pltpu.VMEM((EDGE, D), F32),
        pltpu.VMEM((EDGE, D), BF),
        pltpu.VMEM((2 * HALO, D), BF),
        pltpu.VMEM((NCHUNK, NODE, CHUNK), BF),
        pltpu.VMEM((EDGE, D), BF),
        pltpu.VMEM((EDGE, D), F32),
        pltpu.VMEM((EDGE, LANE), F32),
        pltpu.VMEM((NODE, D), F32),
        pltpu.VMEM((NODE, D), BF),
        pltpu.VMEM((TABLE, D), F32),
        pltpu.VMEM((NODE, D), F32),
        pltpu.VMEM((D, D), F32),
        pltpu.VMEM((D, D), F32),
        pltpu.VMEM((8, D), F32),
        pltpu.VMEM((NODE, D), F32),
        pltpu.VMEM((2, N_DOM, ROWS, LANE), F32),
        pltpu.SemaphoreType.DMA((NCHUNK,)),
    ]
    return on_device(layer_kernel, outs, scratch, "vvssvvvvvvvvvvvvvv", "avvvvv", 32)(*args)


def finish(rows, own, low, up):
    return on_device(finish_kernel, shape(NODE, D, dtype=BF), [], "vvvv")(rows, own, low, up)


def unpack(core, mine, other):
    outs = (shape(24, D), shape(8, D), shape(16, D), shape(8, D)) + (shape(1, 8),) * 4
    return on_device(unpack_kernel, outs, [], "svv")(core, mine, other)


def swap(values, axis, flip):
    count = lax.axis_size(axis)
    return lax.ppermute(values, axis, [(i, i ^ flip) for i in range(count)])


def per_device(
    node_latent,
    edge_latent,
    node_cot,
    edge_cot,
    edge_w_in,
    edge_b_in,
    edge_w_out,
    edge_gain,
    node_w_in,
    node_b_in,
    node_w_out,
    node_gain,
    edge_senders,
    edge_receivers,
    block_fill,
    send_rows,
):
    node_rows = node_latent[0]
    lists = send_rows[0]
    count = lax.axis_size("dom")
    rise = [(i, i + 1) for i in range(count - 1)]
    fall = [(i + 1, i) for i in range(count - 1)]
    core = lax.rem(lax.axis_index("rep"), 2).reshape(1, 1)
    to_lower, to_upper = pick(lists, node_rows)
    halo_lower = lax.ppermute(to_upper, "dom", rise)
    halo_upper = lax.ppermute(to_lower, "dom", fall)
    half = local(
        edge_senders,
        edge_receivers,
        block_fill,
        edge_latent[0],
        node_rows,
        edge_w_in,
        edge_b_in[None],
    )
    gedge, own, glow, gup, away, kept = layer(
        edge_senders,
        edge_receivers,
        block_fill,
        core,
        half,
        edge_latent[0],
        edge_cot[0],
        node_rows,
        halo_lower,
        halo_upper,
        node_cot[0],
        edge_w_in,
        edge_w_out,
        edge_gain[None],
        node_w_in,
        node_b_in[None],
        node_w_out,
        node_gain[None],
    )
    back_upper = lax.ppermute(glow, "dom", fall)
    back_lower = lax.ppermute(gup, "dom", rise)
    values = (kept + swap(away, "rep", 1).astype(F32)).astype(BF)
    parts = lax.all_to_all(values, "dom", 0, 0, tiled=True)
    values = jnp.sum(parts.astype(F32), 0)
    values, back_lower, back_upper = lax.optimization_barrier((values, back_lower, back_upper))
    others = [swap(values, "rep", flip) for flip in (2, 4, 6)]
    grad_nodes = finish(lists, own, back_lower, back_upper)
    others, grad_nodes = lax.optimization_barrier((others, grad_nodes))
    values = values + others[0] + others[1] + others[2]
    ewi, ewo, nwi, nwo, *vec = unpack(core, values, swap(values, "rep", 1))
    return (
        grad_nodes[None],
        gedge[None],
        ewi,
        vec[0].reshape(8),
        ewo,
        vec[1].reshape(8),
        nwi,
        vec[2].reshape(8),
        nwo,
        vec[3].reshape(8),
    )


def solution(mesh):
    placed = (
        P("rep", "dom", None),
        P("rep", "dom", None),
        P("rep", "dom", None),
        P("rep", "dom", None),
        P(),
        P(),
        P(),
        P(),
        P(),
        P(),
        P(),
        P(),
        P("rep", "dom"),
        P("rep", "dom"),
        P("rep", "dom"),
        P("rep", "dom", None),
    )
    return jax.shard_map(
        per_device,
        mesh=mesh,
        in_specs=placed,
        out_specs=(
            P("rep", "dom", None),
            P("rep", "dom", None),
            P("dom", None),
            P("dom"),
            P("dom", None),
            P("dom"),
            P("dom", None),
            P("dom"),
            P("dom", None),
            P("dom"),
        ),
        check_vma=False,
    )
```

time: 89.1 us -> 73 us (0.82)
  blocking collectives: 12.9 us -> 0 us
  Pallas kernels: 28.2 us -> 21.7 us
  starting transfers between devices: 30 us -> 34.6 us
  waiting for transfers between devices: 11.9 us -> 14.7 us
  local copies, waits for them, and re-layouts: 2.67 us -> 0.09 us
  other arithmetic: 2.28 us -> 1.04 us
    all_to_all x1 -> x0, blocking collectives: 12.9 us -> none  [exchange_sum(): lax.all_to_all(values, axis, 0, 0, tiled=True, axis_index_groups=groups)]
    pallas_call x3, Pallas kernels: 24.8 us -> 20.1 us  [the longest x1 14.3 us: layer(): on_device(layer_kernel, outs, scratch, 'vvssvvvvvvvvvvvvvv', 'avvvvv', 32)]
    all_to_all x1, waiting for transfers between devices: 6.31 us -> 9.7 us  [per_device(): parts = lax.all_to_all(values, 'dom', 0, 0, tiled=True)]
    ppermute x5, starting transfers between devices: 8.85 us -> 11.4 us  [swap(): return lax.ppermute(values, axis, [(i, i ^ flip) for i in range(count)])]
    ppermute x1, starting transfers between devices: 1.28 us -> 3.14 us  [per_device(): back_lower = lax.ppermute(gup, 'dom', rise)]
    squeeze x1 -> x0, local copies, waits for them, and re-layouts: 1.42 us -> none  [per_device(): vec[0, 24:32]]
    convert_element_type x1, other arithmetic: 2.17 us -> 0.95 us  [per_device(): values = (kept + swap(away, 'rep', 1).astype(F32)).astype(BF)]
    unnamed x16 -> x30, local copies, waits for them, and re-layouts: 1.25 us -> 0.09 us
  transfers between devices with their start and end apart: 10 -> 10, of which waited for: 4 -> 5; matrix products, arithmetic and copies ran while one was open for 0% -> 0% of each run, Pallas kernels for 9% -> 7%
where the time goes in v3:
time: 73 us
  starting transfers between devices  34.6 us (47%)
  Pallas kernels  21.7 us (30%)
  waiting for transfers between devices  14.7 us (20%)
  other arithmetic  1.04 us (1%)
  between operations  0.98 us (1%)
    pallas_call x1, Pallas kernels, layer(): on_device(layer_kernel, outs, scratch, 'vvssvvvvvvvvvvvvvv', 'avvvvv', 32)  14.3 us
    all_to_all x1, starting transfers between devices, per_device(): parts = lax.all_to_all(values, 'dom', 0, 0, tiled=True)  13.1 us
    ppermute x5, starting transfers between devices, swap(): return lax.ppermute(values, axis, [(i, i ^ flip) for i in range(count)])  11.4 us
    all_to_all x1, waiting for transfers between devices, per_device(): parts = lax.all_to_all(values, 'dom', 0, 0, tiled=True)  9.7 us
    ppermute x5, waiting for transfers between devices, swap(): return lax.ppermute(values, axis, [(i, i ^ flip) for i in range(count)])  4.97 us
    pallas_call x1, Pallas kernels, local(): on_device(local_kernel, shape(EDGE, D), scratch, 'hhhhhhh', 'v', 16)  4.51 us
    ppermute x1, starting transfers between devices, per_device(): halo_lower = lax.ppermute(to_upper, 'dom', rise)  4.37 us
    ppermute x1, starting transfers between devices, per_device(): back_lower = lax.ppermute(gup, 'dom', rise)  3.14 us
  transfers between devices with their start and end apart: 10, of which 5 were waited for; matrix products, arithmetic and copies ran while one was open for 0% of the time, Pallas kernels for 7%

profile of v3, /device:TPU:1, one launch (start us, length us, event | category | flops | bytes accessed | tf_op | source)
XLA Modules:
  0.0 73.0 jit_solution(16904242963900378031)
XLA Ops:
  0.6 1.3 %shard_map.232 = (bf16[128,256]{1,0:T(8,128)(2,1)S(1)}, bf16[128,256]{1,0:T(8,128)(2,1)S(1)}) custom-call(s32[2,128]{1,0:T(2,128)} %bitcast.23, bf16[512,256]{1,0:T(8,128)(2,1)} %bitcast.18), custom_call_target="tpu_custom_call" | custom-call | tf_op jit(solution)/shard_map/pallas_call | solution.py:460
  1.9 4.4 %collective-permute-start = (bf16[128,256]{1,0:T(8,128)(2,1)S(1)}, bf16[128,256]{1,0:T(8,128)(2,1)S(1)}, u32[]{:S(2)}, u32[]{:S(2)}) collective-permute-start(bf16[128,256]{1,0:T(8,128)(2,1)S(1)} %get-tuple-element.33), channel_id=1, source_target_pairs={{0,1},{1,2},{2,3},{3,4},{4,5},{5,6},{6,7},{7,8},{8,9},{9,10},{10,1... | collective-permute-start | bytes 196616 | tf_op jit(solution)/shard_map/ppermute | solution.py:548
  6.3 1.3 %collective-permute-start.1 = (bf16[128,256]{1,0:T(8,128)(2,1)S(1)}, bf16[128,256]{1,0:T(8,128)(2,1)S(1)}, u32[]{:S(2)}, u32[]{:S(2)}) collective-permute-start(bf16[128,256]{1,0:T(8,128)(2,1)S(1)} %get-tuple-element.34), channel_id=1, source_target_pairs={{1,0},{2,1},{3,2},{4,3},{5,4},{6,5},{7,6},{8,7},{9,8},{10,9},{11,1... | collective-permute-start | bytes 196616 | tf_op jit(solution)/shard_map/ppermute | solution.py:549
  7.6 0.0 copy-start
  7.6 0.0 copy-start.1
  7.6 0.0 copy-start.2
  7.6 0.0 copy-start.3
  7.6 0.0 copy-start.4
  7.7 0.0 copy-start.5
  7.7 0.0 copy-start.6
  7.7 0.0 copy-start.7
  7.7 0.0 copy-start.8
  7.7 0.0 copy-start.9
  7.7 0.0 copy-start.11
  7.7 0.0 copy-start.12
  7.7 0.0 copy-start.13
  7.8 0.0 copy-start.14
  7.8 4.5 %shard_map.231.half_ref = f32[4096,256]{1,0:T(8,128)S(1)} custom-call(s32[1,4096]{1,0:T(1,128)} %send_ref.1, s32[1,4096]{1,0:T(1,128)} %recv_ref.1, s32[1,32]{1,0:T(1,128)} %fill_ref.1, bf16[4096,256]{1,0:T(8,128)(2,1)} %bitcast.16, bf16[512,256]{1,0:T(8,128)(2,1)} %bitcast.19, bf16[768,256]{1,0:T(8,128)(2,1)} %ewi_ref.1, f32[1,256]{1,0:T(1,128)} %bitcast.29), custom_call_target="tpu_custom_call" | custom-call | tf_op jit(solution)/shard_map/pallas_call | solution.py:475
  12.3 0.0 collective-permute-done.hlow_ref
  12.3 0.0 collective-permute-done.1.hup_ref
  12.3 0.0 copy-done
  12.3 0.0 copy-done.1
  12.3 0.0 copy-done.2
  12.3 0.0 copy-done.3
  12.3 0.0 copy-done.4
  12.4 0.0 copy-done.5
  12.4 14.3 %shard_map.233 = (bf16[4096,256]{1,0:T(8,128)(2,1)}, f32[512,256]{1,0:T(8,128)S(1)}, bf16[128,256]{1,0:T(8,128)(2,1)S(1)}, bf16[128,256]{1,0:T(8,128)(2,1)S(1)},...) custom-call(s32[1,4096]{1,0:T(1,128)S(1)} %copy-done.8, s32[1,4096]{1,0:T(1,128)S(1)} %copy-done.9, ...), custom_call_target="tpu_custom_call" | custom-call | tf_op jit(solution)/shard_map/pallas_call | solution.py:506
  26.8 0.0 copy-start.10
  26.8 1.1 %collective-permute-start.2 = (bf16[32,64,128]{2,1,0:T(8,128)(2,1)S(1)}, bf16[32,64,128]{2,1,0:T(8,128)(2,1)S(1)}, u32[]{:S(2)}, u32[]{:S(2)}) collective-permute-start(bf16[32,64,128]{2,1,0:T(8,128)(2,1)S(1)} %get-tuple-element.36), channel_id=1, source_target_pairs={{0,32},{32,0},{64,96},{96,64},{128,160},{160,128},{192,224},{224,1... | collective-permute-start | bytes 1572872 | tf_op jit(solution)/shard_map/ppermute | solution.py:520
  27.9 1.5 %collective-permute-done.2 = bf16[32,64,128]{2,1,0:T(8,128)(2,1)S(1)} collective-permute-done((bf16[32,64,128]{2,1,0:T(8,128)(2,1)S(1)}, bf16[32,64,128]{2,1,0:T(8,128)(2,1)S(1)}, u32[]{:S(2)}, u32[]{:S(2)}) %collective-permute-start.2) | collective-permute-done | bytes 524320 | tf_op jit(solution)/shard_map/ppermute | solution.py:520
  29.4 1.0 %add_convert_fusion = bf16[32,64,128]{2,1,0:T(8,128)(2,1)} fusion(f32[32,64,128]{2,1,0:T(8,128)S(1)} %get-tuple-element.35, bf16[32,64,128]{2,1,0:T(8,128)(2,1)S(1)} %collective-permute-done.2), kind=kLoop, calls=%fused_computation.1 | loop fusion | flops 786432 | bytes 2097152 | tf_op jit(solution)/shard_map/convert_element_type | solution.py:581
  30.4 13.1 %all-to-all-start = ((bf16[32,64,128]{2,1,0:T(8,128)(2,1)}), bf16[32,64,128]{2,1,0:T(8,128)(2,1)S(1)}, u32[]{:S(2)}, u32[]{:S(2)}) async-start(bf16[32,64,128]{2,1,0:T(8,128)(2,1)} %add_convert_fusion), calls=%async_computation | async-start | bytes 1048576 | tf_op jit(solution)/shard_map/all_to_all | solution.py:582
  43.5 3.1 %collective-permute-start.3 = (bf16[128,256]{1,0:T(8,128)(2,1)S(1)}, bf16[128,256]{1,0:T(8,128)(2,1)S(1)}, u32[]{:S(2)}, u32[]{:S(2)}) collective-permute-start(bf16[128,256]{1,0:T(8,128)(2,1)S(1)} %get-tuple-element.37), channel_id=1, source_target_pairs={{0,1},{1,2},{2,3},{3,4},{4,5},{5,6},{6,7},{7,8},{8,9},{9,10},{10,1... | collective-permute-start | bytes 196616 | tf_op jit(solution)/shard_map/ppermute | solution.py:580
  46.6 1.3 %collective-permute-start.4 = (bf16[128,256]{1,0:T(8,128)(2,1)S(1)}, bf16[128,256]{1,0:T(8,128)(2,1)S(1)}, u32[]{:S(2)}, u32[]{:S(2)}) collective-permute-start(bf16[128,256]{1,0:T(8,128)(2,1)S(1)} %get-tuple-element.38), channel_id=1, source_target_pairs={{1,0},{2,1},{3,2},{4,3},{5,4},{6,5},{7,6},{8,7},{9,8},{10,9},{11,1... | collective-permute-start | bytes 196616 | tf_op jit(solution)/shard_map/ppermute | solution.py:579
  47.9 9.7 %all-to-all-done = bf16[32,64,128]{2,1,0:T(8,128)(2,1)S(1)} async-done(((bf16[32,64,128]{2,1,0:T(8,128)(2,1)}), bf16[32,64,128]{2,1,0:T(8,128)(2,1)S(1)}, u32[]{:S(2)}, u32[]{:S(2)}) %all-to-all-start) | async-done | bytes 524320 | tf_op jit(solution)/shard_map/all_to_all | solution.py:582
  57.6 0.1 convert_reduce_fusion
  57.7 0.0 collective-permute-done.3.low_ref
  57.7 0.0 collective-permute-done.4.up_ref
  57.7 2.6 %collective-permute-start.7 = (f32[64,128]{1,0:T(8,128)S(1)}, f32[64,128]{1,0:T(8,128)S(1)}, u32[]{:S(2)}, u32[]{:S(2)}) collective-permute-start(f32[64,128]{1,0:T(8,128)S(1)} %convert_reduce_fusion), channel_id=1, source_target_pairs={{0,192},{32,224},{64,128},{96,160},{128,64},{160,96},{192,0},{224,... | collective-permute-start | bytes 98312 | tf_op jit(solution)/shard_map/ppermute | solution.py:520
  60.3 0.3 collective-permute-start.6
  60.6 0.4 collective-permute-start.5
  61.1 0.9 %shard_map.234 = bf16[512,256]{1,0:T(8,128)(2,1)} custom-call(s32[2,128]{1,0:T(2,128)S(1)} %bitcast.24, f32[512,256]{1,0:T(8,128)S(1)} %get-tuple-element.40.own_ref, bf16[128,256]{1,0:T(8,128)(2,1)S(1)} %collective-permute-done.3.low_ref, bf16[128,256]{1,0:T(8,128)(2,1)S(1)} %collective-permute-done.4.up_ref), custom_call_target="tpu_custom_call" | custom-call | tf_op jit(solution)/shard_map/pallas_call | solution.py:510
  62.0 0.1 collective-permute-done.7
  62.1 2.5 %collective-permute-done.6 = f32[64,128]{1,0:T(8,128)S(1)} collective-permute-done((f32[64,128]{1,0:T(8,128)S(1)}, f32[64,128]{1,0:T(8,128)S(1)}, u32[]{:S(2)}, u32[]{:S(2)}) %collective-permute-start.6) | collective-permute-done | bytes 32800 | tf_op jit(solution)/shard_map/ppermute | solution.py:520
  64.6 0.0 collective-permute-done.5
  64.6 6.9 %collective-permute-start.8 = (f32[64,128]{1,0:T(8,128)S(1)}, f32[64,128]{1,0:T(8,128)S(1)}, u32[]{:S(2)}, u32[]{:S(2)}) collective-permute-start(f32[64,128]{1,0:T(8,128)S(1)} %add_add_fusion.mine_ref), channel_id=1, source_target_pairs={{0,32},{32,0},{64,96},{96,64},{128,160},{160,128},{192,224},{224,1... | collective-permute-start | bytes 98312 | tf_op jit(solution)/shard_map/ppermute | solution.py:520
  71.5 0.9 %collective-permute-done.8.other_ref = f32[64,128]{1,0:T(8,128)S(1)} collective-permute-done((f32[64,128]{1,0:T(8,128)S(1)}, f32[64,128]{1,0:T(8,128)S(1)}, u32[]{:S(2)}, u32[]{:S(2)}) %collective-permute-start.8) | collective-permute-done | bytes 32800 | tf_op jit(solution)/shard_map/ppermute | solution.py:520
  72.4 0.6 shard_map.235
  (10 shorter events, 0.0 us)
Async XLA Ops:
  1.9 10.4 %collective-permute-start = (bf16[128,256]{1,0:T(8,128)(2,1)S(1)}, bf16[128,256]{1,0:T(8,128)(2,1)S(1)}, u32[]{:S(2)}, u32[]{:S(2)}) collective-permute-start(bf16[128,256]{1,0:T(8,128)(2,1)S(1)} %get-tuple-element.33), channel_id=1, source_target_pairs={{0,1},{1,2},{2,3},{3,4},{4,5},{5,6},{6,7},{7,8},{8,9},{9,10},{10,1... | collective-permute-start | bytes 196616 | tf_op jit(solution)/shard_map/ppermute | solution.py:548
  6.3 6.0 %collective-permute-start.1 = (bf16[128,256]{1,0:T(8,128)(2,1)S(1)}, bf16[128,256]{1,0:T(8,128)(2,1)S(1)}, u32[]{:S(2)}, u32[]{:S(2)}) collective-permute-start(bf16[128,256]{1,0:T(8,128)(2,1)S(1)} %get-tuple-element.34), channel_id=1, source_target_pairs={{1,0},{2,1},{3,2},{4,3},{5,4},{6,5},{7,6},{8,7},{9,8},{10,9},{11,1... | collective-permute-start | bytes 196616 | tf_op jit(solution)/shard_map/ppermute | solution.py:549
  7.6 4.7 %copy-start = (bf16[1,4096,256]{2,1,0:T(8,128)(2,1)S(1)}, bf16[1,4096,256]{2,1,0:T(8,128)(2,1)}, u32[]{:S(2)}) copy-start(bf16[1,4096,256]{2,1,0:T(8,128)(2,1)} %param.17) | copy-start | bytes 6291460
  7.6 4.7 %copy-start.1 = (bf16[1,512,256]{2,1,0:T(8,128)(2,1)S(1)}, bf16[1,512,256]{2,1,0:T(8,128)(2,1)}, u32[]{:S(2)}) copy-start(bf16[1,512,256]{2,1,0:T(8,128)(2,1)} %param.16) | copy-start | bytes 786436
  7.6 4.7 %copy-start.2 = (bf16[1,4096,256]{2,1,0:T(8,128)(2,1)S(1)}, bf16[1,4096,256]{2,1,0:T(8,128)(2,1)}, u32[]{:S(2)}) copy-start(bf16[1,4096,256]{2,1,0:T(8,128)(2,1)} %param.19) | copy-start | bytes 6291460
  7.6 4.7 %copy-start.3 = (bf16[768,256]{1,0:T(8,128)(2,1)S(1)}, bf16[768,256]{1,0:T(8,128)(2,1)}, u32[]{:S(2)}) copy-start(bf16[768,256]{1,0:T(8,128)(2,1)} %ewi_ref.1) | copy-start | bytes 1179652
  7.6 4.7 %copy-start.4 = (bf16[1,512,256]{2,1,0:T(8,128)(2,1)S(1)}, bf16[1,512,256]{2,1,0:T(8,128)(2,1)}, u32[]{:S(2)}) copy-start(bf16[1,512,256]{2,1,0:T(8,128)(2,1)} %param.18) | copy-start | bytes 786436
  7.7 4.7 %copy-start.5 = (bf16[512,256]{1,0:T(8,128)(2,1)S(1)}, bf16[512,256]{1,0:T(8,128)(2,1)}, u32[]{:S(2)}) copy-start(bf16[512,256]{1,0:T(8,128)(2,1)} %nwi_ref.1) | copy-start | bytes 786436
  7.7 4.7 %copy-start.6 = (bf16[256,256]{1,0:T(8,128)(2,1)S(1)}, bf16[256,256]{1,0:T(8,128)(2,1)}, u32[]{:S(2)}) copy-start(bf16[256,256]{1,0:T(8,128)(2,1)} %ewo_ref.1) | copy-start | bytes 393220
  7.7 4.7 %copy-start.7 = (bf16[256,256]{1,0:T(8,128)(2,1)S(1)}, bf16[256,256]{1,0:T(8,128)(2,1)}, u32[]{:S(2)}) copy-start(bf16[256,256]{1,0:T(8,128)(2,1)} %nwo_ref.1) | copy-start | bytes 393220
  7.7 4.7 %copy-start.8 = (s32[1,4096]{1,0:T(1,128)S(1)}, s32[1,4096]{1,0:T(1,128)}, u32[]{:S(2)}) copy-start(s32[1,4096]{1,0:T(1,128)} %send_ref.1) | copy-start | bytes 49156
  7.7 4.7 %copy-start.9 = (s32[1,4096]{1,0:T(1,128)S(1)}, s32[1,4096]{1,0:T(1,128)}, u32[]{:S(2)}) copy-start(s32[1,4096]{1,0:T(1,128)} %recv_ref.1) | copy-start | bytes 49156
  7.7 4.7 %copy-start.11 = (s32[1,32]{1,0:T(1,128)S(1)}, s32[1,32]{1,0:T(1,128)}, u32[]{:S(2)}) copy-start(s32[1,32]{1,0:T(1,128)} %fill_ref.1) | copy-start | bytes 388
  7.7 4.7 %copy-start.12 = (f32[256]{0:T(256)S(1)}, f32[256]{0:T(256)}, u32[]{:S(2)}) copy-start(f32[256]{0:T(256)} %param.23) | copy-start | bytes 3076
  7.7 4.7 %copy-start.13 = (f32[256]{0:T(256)S(1)}, f32[256]{0:T(256)}, u32[]{:S(2)}) copy-start(f32[256]{0:T(256)} %param.25) | copy-start | bytes 3076
  7.8 4.7 %copy-start.14 = (f32[256]{0:T(256)S(1)}, f32[256]{0:T(256)}, u32[]{:S(2)}) copy-start(f32[256]{0:T(256)} %param.27) | copy-start | bytes 3076
  26.8 34.3 %copy-start.10 = (s32[1,2,128]{2,1,0:T(2,128)S(1)}, s32[1,2,128]{2,1,0:T(2,128)}, u32[]{:S(2)}) copy-start(s32[1,2,128]{2,1,0:T(2,128)} %param.31) | copy-start | bytes 3076
  26.8 2.6 %collective-permute-start.2 = (bf16[32,64,128]{2,1,0:T(8,128)(2,1)S(1)}, bf16[32,64,128]{2,1,0:T(8,128)(2,1)S(1)}, u32[]{:S(2)}, u32[]{:S(2)}) collective-permute-start(bf16[32,64,128]{2,1,0:T(8,128)(2,1)S(1)} %get-tuple-element.36), channel_id=1, source_target_pairs={{0,32},{32,0},{64,96},{96,64},{128,160},{160,128},{192,224},{224,1... | collective-permute-start | bytes 1572872 | tf_op jit(solution)/shard_map/ppermute | solution.py:520
  30.4 27.3 %all-to-all-start = ((bf16[32,64,128]{2,1,0:T(8,128)(2,1)}), bf16[32,64,128]{2,1,0:T(8,128)(2,1)S(1)}, u32[]{:S(2)}, u32[]{:S(2)}) async-start(bf16[32,64,128]{2,1,0:T(8,128)(2,1)} %add_convert_fusion), calls=%async_computation | async-start | bytes 1048576 | tf_op jit(solution)/shard_map/all_to_all | solution.py:582
  43.5 14.2 %collective-permute-start.3 = (bf16[128,256]{1,0:T(8,128)(2,1)S(1)}, bf16[128,256]{1,0:T(8,128)(2,1)S(1)}, u32[]{:S(2)}, u32[]{:S(2)}) collective-permute-start(bf16[128,256]{1,0:T(8,128)(2,1)S(1)} %get-tuple-element.37), channel_id=1, source_target_pairs={{0,1},{1,2},{2,3},{3,4},{4,5},{5,6},{6,7},{7,8},{8,9},{9,10},{10,1... | collective-permute-start | bytes 196616 | tf_op jit(solution)/shard_map/ppermute | solution.py:580
  46.6 11.1 %collective-permute-start.4 = (bf16[128,256]{1,0:T(8,128)(2,1)S(1)}, bf16[128,256]{1,0:T(8,128)(2,1)S(1)}, u32[]{:S(2)}, u32[]{:S(2)}) collective-permute-start(bf16[128,256]{1,0:T(8,128)(2,1)S(1)} %get-tuple-element.38), channel_id=1, source_target_pairs={{1,0},{2,1},{3,2},{4,3},{5,4},{6,5},{7,6},{8,7},{9,8},{10,9},{11,1... | collective-permute-start | bytes 196616 | tf_op jit(solution)/shard_map/ppermute | solution.py:579
  57.7 4.4 %collective-permute-start.7 = (f32[64,128]{1,0:T(8,128)S(1)}, f32[64,128]{1,0:T(8,128)S(1)}, u32[]{:S(2)}, u32[]{:S(2)}) collective-permute-start(f32[64,128]{1,0:T(8,128)S(1)} %convert_reduce_fusion), channel_id=1, source_target_pairs={{0,192},{32,224},{64,128},{96,160},{128,64},{160,96},{192,0},{224,... | collective-permute-start | bytes 98312 | tf_op jit(solution)/shard_map/ppermute | solution.py:520
  60.3 4.3 %collective-permute-start.6 = (f32[64,128]{1,0:T(8,128)S(1)}, f32[64,128]{1,0:T(8,128)S(1)}, u32[]{:S(2)}, u32[]{:S(2)}) collective-permute-start(f32[64,128]{1,0:T(8,128)S(1)} %convert_reduce_fusion), channel_id=1, source_target_pairs={{0,128},{32,160},{64,192},{96,224},{128,0},{160,32},{192,64},{224,... | collective-permute-start | bytes 98312 | tf_op jit(solution)/shard_map/ppermute | solution.py:520
  60.6 3.9 %collective-permute-start.5 = (f32[64,128]{1,0:T(8,128)S(1)}, f32[64,128]{1,0:T(8,128)S(1)}, u32[]{:S(2)}, u32[]{:S(2)}) collective-permute-start(f32[64,128]{1,0:T(8,128)S(1)} %convert_reduce_fusion), channel_id=1, source_target_pairs={{0,64},{32,96},{64,0},{96,32},{128,192},{160,224},{192,128},{224,1... | collective-permute-start | bytes 98312 | tf_op jit(solution)/shard_map/ppermute | solution.py:520
  64.6 7.8 %collective-permute-start.8 = (f32[64,128]{1,0:T(8,128)S(1)}, f32[64,128]{1,0:T(8,128)S(1)}, u32[]{:S(2)}, u32[]{:S(2)}) collective-permute-start(f32[64,128]{1,0:T(8,128)S(1)} %add_add_fusion.mine_ref), channel_id=1, source_target_pairs={{0,32},{32,0},{64,96},{96,64},{128,160},{160,128},{192,224},{224,1... | collective-permute-start | bytes 98312 | tf_op jit(solution)/shard_map/ppermute | solution.py:520

commit v4 on v3

--- a/solution.py
+++ b/solution.py
@@ -225,14 +225,16 @@
     nb_ref,
     nwo_ref,
     ng_ref,
-    gedge_hbm,
-    own_ref,
+    msg_hbm,
+    grad_hbm,
+    base_ref,
+    nsum_ref,
     glow_ref,
     gup_ref,
     away_ref,
     kept_ref,
-    slope_ref,
-    gedge_ref,
+    msg_ref,
+    grad_ref,
     halo_ref,
     hott_ref,
     act_ref,
@@ -245,16 +247,17 @@
     dw0_ref,
     dwo_ref,
     dgain_ref,
-    base_ref,
     share_ref,
-    out_sem,
+    sems,
 ):
+    def flush(i):
+        here = pl.ds(i * CHUNK, CHUNK)
+        return (
+            pltpu.make_async_copy(msg_ref.at[here], msg_hbm.at[here], sems.at[0, i]),
+            pltpu.make_async_copy(grad_ref.at[here], grad_hbm.at[here], sems.at[1, i]),
+        )
+
     def body(firsts):
-        def copy_of(source, target, sems, i):
-            here = pl.ds(i * CHUNK, CHUNK)
-            return pltpu.make_async_copy(source.at[here], target.at[here], sems.at[i])
-
-
         halo = jnp.concatenate([hlow_ref[...], hup_ref[...]], 0)
         halo_ref[...] = (mm(halo, ewi_ref[D : 2 * D, :]) * 0.5).astype(BF)
         agg_ref[...] = jnp.zeros_like(agg_ref)
@@ -268,13 +271,14 @@
             ht = half * t
             act = (half + ht).astype(BF)
             act_ref[here, :] = act
-            slope_ref[here, :] = (t + 1.0) * ((half - ht) + 1.0)
+            msg_ref[here, :] = ((t + 1.0) * ((half - ht) + 1.0)).astype(BF)
             normed, inverse = norm_forward(mm(act, ewo_ref[...]))
             normed_ref[here, :] = normed
             inv_ref[here, :] = jnp.broadcast_to(inverse, (CHUNK, LANE))
             message = (edge_ref[here, :].astype(F32) + gain * normed).astype(BF)
             hott = one_hot_rows(recv - first, width)
-            hott_ref[i, 0:width, :] = hott
+            if width == WINDOW:
+                hott_ref[i] = hott
             agg_ref[pl.ds(first, width), :] += mm(hott, message)
 
         over_chunks(forward, lambda i: None, fill_ref, firsts)
@@ -301,12 +305,14 @@
         base_ref[...] = up + input_grad[:, 0:D]
         back_node_ref[...] = input_grad[:, D:].astype(BF)
         mean = 1.0 / 256.0
+        odd = core_ref[0, 0] == 1
 
         def put(row, block):
             size = block.shape[0] // N_DOM
             block = (block * mean).reshape(N_DOM, size, D)
-            for side in range(2):
-                share_ref[side, :, row : row + size, :] = block[:, :, side * LANE : (side + 1) * LANE]
+            left, right = block[:, :, 0:LANE], block[:, :, LANE:]
+            kept_ref[:, row : row + size, :] = jnp.where(odd, right, left)
+            share_ref[:, row : row + size, :] = jnp.where(odd, left, right)
 
         put(32, mm_tn(both, pre_grad))
         put(48, mm_tn(act, back))
@@ -338,13 +344,14 @@
                 inverse
                 * (c - jnp.mean(c, -1, keepdims=True) - normed * jnp.mean(q, -1, keepdims=True))
             ).astype(BF)
-            pre_grad = (mm_nt(back, wo_half) * slope_ref[here, :]).astype(BF)
-            gedge_ref[here, :] = (msg + mm_nt(pre_grad, ewi_ref[0:D, :])).astype(BF)
+            pre_grad = (mm_nt(back, wo_half) * msg_ref[here, :].astype(F32)).astype(BF)
+            msg_ref[here, :] = msg.astype(BF)
+            grad_ref[here, :] = pre_grad
             dwo_ref[...] += mm_tn(act_ref[here, :], back)
             dw0_ref[...] += mm_tn(edge_ref[here, :], pre_grad)
             hott = jnp.concatenate(
                 [
-                    hott_ref[i, 0:width, :],
+                    hott_ref[i] if width == WINDOW else one_hot_rows(recv - first, width),
                     one_hot_rows(send - first, width),
                     one_hot_rows(send - NODE, 2 * HALO),
                 ],
@@ -354,13 +361,17 @@
             sumr_ref[pl.ds(first, width), :] += sums[0:width]
             sums_ref[pl.ds(first, width), :] += sums[width : 2 * width]
             sums_ref[NODE:, :] += sums[2 * width :]
+            for copy in flush(i):
+                copy.start()
 
         def padding(i):
-            gedge_ref[pl.ds(i * CHUNK, CHUNK), :] = jnp.zeros((CHUNK, D), BF)
+            here = pl.ds(i * CHUNK, CHUNK)
+            msg_ref[here, :] = jnp.zeros((CHUNK, D), BF)
+            grad_ref[here, :] = jnp.zeros((CHUNK, D), BF)
+            for copy in flush(i):
+                copy.start()
 
         over_chunks(backward, padding, fill_ref, firsts)
-        for i in range(NCHUNK):
-            copy_of(gedge_ref, gedge_hbm, out_sem, i).start()
 
         table = jnp.concatenate([node_ref[...], hlow_ref[...], hup_ref[...]], 0)
         sums = sums_ref[...]
@@ -386,19 +397,56 @@
         large = spread.astype(BF)
         row = mm(large, moves) + mm((spread - large.astype(F32)).astype(BF), moves)
         eight = lax.broadcasted_iota(jnp.int32, (N_DOM, 8, LANE), 1)
-        share_ref[0, :, VECTOR_ROW:, :] = jnp.where(eight == 0, row[:, None, :], 0.0)
-        share_ref[1, :, VECTOR_ROW:, :] = jnp.zeros((N_DOM, 8, LANE), F32)
-        core = core_ref[0, 0]
-        kept_ref[...] = share_ref[core]
-        away_ref[...] = share_ref[1 - core].astype(BF)
-        table_grad = mm_nt(sums_bf, ewi_ref[D : 2 * D, :])
-        own_ref[...] = base_ref[...] + mm_nt(sumr, ewi_ref[2 * D :, :]) + table_grad[0:NODE]
-        glow_ref[...] = table_grad[NODE : NODE + HALO].astype(BF)
-        gup_ref[...] = table_grad[NODE + HALO :].astype(BF)
+        rows = jnp.where(eight == 0, row[:, None, :], 0.0)
+        kept_ref[:, VECTOR_ROW:, :] = jnp.where(odd, 0.0, rows)
+        share_ref[:, VECTOR_ROW:, :] = jnp.where(odd, rows, 0.0)
+        away_ref[...] = share_ref[...].astype(BF)
+        halo_grad = mm_nt(sums_bf[NODE:], ewi_ref[D : 2 * D, :])
+        glow_ref[...] = halo_grad[0:HALO].astype(BF)
+        gup_ref[...] = halo_grad[HALO:].astype(BF)
+        nsum_ref[:, 0:D] = sums_bf[0:NODE]
+        nsum_ref[:, D:] = sumr
         for i in range(NCHUNK):
-            copy_of(gedge_ref, gedge_hbm, out_sem, i).wait()
+            for copy in flush(i):
+                copy.wait()
 
     either_way(body, send_ref, recv_ref, fill_ref)
+
+
+def inputs_kernel(
+    msg_hbm,
+    grad_hbm,
+    base_ref,
+    nsum_ref,
+    ewi_ref,
+    gedge_hbm,
+    own_ref,
+    msg_ref,
+    grad_ref,
+    gedge_ref,
+    in_sems,
+    sems,
+):
+    def flush(i):
+        here = pl.ds(i * CHUNK, CHUNK)
+        return pltpu.make_async_copy(gedge_ref.at[here], gedge_hbm.at[here], sems.at[i])
+
+    copies = fetch_all((msg_hbm, grad_hbm), (msg_ref, grad_ref), in_sems)
+    own_ref[...] = (
+        base_ref[...]
+        + mm_nt(nsum_ref[:, 0:D], ewi_ref[D : 2 * D, :])
+        + mm_nt(nsum_ref[:, D:], ewi_ref[2 * D :, :])
+    )
+    for copy in copies:
+        copy.wait()
+    for i in range(NCHUNK):
+        here = pl.ds(i * CHUNK, CHUNK)
+        gedge_ref[here, :] = (
+            msg_ref[here, :].astype(F32) + mm_nt(grad_ref[here, :], ewi_ref[0:D, :])
+        ).astype(BF)
+        flush(i).start()
+    for i in range(NCHUNK):
+        flush(i).wait()
 
 
 def finish_kernel(rows_ref, own_ref, low_ref, up_ref, out_ref):
@@ -472,23 +520,25 @@
         pltpu.VMEM((D + 2 * NODE, D), BF),
         pltpu.SemaphoreType.DMA((7,)),
     ]
-    return on_device(local_kernel, shape(EDGE, D), scratch, "hhhhhhh", "v", 16)(*in_hbm(*args))
+    return on_device(local_kernel, shape(EDGE, D), scratch, "hhhhhhh", "v", 10)(*in_hbm(*args))
 
 
 def layer(*args):
     outs = (
-        shape(EDGE, D, dtype=BF),
+        pltpu.HBM((EDGE, D), BF),
+        pltpu.HBM((EDGE, D), BF),
         shape(NODE, D),
+        shape(NODE, 2 * D, dtype=BF),
         shape(HALO, D, dtype=BF),
         shape(HALO, D, dtype=BF),
         shape(N_DOM, ROWS, LANE, dtype=BF),
         shape(N_DOM, ROWS, LANE),
     )
     scratch = [
-        pltpu.VMEM((EDGE, D), F32),
+        pltpu.VMEM((EDGE, D), BF),
         pltpu.VMEM((EDGE, D), BF),
         pltpu.VMEM((2 * HALO, D), BF),
-        pltpu.VMEM((NCHUNK, NODE, CHUNK), BF),
+        pltpu.VMEM((NCHUNK, WINDOW, CHUNK), BF),
         pltpu.VMEM((EDGE, D), BF),
         pltpu.VMEM((EDGE, D), F32),
         pltpu.VMEM((EDGE, LANE), F32),
@@ -499,11 +549,21 @@
         pltpu.VMEM((D, D), F32),
         pltpu.VMEM((D, D), F32),
         pltpu.VMEM((8, D), F32),
-        pltpu.VMEM((NODE, D), F32),
-        pltpu.VMEM((2, N_DOM, ROWS, LANE), F32),
+        pltpu.VMEM((N_DOM, ROWS, LANE), F32),
+        pltpu.SemaphoreType.DMA((2, NCHUNK)),
+    ]
+    return on_device(layer_kernel, outs, scratch, "vvssvvvvvvvvvvvvvv", "hhvvvvvv", 30)(*args)
+
+
+def inputs(*args):
+    outs = (shape(EDGE, D, dtype=BF), shape(NODE, D))
+    scratch = [pltpu.VMEM((EDGE, D), BF)] * 3 + [
+        pltpu.SemaphoreType.DMA((2,)),
         pltpu.SemaphoreType.DMA((NCHUNK,)),
     ]
-    return on_device(layer_kernel, outs, scratch, "vvssvvvvvvvvvvvvvv", "avvvvv", 32)(*args)
+    return on_device(inputs_kernel, outs, scratch, "hhvvv", "hv", 10)(
+        *in_hbm(*args[:2]), *args[2:]
+    )
 
 
 def finish(rows, own, low, up):
@@ -556,7 +616,7 @@
         edge_w_in,
         edge_b_in[None],
     )
-    gedge, own, glow, gup, away, kept = layer(
+    msg, grad, base, node_sums, glow, gup, away, kept = layer(
         edge_senders,
         edge_receivers,
         block_fill,
@@ -579,9 +639,13 @@
     back_upper = lax.ppermute(glow, "dom", fall)
     back_lower = lax.ppermute(gup, "dom", rise)
     values = (kept + swap(away, "rep", 1).astype(F32)).astype(BF)
+    values, msg, grad = lax.optimization_barrier((values, msg, grad))
     parts = lax.all_to_all(values, "dom", 0, 0, tiled=True)
+    gedge, own = inputs(msg, grad, base, node_sums, edge_w_in)
     values = jnp.sum(parts.astype(F32), 0)
-    values, back_lower, back_upper = lax.optimization_barrier((values, back_lower, back_upper))
+    values, back_lower, back_upper, own = lax.optimization_barrier(
+        (values, back_lower, back_upper, own)
+    )
     others = [swap(values, "rep", flip) for flip in (2, 4, 6)]
     grad_nodes = finish(lists, own, back_lower, back_upper)
     others, grad_nodes = lax.optimization_barrier((others, grad_nodes))

time: 73 us -> 72.1 us (0.988)
  waiting for transfers between devices: 14.7 us -> 10.7 us
  Pallas kernels: 21.7 us -> 24.3 us
    all_to_all x1, waiting for transfers between devices: 9.7 us -> 5.61 us  [per_device(): parts = lax.all_to_all(values, 'dom', 0, 0, tiled=True)]
    pallas_call x2 -> x3, Pallas kernels: 18.8 us -> 21.5 us  [the longest x1 13.3 us: layer(): on_device(layer_kernel, outs, scratch, 'vvssvvvvvvvvvvvvvv', 'hhvvvvvv', 30)]
  transfers between devices with their start and end apart: 10 -> 10, of which waited for: 5 -> 4; matrix products, arithmetic and copies ran while one was open for 0% -> 0% of each run, Pallas kernels for 7% -> 13%
where the time goes in v4:
time: 72.1 us; the launch traced here: 71.9 us
  starting transfers between devices  34.7 us (48%)
  Pallas kernels  24.3 us (34%)
  waiting for transfers between devices  10.7 us (15%)
  other arithmetic  1.05 us (1%)
  between operations  0.99 us (1%)
    pallas_call x1, Pallas kernels, layer(): on_device(layer_kernel, outs, scratch, 'vvssvvvvvvvvvvvvvv', 'hhvvvvvv', 30)  13.3 us
    all_to_all x1, starting transfers between devices, per_device(): parts = lax.all_to_all(values, 'dom', 0, 0, tiled=True)  12.8 us
    ppermute x5, starting transfers between devices, swap(): return lax.ppermute(values, axis, [(i, i ^ flip) for i in range(count)])  11.8 us
    all_to_all x1, waiting for transfers between devices, per_device(): parts = lax.all_to_all(values, 'dom', 0, 0, tiled=True)  5.61 us
    ppermute x5, waiting for transfers between devices, swap(): return lax.ppermute(values, axis, [(i, i ^ flip) for i in range(count)])  5.06 us
    ppermute x1, starting transfers between devices, per_device(): halo_lower = lax.ppermute(to_upper, 'dom', rise)  4.37 us
    pallas_call x1, Pallas kernels, local(): on_device(local_kernel, shape(EDGE, D), scratch, 'hhhhhhh', 'v', 10)  4.13 us
    pallas_call x1, Pallas kernels, inputs(): on_device(inputs_kernel, outs, scratch, 'hhvvv', 'hv', 10)  4.07 us
  transfers between devices with their start and end apart: 10, of which 4 were waited for; matrix products, arithmetic and copies ran while one was open for 0% of the time, Pallas kernels for 13%

profile of v4, /device:TPU:1, one launch (start us, length us, event | category | flops | bytes accessed | tf_op | source)
XLA Modules:
  0.0 71.9 jit_solution(2185566846140254394)
XLA Ops:
  0.6 1.3 %shard_map.232 = (bf16[128,256]{1,0:T(8,128)(2,1)S(1)}, bf16[128,256]{1,0:T(8,128)(2,1)S(1)}) custom-call(s32[2,128]{1,0:T(2,128)} %bitcast.23, bf16[512,256]{1,0:T(8,128)(2,1)} %bitcast.18), custom_call_target="tpu_custom_call" | custom-call | tf_op jit(solution)/shard_map/pallas_call | solution.py:508
  1.9 4.4 %collective-permute-start = (bf16[128,256]{1,0:T(8,128)(2,1)S(1)}, bf16[128,256]{1,0:T(8,128)(2,1)S(1)}, u32[]{:S(2)}, u32[]{:S(2)}) collective-permute-start(bf16[128,256]{1,0:T(8,128)(2,1)S(1)} %get-tuple-element.41), channel_id=1, source_target_pairs={{0,1},{1,2},{2,3},{3,4},{4,5},{5,6},{6,7},{7,8},{8,9},{9,10},{10,1... | collective-permute-start | bytes 196616 | tf_op jit(solution)/shard_map/ppermute | solution.py:608
  6.3 1.3 %collective-permute-start.1 = (bf16[128,256]{1,0:T(8,128)(2,1)S(1)}, bf16[128,256]{1,0:T(8,128)(2,1)S(1)}, u32[]{:S(2)}, u32[]{:S(2)}) collective-permute-start(bf16[128,256]{1,0:T(8,128)(2,1)S(1)} %get-tuple-element.42), channel_id=1, source_target_pairs={{1,0},{2,1},{3,2},{4,3},{5,4},{6,5},{7,6},{8,7},{9,8},{10,9},{11,1... | collective-permute-start | bytes 196616 | tf_op jit(solution)/shard_map/ppermute | solution.py:609
  7.6 0.0 copy-start
  7.6 0.0 copy-start.1
  7.6 0.0 copy-start.2
  7.6 0.0 copy-start.3
  7.6 0.0 copy-start.4
  7.7 0.0 copy-start.5
  7.7 0.0 copy-start.6
  7.7 0.0 copy-start.7
  7.7 0.0 copy-start.8
  7.7 0.0 copy-start.9
  7.7 0.0 copy-start.11
  7.7 0.0 copy-start.12
  7.7 0.0 copy-start.13
  7.8 0.0 copy-start.14
  7.8 4.1 %shard_map.231.half_ref = f32[4096,256]{1,0:T(8,128)S(1)} custom-call(s32[1,4096]{1,0:T(1,128)} %send_ref.1, s32[1,4096]{1,0:T(1,128)} %recv_ref.1, s32[1,32]{1,0:T(1,128)} %fill_ref.1, bf16[4096,256]{1,0:T(8,128)(2,1)} %bitcast.16, bf16[512,256]{1,0:T(8,128)(2,1)} %bitcast.19, bf16[768,256]{1,0:T(8,128)(2,1)} %ewi_ref.3, f32[1,256]{1,0:T(1,128)} %bitcast.29), custom_call_target="tpu_custom_call" | custom-call | tf_op jit(solution)/shard_map/pallas_call | solution.py:523
  11.9 0.0 collective-permute-done.hlow_ref
  11.9 0.0 collective-permute-done.1.hup_ref
  11.9 0.0 copy-done
  11.9 0.0 copy-done.1
  11.9 0.0 copy-done.2
  11.9 0.0 copy-done.3
  12.0 0.0 copy-done.4
  12.1 13.3 %shard_map.233 = (bf16[4096,256]{1,0:T(8,128)(2,1)}, bf16[4096,256]{1,0:T(8,128)(2,1)}, f32[512,256]{1,0:T(8,128)S(1)}, bf16[512,512]{1,0:T(8,128)(2,1)S(1)}, bf...) custom-call(s32[1,4096]{1,0:T(1,128)S(1)} %copy-done.8, ...), custom_call_target="tpu_custom_call" | custom-call | tf_op jit(solution)/shard_map/pallas_call | solution.py:555
  25.4 1.4 %collective-permute-start.2 = (bf16[32,64,128]{2,1,0:T(8,128)(2,1)S(1)}, bf16[32,64,128]{2,1,0:T(8,128)(2,1)S(1)}, u32[]{:S(2)}, u32[]{:S(2)}) collective-permute-start(bf16[32,64,128]{2,1,0:T(8,128)(2,1)S(1)} %get-tuple-element.44), channel_id=1, source_target_pairs={{0,32},{32,0},{64,96},{96,64},{128,160},{160,128},{192,224},{224,1... | collective-permute-start | bytes 1572872 | tf_op jit(solution)/shard_map/ppermute | solution.py:580
  26.8 1.5 %collective-permute-done.2 = bf16[32,64,128]{2,1,0:T(8,128)(2,1)S(1)} collective-permute-done((bf16[32,64,128]{2,1,0:T(8,128)(2,1)S(1)}, bf16[32,64,128]{2,1,0:T(8,128)(2,1)S(1)}, u32[]{:S(2)}, u32[]{:S(2)}) %collective-permute-start.2) | collective-permute-done | bytes 524320 | tf_op jit(solution)/shard_map/ppermute | solution.py:580
  28.4 1.0 %add_convert_fusion = bf16[32,64,128]{2,1,0:T(8,128)(2,1)} fusion(f32[32,64,128]{2,1,0:T(8,128)S(1)} %get-tuple-element.43, bf16[32,64,128]{2,1,0:T(8,128)(2,1)S(1)} %collective-permute-done.2), kind=kLoop, calls=%fused_computation.1 | loop fusion | flops 786432 | bytes 2097152 | tf_op jit(solution)/shard_map/convert_element_type | solution.py:641
  29.3 12.8 %all-to-all-start = ((bf16[32,64,128]{2,1,0:T(8,128)(2,1)}), bf16[32,64,128]{2,1,0:T(8,128)(2,1)S(1)}, u32[]{:S(2)}, u32[]{:S(2)}) async-start(bf16[32,64,128]{2,1,0:T(8,128)(2,1)} %add_convert_fusion), calls=%async_computation | async-start | bytes 1048576 | tf_op jit(solution)/shard_map/all_to_all | solution.py:643
  42.2 3.1 %collective-permute-start.3 = (bf16[128,256]{1,0:T(8,128)(2,1)S(1)}, bf16[128,256]{1,0:T(8,128)(2,1)S(1)}, u32[]{:S(2)}, u32[]{:S(2)}) collective-permute-start(bf16[128,256]{1,0:T(8,128)(2,1)S(1)} %get-tuple-element.48), channel_id=1, source_target_pairs={{0,1},{1,2},{2,3},{3,4},{4,5},{5,6},{6,7},{7,8},{8,9},{9,10},{10,1... | collective-permute-start | bytes 196616 | tf_op jit(solution)/shard_map/ppermute | solution.py:640
  45.3 1.3 %collective-permute-start.4 = (bf16[128,256]{1,0:T(8,128)(2,1)S(1)}, bf16[128,256]{1,0:T(8,128)(2,1)S(1)}, u32[]{:S(2)}, u32[]{:S(2)}) collective-permute-start(bf16[128,256]{1,0:T(8,128)(2,1)S(1)} %get-tuple-element.49), channel_id=1, source_target_pairs={{1,0},{2,1},{3,2},{4,3},{5,4},{6,5},{7,6},{8,7},{9,8},{10,9},{11,1... | collective-permute-start | bytes 196616 | tf_op jit(solution)/shard_map/ppermute | solution.py:639
  46.6 0.0 copy-start.10
  46.6 4.1 %shard_map.234 = (bf16[4096,256]{1,0:T(8,128)(2,1)}, f32[512,256]{1,0:T(8,128)S(1)}) custom-call(bf16[4096,256]{1,0:T(8,128)(2,1)} %get-tuple-element.50.msg_hbm, bf16[4096,256]{1,0:T(8,128)(2,1)} %get-tuple-element.51.grad_hbm, f32[512,256]{1,0:T(8,128)S(1)} %get-tuple-element.52.base_ref, bf16[512,512]{1,0:T(8,128)(2,1)S(1)} %get-tuple-element.53.nsum_ref, ...), custom_call_target="tpu_custom_call" | custom-call | tf_op jit(solution)/shard_map/pallas_call | solution.py:564
  50.7 5.6 %all-to-all-done = bf16[32,64,128]{2,1,0:T(8,128)(2,1)S(1)} async-done(((bf16[32,64,128]{2,1,0:T(8,128)(2,1)}), bf16[32,64,128]{2,1,0:T(8,128)(2,1)S(1)}, u32[]{:S(2)}, u32[]{:S(2)}) %all-to-all-start) | async-done | bytes 524320 | tf_op jit(solution)/shard_map/all_to_all | solution.py:643
  56.3 0.1 convert_reduce_fusion
  56.4 0.0 collective-permute-done.3.low_ref
  56.4 0.0 collective-permute-done.4.up_ref
  56.4 2.7 %collective-permute-start.7 = (f32[64,128]{1,0:T(8,128)S(1)}, f32[64,128]{1,0:T(8,128)S(1)}, u32[]{:S(2)}, u32[]{:S(2)}) collective-permute-start(f32[64,128]{1,0:T(8,128)S(1)} %convert_reduce_fusion), channel_id=1, source_target_pairs={{0,192},{32,224},{64,128},{96,160},{128,64},{160,96},{192,0},{224,... | collective-permute-start | bytes 98312 | tf_op jit(solution)/shard_map/ppermute | solution.py:580
  59.2 0.2 collective-permute-start.6
  59.4 0.5 collective-permute-start.5
  59.9 0.9 %shard_map.235 = bf16[512,256]{1,0:T(8,128)(2,1)} custom-call(s32[2,128]{1,0:T(2,128)S(1)} %bitcast.24, f32[512,256]{1,0:T(8,128)S(1)} %get-tuple-element.56.own_ref, bf16[128,256]{1,0:T(8,128)(2,1)S(1)} %collective-permute-done.3.low_ref, bf16[128,256]{1,0:T(8,128)(2,1)S(1)} %collective-permute-done.4.up_ref), custom_call_target="tpu_custom_call" | custom-call | tf_op jit(solution)/shard_map/pallas_call | solution.py:570
  60.8 0.0 collective-permute-done.7
  60.8 2.7 %collective-permute-done.6 = f32[64,128]{1,0:T(8,128)S(1)} collective-permute-done((f32[64,128]{1,0:T(8,128)S(1)}, f32[64,128]{1,0:T(8,128)S(1)}, u32[]{:S(2)}, u32[]{:S(2)}) %collective-permute-start.6) | collective-permute-done | bytes 32800 | tf_op jit(solution)/shard_map/ppermute | solution.py:580
  63.4 0.0 collective-permute-done.5
  63.5 6.9 %collective-permute-start.8 = (f32[64,128]{1,0:T(8,128)S(1)}, f32[64,128]{1,0:T(8,128)S(1)}, u32[]{:S(2)}, u32[]{:S(2)}) collective-permute-start(f32[64,128]{1,0:T(8,128)S(1)} %add_add_fusion.mine_ref), channel_id=1, source_target_pairs={{0,32},{32,0},{64,96},{96,64},{128,160},{160,128},{192,224},{224,1... | collective-permute-start | bytes 98312 | tf_op jit(solution)/shard_map/ppermute | solution.py:580
  70.4 0.9 %collective-permute-done.8.other_ref = f32[64,128]{1,0:T(8,128)S(1)} collective-permute-done((f32[64,128]{1,0:T(8,128)S(1)}, f32[64,128]{1,0:T(8,128)S(1)}, u32[]{:S(2)}, u32[]{:S(2)}) %collective-permute-start.8) | collective-permute-done | bytes 32800 | tf_op jit(solution)/shard_map/ppermute | solution.py:580
  71.3 0.6 shard_map.236
  (11 shorter events, 0.0 us)
Async XLA Ops:
  1.9 10.0 %collective-permute-start = (bf16[128,256]{1,0:T(8,128)(2,1)S(1)}, bf16[128,256]{1,0:T(8,128)(2,1)S(1)}, u32[]{:S(2)}, u32[]{:S(2)}) collective-permute-start(bf16[128,256]{1,0:T(8,128)(2,1)S(1)} %get-tuple-element.41), channel_id=1, source_target_pairs={{0,1},{1,2},{2,3},{3,4},{4,5},{5,6},{6,7},{7,8},{8,9},{9,10},{10,1... | collective-permute-start | bytes 196616 | tf_op jit(solution)/shard_map/ppermute | solution.py:608
  6.3 5.6 %collective-permute-start.1 = (bf16[128,256]{1,0:T(8,128)(2,1)S(1)}, bf16[128,256]{1,0:T(8,128)(2,1)S(1)}, u32[]{:S(2)}, u32[]{:S(2)}) collective-permute-start(bf16[128,256]{1,0:T(8,128)(2,1)S(1)} %get-tuple-element.42), channel_id=1, source_target_pairs={{1,0},{2,1},{3,2},{4,3},{5,4},{6,5},{7,6},{8,7},{9,8},{10,9},{11,1... | collective-permute-start | bytes 196616 | tf_op jit(solution)/shard_map/ppermute | solution.py:609
  7.6 4.3 %copy-start = (bf16[1,4096,256]{2,1,0:T(8,128)(2,1)S(1)}, bf16[1,4096,256]{2,1,0:T(8,128)(2,1)}, u32[]{:S(2)}) copy-start(bf16[1,4096,256]{2,1,0:T(8,128)(2,1)} %param.17) | copy-start | bytes 6291460
  7.6 4.3 %copy-start.1 = (bf16[768,256]{1,0:T(8,128)(2,1)S(1)}, bf16[768,256]{1,0:T(8,128)(2,1)}, u32[]{:S(2)}) copy-start(bf16[768,256]{1,0:T(8,128)(2,1)} %ewi_ref.3) | copy-start | bytes 1179652
  7.6 4.3 %copy-start.2 = (bf16[1,512,256]{2,1,0:T(8,128)(2,1)S(1)}, bf16[1,512,256]{2,1,0:T(8,128)(2,1)}, u32[]{:S(2)}) copy-start(bf16[1,512,256]{2,1,0:T(8,128)(2,1)} %param.16) | copy-start | bytes 786436
  7.6 4.3 %copy-start.3 = (bf16[1,4096,256]{2,1,0:T(8,128)(2,1)S(1)}, bf16[1,4096,256]{2,1,0:T(8,128)(2,1)}, u32[]{:S(2)}) copy-start(bf16[1,4096,256]{2,1,0:T(8,128)(2,1)} %param.19) | copy-start | bytes 6291460
  7.6 4.3 %copy-start.4 = (bf16[1,512,256]{2,1,0:T(8,128)(2,1)S(1)}, bf16[1,512,256]{2,1,0:T(8,128)(2,1)}, u32[]{:S(2)}) copy-start(bf16[1,512,256]{2,1,0:T(8,128)(2,1)} %param.18) | copy-start | bytes 786436
  7.7 4.3 %copy-start.5 = (bf16[512,256]{1,0:T(8,128)(2,1)S(1)}, bf16[512,256]{1,0:T(8,128)(2,1)}, u32[]{:S(2)}) copy-start(bf16[512,256]{1,0:T(8,128)(2,1)} %nwi_ref.1) | copy-start | bytes 786436
  7.7 4.3 %copy-start.6 = (bf16[256,256]{1,0:T(8,128)(2,1)S(1)}, bf16[256,256]{1,0:T(8,128)(2,1)}, u32[]{:S(2)}) copy-start(bf16[256,256]{1,0:T(8,128)(2,1)} %ewo_ref.1) | copy-start | bytes 393220
  7.7 4.3 %copy-start.7 = (bf16[256,256]{1,0:T(8,128)(2,1)S(1)}, bf16[256,256]{1,0:T(8,128)(2,1)}, u32[]{:S(2)}) copy-start(bf16[256,256]{1,0:T(8,128)(2,1)} %nwo_ref.1) | copy-start | bytes 393220
  7.7 4.3 %copy-start.8 = (s32[1,4096]{1,0:T(1,128)S(1)}, s32[1,4096]{1,0:T(1,128)}, u32[]{:S(2)}) copy-start(s32[1,4096]{1,0:T(1,128)} %send_ref.1) | copy-start | bytes 49156
  7.7 4.3 %copy-start.9 = (s32[1,4096]{1,0:T(1,128)S(1)}, s32[1,4096]{1,0:T(1,128)}, u32[]{:S(2)}) copy-start(s32[1,4096]{1,0:T(1,128)} %recv_ref.1) | copy-start | bytes 49156
  7.7 4.3 %copy-start.11 = (s32[1,32]{1,0:T(1,128)S(1)}, s32[1,32]{1,0:T(1,128)}, u32[]{:S(2)}) copy-start(s32[1,32]{1,0:T(1,128)} %fill_ref.1) | copy-start | bytes 388
  7.7 4.3 %copy-start.12 = (f32[256]{0:T(256)S(1)}, f32[256]{0:T(256)}, u32[]{:S(2)}) copy-start(f32[256]{0:T(256)} %param.23) | copy-start | bytes 3076
  7.7 4.3 %copy-start.13 = (f32[256]{0:T(256)S(1)}, f32[256]{0:T(256)}, u32[]{:S(2)}) copy-start(f32[256]{0:T(256)} %param.25) | copy-start | bytes 3076
  7.8 4.3 %copy-start.14 = (f32[256]{0:T(256)S(1)}, f32[256]{0:T(256)}, u32[]{:S(2)}) copy-start(f32[256]{0:T(256)} %param.27) | copy-start | bytes 3076
  25.4 3.0 %collective-permute-start.2 = (bf16[32,64,128]{2,1,0:T(8,128)(2,1)S(1)}, bf16[32,64,128]{2,1,0:T(8,128)(2,1)S(1)}, u32[]{:S(2)}, u32[]{:S(2)}) collective-permute-start(bf16[32,64,128]{2,1,0:T(8,128)(2,1)S(1)} %get-tuple-element.44), channel_id=1, source_target_pairs={{0,32},{32,0},{64,96},{96,64},{128,160},{160,128},{192,224},{224,1... | collective-permute-start | bytes 1572872 | tf_op jit(solution)/shard_map/ppermute | solution.py:580
  29.3 27.0 %all-to-all-start = ((bf16[32,64,128]{2,1,0:T(8,128)(2,1)}), bf16[32,64,128]{2,1,0:T(8,128)(2,1)S(1)}, u32[]{:S(2)}, u32[]{:S(2)}) async-start(bf16[32,64,128]{2,1,0:T(8,128)(2,1)} %add_convert_fusion), calls=%async_computation | async-start | bytes 1048576 | tf_op jit(solution)/shard_map/all_to_all | solution.py:643
  42.2 14.2 %collective-permute-start.3 = (bf16[128,256]{1,0:T(8,128)(2,1)S(1)}, bf16[128,256]{1,0:T(8,128)(2,1)S(1)}, u32[]{:S(2)}, u32[]{:S(2)}) collective-permute-start(bf16[128,256]{1,0:T(8,128)(2,1)S(1)} %get-tuple-element.48), channel_id=1, source_target_pairs={{0,1},{1,2},{2,3},{3,4},{4,5},{5,6},{6,7},{7,8},{8,9},{9,10},{10,1... | collective-permute-start | bytes 196616 | tf_op jit(solution)/shard_map/ppermute | solution.py:640
  45.3 11.1 %collective-permute-start.4 = (bf16[128,256]{1,0:T(8,128)(2,1)S(1)}, bf16[128,256]{1,0:T(8,128)(2,1)S(1)}, u32[]{:S(2)}, u32[]{:S(2)}) collective-permute-start(bf16[128,256]{1,0:T(8,128)(2,1)S(1)} %get-tuple-element.49), channel_id=1, source_target_pairs={{1,0},{2,1},{3,2},{4,3},{5,4},{6,5},{7,6},{8,7},{9,8},{10,9},{11,1... | collective-permute-start | bytes 196616 | tf_op jit(solution)/shard_map/ppermute | solution.py:639
  46.6 13.2 %copy-start.10 = (s32[1,2,128]{2,1,0:T(2,128)S(1)}, s32[1,2,128]{2,1,0:T(2,128)}, u32[]{:S(2)}) copy-start(s32[1,2,128]{2,1,0:T(2,128)} %param.31) | copy-start | bytes 3076
  56.4 4.4 %collective-permute-start.7 = (f32[64,128]{1,0:T(8,128)S(1)}, f32[64,128]{1,0:T(8,128)S(1)}, u32[]{:S(2)}, u32[]{:S(2)}) collective-permute-start(f32[64,128]{1,0:T(8,128)S(1)} %convert_reduce_fusion), channel_id=1, source_target_pairs={{0,192},{32,224},{64,128},{96,160},{128,64},{160,96},{192,0},{224,... | collective-permute-start | bytes 98312 | tf_op jit(solution)/shard_map/ppermute | solution.py:580
  59.2 4.3 %collective-permute-start.6 = (f32[64,128]{1,0:T(8,128)S(1)}, f32[64,128]{1,0:T(8,128)S(1)}, u32[]{:S(2)}, u32[]{:S(2)}) collective-permute-start(f32[64,128]{1,0:T(8,128)S(1)} %convert_reduce_fusion), channel_id=1, source_target_pairs={{0,128},{32,160},{64,192},{96,224},{128,0},{160,32},{192,64},{224,... | collective-permute-start | bytes 98312 | tf_op jit(solution)/shard_map/ppermute | solution.py:580
  59.4 4.1 %collective-permute-start.5 = (f32[64,128]{1,0:T(8,128)S(1)}, f32[64,128]{1,0:T(8,128)S(1)}, u32[]{:S(2)}, u32[]{:S(2)}) collective-permute-start(f32[64,128]{1,0:T(8,128)S(1)} %convert_reduce_fusion), channel_id=1, source_target_pairs={{0,64},{32,96},{64,0},{96,32},{128,192},{160,224},{192,128},{224,1... | collective-permute-start | bytes 98312 | tf_op jit(solution)/shard_map/ppermute | solution.py:580
  63.5 7.8 %collective-permute-start.8 = (f32[64,128]{1,0:T(8,128)S(1)}, f32[64,128]{1,0:T(8,128)S(1)}, u32[]{:S(2)}, u32[]{:S(2)}) collective-permute-start(f32[64,128]{1,0:T(8,128)S(1)} %add_add_fusion.mine_ref), channel_id=1, source_target_pairs={{0,32},{32,0},{64,96},{96,64},{128,160},{160,128},{192,224},{224,1... | collective-permute-start | bytes 98312 | tf_op jit(solution)/shard_map/ppermute | solution.py:580

commit v5 on v4

--- a/solution.py
+++ b/solution.py
@@ -643,12 +643,9 @@
     parts = lax.all_to_all(values, "dom", 0, 0, tiled=True)
     gedge, own = inputs(msg, grad, base, node_sums, edge_w_in)
     values = jnp.sum(parts.astype(F32), 0)
-    values, back_lower, back_upper, own = lax.optimization_barrier(
-        (values, back_lower, back_upper, own)
-    )
+    grad_nodes = finish(lists, own, back_lower, back_upper)
+    values, grad_nodes = lax.optimization_barrier((values, grad_nodes))
     others = [swap(values, "rep", flip) for flip in (2, 4, 6)]
-    grad_nodes = finish(lists, own, back_lower, back_upper)
-    others, grad_nodes = lax.optimization_barrier((others, grad_nodes))
     values = values + others[0] + others[1] + others[2]
     ewi, ewo, nwi, nwo, *vec = unpack(core, values, swap(values, "rep", 1))
     return (

time: 72.1 us -> 72.1 us (level)
    all_to_all x1, waiting for transfers between devices: 5.61 us -> 0.01 us  [per_device(): parts = lax.all_to_all(values, 'dom', 0, 0, tiled=True)]
    ppermute x1, waiting for transfers between devices: 0.01 us -> 2.91 us  [per_device(): back_upper = lax.ppermute(glow, 'dom', fall)]
    ppermute x1, waiting for transfers between devices: 0.01 us -> 2.14 us  [per_device(): back_lower = lax.ppermute(gup, 'dom', rise)]
    ppermute x5, waiting for transfers between devices: 5.06 us -> 5.9 us  [swap(): return lax.ppermute(values, axis, [(i, i ^ flip) for i in range(count)])]
  transfers between devices with their start and end apart: 10 -> 10, of which waited for: 4 -> 6; matrix products, arithmetic and copies ran while one was open for 0% -> 0% of each run, Pallas kernels for 13% -> 13%
where the time goes in v5:
time: 72.1 us; the launch traced here: 71.7 us
  starting transfers between devices  34.3 us (48%)
  Pallas kernels  24.3 us (34%)
  waiting for transfers between devices  11 us (15%)
  other arithmetic  1.05 us (1%)
  between operations  0.98 us (1%)
    pallas_call x1, Pallas kernels, layer(): on_device(layer_kernel, outs, scratch, 'vvssvvvvvvvvvvvvvv', 'hhvvvvvv', 30)  13.3 us
    all_to_all x1, starting transfers between devices, per_device(): parts = lax.all_to_all(values, 'dom', 0, 0, tiled=True)  12.8 us
    ppermute x5, starting transfers between devices, swap(): return lax.ppermute(values, axis, [(i, i ^ flip) for i in range(count)])  11.3 us
    ppermute x5, waiting for transfers between devices, swap(): return lax.ppermute(values, axis, [(i, i ^ flip) for i in range(count)])  5.9 us
    ppermute x1, starting transfers between devices, per_device(): halo_lower = lax.ppermute(to_upper, 'dom', rise)  4.37 us
    pallas_call x1, Pallas kernels, local(): on_device(local_kernel, shape(EDGE, D), scratch, 'hhhhhhh', 'v', 10)  4.13 us
    pallas_call x1, Pallas kernels, inputs(): on_device(inputs_kernel, outs, scratch, 'hhvvv', 'hv', 10)  4.07 us
    ppermute x1, starting transfers between devices, per_device(): back_lower = lax.ppermute(gup, 'dom', rise)  3.14 us
  transfers between devices with their start and end apart: 10, of which 6 were waited for; matrix products, arithmetic and copies ran while one was open for 0% of the time, Pallas kernels for 13%

profile of v5, /device:TPU:1, one launch (start us, length us, event | category | flops | bytes accessed | tf_op | source)
XLA Modules:
  0.0 71.7 jit_solution(5203578998145778456)
XLA Ops:
  0.6 1.3 %shard_map.232 = (bf16[128,256]{1,0:T(8,128)(2,1)S(1)}, bf16[128,256]{1,0:T(8,128)(2,1)S(1)}) custom-call(s32[2,128]{1,0:T(2,128)} %bitcast.23, bf16[512,256]{1,0:T(8,128)(2,1)} %bitcast.18), custom_call_target="tpu_custom_call" | custom-call | tf_op jit(solution)/shard_map/pallas_call | solution.py:508
  1.9 4.4 %collective-permute-start = (bf16[128,256]{1,0:T(8,128)(2,1)S(1)}, bf16[128,256]{1,0:T(8,128)(2,1)S(1)}, u32[]{:S(2)}, u32[]{:S(2)}) collective-permute-start(bf16[128,256]{1,0:T(8,128)(2,1)S(1)} %get-tuple-element.35), channel_id=1, source_target_pairs={{0,1},{1,2},{2,3},{3,4},{4,5},{5,6},{6,7},{7,8},{8,9},{9,10},{10,1... | collective-permute-start | bytes 196616 | tf_op jit(solution)/shard_map/ppermute | solution.py:608
  6.3 1.3 %collective-permute-start.1 = (bf16[128,256]{1,0:T(8,128)(2,1)S(1)}, bf16[128,256]{1,0:T(8,128)(2,1)S(1)}, u32[]{:S(2)}, u32[]{:S(2)}) collective-permute-start(bf16[128,256]{1,0:T(8,128)(2,1)S(1)} %get-tuple-element.36), channel_id=1, source_target_pairs={{1,0},{2,1},{3,2},{4,3},{5,4},{6,5},{7,6},{8,7},{9,8},{10,9},{11,1... | collective-permute-start | bytes 196616 | tf_op jit(solution)/shard_map/ppermute | solution.py:609
  7.6 0.0 copy-start
  7.6 0.0 copy-start.1
  7.6 0.0 copy-start.2
  7.6 0.0 copy-start.3
  7.6 0.0 copy-start.4
  7.7 0.0 copy-start.5
  7.7 0.0 copy-start.6
  7.7 0.0 copy-start.7
  7.7 0.0 copy-start.8
  7.7 0.0 copy-start.9
  7.7 0.0 copy-start.11
  7.7 0.0 copy-start.12
  7.7 0.0 copy-start.13
  7.8 0.0 copy-start.14
  7.8 4.1 %shard_map.231.half_ref = f32[4096,256]{1,0:T(8,128)S(1)} custom-call(s32[1,4096]{1,0:T(1,128)} %send_ref.1, s32[1,4096]{1,0:T(1,128)} %recv_ref.1, s32[1,32]{1,0:T(1,128)} %fill_ref.1, bf16[4096,256]{1,0:T(8,128)(2,1)} %bitcast.16, bf16[512,256]{1,0:T(8,128)(2,1)} %bitcast.19, bf16[768,256]{1,0:T(8,128)(2,1)} %ewi_ref.3, f32[1,256]{1,0:T(1,128)} %bitcast.29), custom_call_target="tpu_custom_call" | custom-call | tf_op jit(solution)/shard_map/pallas_call | solution.py:523
  11.9 0.0 collective-permute-done.hlow_ref
  11.9 0.0 collective-permute-done.1.hup_ref
  11.9 0.0 copy-done
  11.9 0.0 copy-done.1
  11.9 0.0 copy-done.2
  11.9 0.0 copy-done.3
  12.0 0.0 copy-done.4
  12.1 13.3 %shard_map.233 = (bf16[4096,256]{1,0:T(8,128)(2,1)}, bf16[4096,256]{1,0:T(8,128)(2,1)}, f32[512,256]{1,0:T(8,128)S(1)}, bf16[512,512]{1,0:T(8,128)(2,1)S(1)}, bf...) custom-call(s32[1,4096]{1,0:T(1,128)S(1)} %copy-done.8, ...), custom_call_target="tpu_custom_call" | custom-call | tf_op jit(solution)/shard_map/pallas_call | solution.py:555
  25.4 1.4 %collective-permute-start.2 = (bf16[32,64,128]{2,1,0:T(8,128)(2,1)S(1)}, bf16[32,64,128]{2,1,0:T(8,128)(2,1)S(1)}, u32[]{:S(2)}, u32[]{:S(2)}) collective-permute-start(bf16[32,64,128]{2,1,0:T(8,128)(2,1)S(1)} %get-tuple-element.38), channel_id=1, source_target_pairs={{0,32},{32,0},{64,96},{96,64},{128,160},{160,128},{192,224},{224,1... | collective-permute-start | bytes 1572872 | tf_op jit(solution)/shard_map/ppermute | solution.py:580
  26.8 1.5 %collective-permute-done.2 = bf16[32,64,128]{2,1,0:T(8,128)(2,1)S(1)} collective-permute-done((bf16[32,64,128]{2,1,0:T(8,128)(2,1)S(1)}, bf16[32,64,128]{2,1,0:T(8,128)(2,1)S(1)}, u32[]{:S(2)}, u32[]{:S(2)}) %collective-permute-start.2) | collective-permute-done | bytes 524320 | tf_op jit(solution)/shard_map/ppermute | solution.py:580
  28.4 1.0 %add_convert_fusion = bf16[32,64,128]{2,1,0:T(8,128)(2,1)} fusion(f32[32,64,128]{2,1,0:T(8,128)S(1)} %get-tuple-element.37, bf16[32,64,128]{2,1,0:T(8,128)(2,1)S(1)} %collective-permute-done.2), kind=kLoop, calls=%fused_computation.1 | loop fusion | flops 786432 | bytes 2097152 | tf_op jit(solution)/shard_map/convert_element_type | solution.py:641
  29.3 12.8 %all-to-all-start = ((bf16[32,64,128]{2,1,0:T(8,128)(2,1)}), bf16[32,64,128]{2,1,0:T(8,128)(2,1)S(1)}, u32[]{:S(2)}, u32[]{:S(2)}) async-start(bf16[32,64,128]{2,1,0:T(8,128)(2,1)} %add_convert_fusion), calls=%async_computation | async-start | bytes 1048576 | tf_op jit(solution)/shard_map/all_to_all | solution.py:643
  42.2 3.1 %collective-permute-start.3 = (bf16[128,256]{1,0:T(8,128)(2,1)S(1)}, bf16[128,256]{1,0:T(8,128)(2,1)S(1)}, u32[]{:S(2)}, u32[]{:S(2)}) collective-permute-start(bf16[128,256]{1,0:T(8,128)(2,1)S(1)} %get-tuple-element.47), channel_id=1, source_target_pairs={{0,1},{1,2},{2,3},{3,4},{4,5},{5,6},{6,7},{7,8},{8,9},{9,10},{10,1... | collective-permute-start | bytes 196616 | tf_op jit(solution)/shard_map/ppermute | solution.py:640
  45.3 1.3 %collective-permute-start.4 = (bf16[128,256]{1,0:T(8,128)(2,1)S(1)}, bf16[128,256]{1,0:T(8,128)(2,1)S(1)}, u32[]{:S(2)}, u32[]{:S(2)}) collective-permute-start(bf16[128,256]{1,0:T(8,128)(2,1)S(1)} %get-tuple-element.48), channel_id=1, source_target_pairs={{1,0},{2,1},{3,2},{4,3},{5,4},{6,5},{7,6},{8,7},{9,8},{10,9},{11,1... | collective-permute-start | bytes 196616 | tf_op jit(solution)/shard_map/ppermute | solution.py:639
  46.6 0.0 copy-start.10
  46.6 4.1 %shard_map.234 = (bf16[4096,256]{1,0:T(8,128)(2,1)}, f32[512,256]{1,0:T(8,128)S(1)}) custom-call(bf16[4096,256]{1,0:T(8,128)(2,1)} %get-tuple-element.42.msg_hbm, bf16[4096,256]{1,0:T(8,128)(2,1)} %get-tuple-element.43.grad_hbm, f32[512,256]{1,0:T(8,128)S(1)} %get-tuple-element.44.base_ref, bf16[512,512]{1,0:T(8,128)(2,1)S(1)} %get-tuple-element.45.nsum_ref, ...), custom_call_target="tpu_custom_call" | custom-call | tf_op jit(solution)/shard_map/pallas_call | solution.py:564
  50.7 2.1 %collective-permute-done.3.low_ref = bf16[128,256]{1,0:T(8,128)(2,1)S(1)} collective-permute-done((bf16[128,256]{1,0:T(8,128)(2,1)S(1)}, bf16[128,256]{1,0:T(8,128)(2,1)S(1)}, u32[]{:S(2)}, u32[]{:S(2)}) %collective-permute-start.3) | collective-permute-done | bytes 65568 | tf_op jit(solution)/shard_map/ppermute | solution.py:640
  52.9 2.9 %collective-permute-done.4.up_ref = bf16[128,256]{1,0:T(8,128)(2,1)S(1)} collective-permute-done((bf16[128,256]{1,0:T(8,128)(2,1)S(1)}, bf16[128,256]{1,0:T(8,128)(2,1)S(1)}, u32[]{:S(2)}, u32[]{:S(2)}) %collective-permute-start.4) | collective-permute-done | bytes 65568 | tf_op jit(solution)/shard_map/ppermute | solution.py:639
  55.8 0.9 %shard_map.235 = bf16[512,256]{1,0:T(8,128)(2,1)} custom-call(s32[2,128]{1,0:T(2,128)S(1)} %bitcast.24, f32[512,256]{1,0:T(8,128)S(1)} %get-tuple-element.46.own_ref, bf16[128,256]{1,0:T(8,128)(2,1)S(1)} %collective-permute-done.3.low_ref, bf16[128,256]{1,0:T(8,128)(2,1)S(1)} %collective-permute-done.4.up_ref), custom_call_target="tpu_custom_call" | custom-call | tf_op jit(solution)/shard_map/pallas_call | solution.py:570
  56.7 0.0 all-to-all-done
  56.7 0.1 convert_reduce_fusion
  56.8 2.6 %collective-permute-start.7 = (f32[64,128]{1,0:T(8,128)S(1)}, f32[64,128]{1,0:T(8,128)S(1)}, u32[]{:S(2)}, u32[]{:S(2)}) collective-permute-start(f32[64,128]{1,0:T(8,128)S(1)} %convert_reduce_fusion), channel_id=1, source_target_pairs={{0,192},{32,224},{64,128},{96,160},{128,64},{160,96},{192,0},{224,... | collective-permute-start | bytes 98312 | tf_op jit(solution)/shard_map/ppermute | solution.py:580
  59.4 0.4 collective-permute-start.6
  59.8 0.4 collective-permute-start.5
  60.1 1.0 %collective-permute-done.7 = f32[64,128]{1,0:T(8,128)S(1)} collective-permute-done((f32[64,128]{1,0:T(8,128)S(1)}, f32[64,128]{1,0:T(8,128)S(1)}, u32[]{:S(2)}, u32[]{:S(2)}) %collective-permute-start.7) | collective-permute-done | bytes 32800 | tf_op jit(solution)/shard_map/ppermute | solution.py:580
  61.1 2.5 %collective-permute-done.6 = f32[64,128]{1,0:T(8,128)S(1)} collective-permute-done((f32[64,128]{1,0:T(8,128)S(1)}, f32[64,128]{1,0:T(8,128)S(1)}, u32[]{:S(2)}, u32[]{:S(2)}) %collective-permute-start.6) | collective-permute-done | bytes 32800 | tf_op jit(solution)/shard_map/ppermute | solution.py:580
  63.6 0.0 collective-permute-done.5
  63.6 6.6 %collective-permute-start.8 = (f32[64,128]{1,0:T(8,128)S(1)}, f32[64,128]{1,0:T(8,128)S(1)}, u32[]{:S(2)}, u32[]{:S(2)}) collective-permute-start(f32[64,128]{1,0:T(8,128)S(1)} %add_add_fusion.mine_ref), channel_id=1, source_target_pairs={{0,32},{32,0},{64,96},{96,64},{128,160},{160,128},{192,224},{224,1... | collective-permute-start | bytes 98312 | tf_op jit(solution)/shard_map/ppermute | solution.py:580
  70.2 0.9 %collective-permute-done.8.other_ref = f32[64,128]{1,0:T(8,128)S(1)} collective-permute-done((f32[64,128]{1,0:T(8,128)S(1)}, f32[64,128]{1,0:T(8,128)S(1)}, u32[]{:S(2)}, u32[]{:S(2)}) %collective-permute-start.8) | collective-permute-done | bytes 32800 | tf_op jit(solution)/shard_map/ppermute | solution.py:580
  71.1 0.6 shard_map.236
  (11 shorter events, 0.0 us)
Async XLA Ops:
  1.9 10.0 %collective-permute-start = (bf16[128,256]{1,0:T(8,128)(2,1)S(1)}, bf16[128,256]{1,0:T(8,128)(2,1)S(1)}, u32[]{:S(2)}, u32[]{:S(2)}) collective-permute-start(bf16[128,256]{1,0:T(8,128)(2,1)S(1)} %get-tuple-element.35), channel_id=1, source_target_pairs={{0,1},{1,2},{2,3},{3,4},{4,5},{5,6},{6,7},{7,8},{8,9},{9,10},{10,1... | collective-permute-start | bytes 196616 | tf_op jit(solution)/shard_map/ppermute | solution.py:608
  6.3 5.6 %collective-permute-start.1 = (bf16[128,256]{1,0:T(8,128)(2,1)S(1)}, bf16[128,256]{1,0:T(8,128)(2,1)S(1)}, u32[]{:S(2)}, u32[]{:S(2)}) collective-permute-start(bf16[128,256]{1,0:T(8,128)(2,1)S(1)} %get-tuple-element.36), channel_id=1, source_target_pairs={{1,0},{2,1},{3,2},{4,3},{5,4},{6,5},{7,6},{8,7},{9,8},{10,9},{11,1... | collective-permute-start | bytes 196616 | tf_op jit(solution)/shard_map/ppermute | solution.py:609
  7.6 4.3 %copy-start = (bf16[1,4096,256]{2,1,0:T(8,128)(2,1)S(1)}, bf16[1,4096,256]{2,1,0:T(8,128)(2,1)}, u32[]{:S(2)}) copy-start(bf16[1,4096,256]{2,1,0:T(8,128)(2,1)} %param.17) | copy-start | bytes 6291460
  7.6 4.3 %copy-start.1 = (bf16[768,256]{1,0:T(8,128)(2,1)S(1)}, bf16[768,256]{1,0:T(8,128)(2,1)}, u32[]{:S(2)}) copy-start(bf16[768,256]{1,0:T(8,128)(2,1)} %ewi_ref.3) | copy-start | bytes 1179652
  7.6 4.3 %copy-start.2 = (bf16[1,512,256]{2,1,0:T(8,128)(2,1)S(1)}, bf16[1,512,256]{2,1,0:T(8,128)(2,1)}, u32[]{:S(2)}) copy-start(bf16[1,512,256]{2,1,0:T(8,128)(2,1)} %param.16) | copy-start | bytes 786436
  7.6 4.3 %copy-start.3 = (bf16[1,4096,256]{2,1,0:T(8,128)(2,1)S(1)}, bf16[1,4096,256]{2,1,0:T(8,128)(2,1)}, u32[]{:S(2)}) copy-start(bf16[1,4096,256]{2,1,0:T(8,128)(2,1)} %param.19) | copy-start | bytes 6291460
  7.6 4.3 %copy-start.4 = (bf16[1,512,256]{2,1,0:T(8,128)(2,1)S(1)}, bf16[1,512,256]{2,1,0:T(8,128)(2,1)}, u32[]{:S(2)}) copy-start(bf16[1,512,256]{2,1,0:T(8,128)(2,1)} %param.18) | copy-start | bytes 786436
  7.7 4.3 %copy-start.5 = (bf16[512,256]{1,0:T(8,128)(2,1)S(1)}, bf16[512,256]{1,0:T(8,128)(2,1)}, u32[]{:S(2)}) copy-start(bf16[512,256]{1,0:T(8,128)(2,1)} %nwi_ref.1) | copy-start | bytes 786436
  7.7 4.3 %copy-start.6 = (bf16[256,256]{1,0:T(8,128)(2,1)S(1)}, bf16[256,256]{1,0:T(8,128)(2,1)}, u32[]{:S(2)}) copy-start(bf16[256,256]{1,0:T(8,128)(2,1)} %ewo_ref.1) | copy-start | bytes 393220
  7.7 4.3 %copy-start.7 = (bf16[256,256]{1,0:T(8,128)(2,1)S(1)}, bf16[256,256]{1,0:T(8,128)(2,1)}, u32[]{:S(2)}) copy-start(bf16[256,256]{1,0:T(8,128)(2,1)} %nwo_ref.1) | copy-start | bytes 393220
  7.7 4.3 %copy-start.8 = (s32[1,4096]{1,0:T(1,128)S(1)}, s32[1,4096]{1,0:T(1,128)}, u32[]{:S(2)}) copy-start(s32[1,4096]{1,0:T(1,128)} %send_ref.1) | copy-start | bytes 49156
  7.7 4.3 %copy-start.9 = (s32[1,4096]{1,0:T(1,128)S(1)}, s32[1,4096]{1,0:T(1,128)}, u32[]{:S(2)}) copy-start(s32[1,4096]{1,0:T(1,128)} %recv_ref.1) | copy-start | bytes 49156
  7.7 4.3 %copy-start.11 = (s32[1,32]{1,0:T(1,128)S(1)}, s32[1,32]{1,0:T(1,128)}, u32[]{:S(2)}) copy-start(s32[1,32]{1,0:T(1,128)} %fill_ref.1) | copy-start | bytes 388
  7.7 4.3 %copy-start.12 = (f32[256]{0:T(256)S(1)}, f32[256]{0:T(256)}, u32[]{:S(2)}) copy-start(f32[256]{0:T(256)} %param.23) | copy-start | bytes 3076
  7.7 4.3 %copy-start.13 = (f32[256]{0:T(256)S(1)}, f32[256]{0:T(256)}, u32[]{:S(2)}) copy-start(f32[256]{0:T(256)} %param.25) | copy-start | bytes 3076
  7.8 4.3 %copy-start.14 = (f32[256]{0:T(256)S(1)}, f32[256]{0:T(256)}, u32[]{:S(2)}) copy-start(f32[256]{0:T(256)} %param.27) | copy-start | bytes 3076
  25.4 3.0 %collective-permute-start.2 = (bf16[32,64,128]{2,1,0:T(8,128)(2,1)S(1)}, bf16[32,64,128]{2,1,0:T(8,128)(2,1)S(1)}, u32[]{:S(2)}, u32[]{:S(2)}) collective-permute-start(bf16[32,64,128]{2,1,0:T(8,128)(2,1)S(1)} %get-tuple-element.38), channel_id=1, source_target_pairs={{0,32},{32,0},{64,96},{96,64},{128,160},{160,128},{192,224},{224,1... | collective-permute-start | bytes 1572872 | tf_op jit(solution)/shard_map/ppermute | solution.py:580
  29.3 27.4 %all-to-all-start = ((bf16[32,64,128]{2,1,0:T(8,128)(2,1)}), bf16[32,64,128]{2,1,0:T(8,128)(2,1)S(1)}, u32[]{:S(2)}, u32[]{:S(2)}) async-start(bf16[32,64,128]{2,1,0:T(8,128)(2,1)} %add_convert_fusion), calls=%async_computation | async-start | bytes 1048576 | tf_op jit(solution)/shard_map/all_to_all | solution.py:643
  42.2 10.7 %collective-permute-start.3 = (bf16[128,256]{1,0:T(8,128)(2,1)S(1)}, bf16[128,256]{1,0:T(8,128)(2,1)S(1)}, u32[]{:S(2)}, u32[]{:S(2)}) collective-permute-start(bf16[128,256]{1,0:T(8,128)(2,1)S(1)} %get-tuple-element.47), channel_id=1, source_target_pairs={{0,1},{1,2},{2,3},{3,4},{4,5},{5,6},{6,7},{7,8},{8,9},{9,10},{10,1... | collective-permute-start | bytes 196616 | tf_op jit(solution)/shard_map/ppermute | solution.py:640
  45.3 10.4 %collective-permute-start.4 = (bf16[128,256]{1,0:T(8,128)(2,1)S(1)}, bf16[128,256]{1,0:T(8,128)(2,1)S(1)}, u32[]{:S(2)}, u32[]{:S(2)}) collective-permute-start(bf16[128,256]{1,0:T(8,128)(2,1)S(1)} %get-tuple-element.48), channel_id=1, source_target_pairs={{1,0},{2,1},{3,2},{4,3},{5,4},{6,5},{7,6},{8,7},{9,8},{10,9},{11,1... | collective-permute-start | bytes 196616 | tf_op jit(solution)/shard_map/ppermute | solution.py:639
  46.6 9.1 %copy-start.10 = (s32[1,2,128]{2,1,0:T(2,128)S(1)}, s32[1,2,128]{2,1,0:T(2,128)}, u32[]{:S(2)}) copy-start(s32[1,2,128]{2,1,0:T(2,128)} %param.31) | copy-start | bytes 3076
  56.8 4.4 %collective-permute-start.7 = (f32[64,128]{1,0:T(8,128)S(1)}, f32[64,128]{1,0:T(8,128)S(1)}, u32[]{:S(2)}, u32[]{:S(2)}) collective-permute-start(f32[64,128]{1,0:T(8,128)S(1)} %convert_reduce_fusion), channel_id=1, source_target_pairs={{0,192},{32,224},{64,128},{96,160},{128,64},{160,96},{192,0},{224,... | collective-permute-start | bytes 98312 | tf_op jit(solution)/shard_map/ppermute | solution.py:580
  59.4 4.3 %collective-permute-start.6 = (f32[64,128]{1,0:T(8,128)S(1)}, f32[64,128]{1,0:T(8,128)S(1)}, u32[]{:S(2)}, u32[]{:S(2)}) collective-permute-start(f32[64,128]{1,0:T(8,128)S(1)} %convert_reduce_fusion), channel_id=1, source_target_pairs={{0,128},{32,160},{64,192},{96,224},{128,0},{160,32},{192,64},{224,... | collective-permute-start | bytes 98312 | tf_op jit(solution)/shard_map/ppermute | solution.py:580
  59.8 3.9 %collective-permute-start.5 = (f32[64,128]{1,0:T(8,128)S(1)}, f32[64,128]{1,0:T(8,128)S(1)}, u32[]{:S(2)}, u32[]{:S(2)}) collective-permute-start(f32[64,128]{1,0:T(8,128)S(1)} %convert_reduce_fusion), channel_id=1, source_target_pairs={{0,64},{32,96},{64,0},{96,32},{128,192},{160,224},{192,128},{224,1... | collective-permute-start | bytes 98312 | tf_op jit(solution)/shard_map/ppermute | solution.py:580
  63.6 7.4 %collective-permute-start.8 = (f32[64,128]{1,0:T(8,128)S(1)}, f32[64,128]{1,0:T(8,128)S(1)}, u32[]{:S(2)}, u32[]{:S(2)}) collective-permute-start(f32[64,128]{1,0:T(8,128)S(1)} %add_add_fusion.mine_ref), channel_id=1, source_target_pairs={{0,32},{32,0},{64,96},{96,64},{128,160},{160,128},{192,224},{224,1... | collective-permute-start | bytes 98312 | tf_op jit(solution)/shard_map/ppermute | solution.py:580
